TPU v7x, 256 devices: a whole 4x4x8 slice. The times are simulated.
256 devices in a mesh: section: 16 (over y, z_lo, core), frame: 16 (over x, z_hi).
Axes of the slice: x: 4, y: 4, z: 8 (z_hi: 4, z_lo: 2; z = z_hi * 2 + z_lo), core: 2. Of those that a mesh axis runs over, the one named last changes fastest.
Arguments:
- gen_in: bfloat16 [64, 32, 128, 128], P(None, 'frame', 'section'), may hold values from -6 to 6
- w_gen_one: bfloat16 [9, 4096], replicated, may hold values from -0.25 to 0.25
- w_gen_rgb: bfloat16 [3, 64, 3, 3], replicated, may hold values from -0.25 to 0.25
- w_disc_one: bfloat16 [64, 3, 3, 3, 3], replicated, may hold values from -0.625 to 0.625
- w_disc_two: bfloat16 [27, 4096], replicated, may hold values from -0.15625 to 0.15625
- w_score: bfloat16 [64], replicated, may hold values from -0.75 to 0.75
- score_grad: float32 [32, 128, 128], P('frame', 'section'), may hold values from -6 to 6
Outputs:
- grad_in: bfloat16 [64, 32, 128, 128], P(None, 'frame', 'section')
- grad_gen_one: float32 [9, 4096], replicated
- grad_gen_rgb: float32 [3, 64, 3, 3], replicated
- grad_disc_one: float32 [64, 3, 3, 3, 3], replicated
- grad_disc_two: float32 [27, 4096], replicated
- grad_score: float32 [64], replicated
All inputs are finite; a program needn't handle non-finite values.
Results may differ from a plain program's by a relative error of at most 0.019.
Values may be sent and summed in bfloat16 or wider, within the bound.
No kernel may reach another device: no remote copies, remote signals or barrier semaphores. Data moves between devices by JAX's collectives and lax.ppermute only.
A program may use at most 64 MiB of HBM per device.

v0:
```python
import jax
import jax.numpy as jnp
from jax import lax
from jax.sharding import PartitionSpec as P


def as_sent(value):
    return jax.tree.map(lambda a: a.astype(jnp.bfloat16) if a.dtype == jnp.float32 else a, value)


def padded(value, sides, width):
    for axis, dim in sides:
        size, length = (lax.axis_size(axis), value.shape[dim])
        up = [(i, (i + 1) % size) for i in range(size - 1)]
        down = [(j, i) for i, j in up]
        last = lax.slice_in_dim(value, length - width, length, axis=dim)
        first = lax.slice_in_dim(value, 0, width, axis=dim)
        before = lax.ppermute(last, axis, up)
        after = lax.ppermute(first, axis, down)
        value = jnp.concatenate([before, value, after], axis=dim)
    return value


def squash(z):
    return jnp.tanh(z)


def slope(a):
    value = a.astype(jnp.float32)
    return 1.0 - value * value


def plane_kernel(flat, outs, ins):
    return jnp.transpose(flat.reshape(3, 3, outs, ins), (2, 3, 0, 1))


def volume_kernel(flat, outs, ins):
    return jnp.transpose(flat.reshape(3, 3, 3, outs, ins), (3, 4, 0, 1, 2))


def plane_flat(kernel):
    return jnp.transpose(kernel, (2, 3, 0, 1)).reshape(9, -1)


def volume_flat(kernel):
    return jnp.transpose(kernel, (2, 3, 4, 0, 1)).reshape(27, -1)


def conv_plane(xp, w):
    return lax.conv_general_dilated(
        xp,
        w,
        (1, 1),
        "VALID",
        dimension_numbers=("CNHW", "OIHW", "CNHW"),
        preferred_element_type=jnp.float32,
    )


def conv_volume(xp, w):
    return lax.conv_general_dilated(
        xp[None],
        w,
        (1, 1, 1),
        "VALID",
        dimension_numbers=("NCDHW", "OIDHW", "NCDHW"),
        preferred_element_type=jnp.float32,
    )[0]


def back_plane(dyp, w):
    return conv_plane(dyp, jnp.swapaxes(jnp.flip(w, (2, 3)), 0, 1))


def back_volume(dyp, w):
    return conv_volume(dyp, jnp.swapaxes(jnp.flip(w, (2, 3, 4)), 0, 1))


def wgrad_plane(xp, dy):
    out = lax.conv_general_dilated(
        xp,
        dy,
        (1, 1),
        "VALID",
        dimension_numbers=("NCHW", "OIHW", "NCHW"),
        preferred_element_type=jnp.float32,
    )
    return jnp.swapaxes(out, 0, 1)


def wgrad_volume(xp, dy):
    out = lax.conv_general_dilated(
        xp[:, None],
        dy[:, None],
        (1, 1, 1),
        "VALID",
        dimension_numbers=("NCDHW", "OIDHW", "NCDHW"),
        preferred_element_type=jnp.float32,
    )
    return jnp.swapaxes(out, 0, 1)


def pad_columns(x):
    return jnp.pad(x, ((0, 0), (0, 0), (0, 0), (1, 1)))


def slab_rim(x):
    extended = padded(as_sent(x), (("section", 2),), 1).astype(x.dtype)
    return pad_columns(extended)


def volume_rim(x):
    extended = padded(as_sent(x), (("frame", 1), ("section", 2)), 1).astype(x.dtype)
    return pad_columns(extended)


def local(gen_in, w_gen_one, w_gen_rgb, w_disc_one, w_disc_two, w_score, score_grad):
    channels = gen_in.shape[0]
    disc_width = w_score.shape[0]
    frames_dev = gen_in.shape[1]
    rows_dev = gen_in.shape[2]
    width = gen_in.shape[3]
    total_cells = frames_dev * lax.axis_size("frame") * rows_dev * lax.axis_size("section") * width
    factor = 1.0 / total_cells**0.5
    kernel_gen = plane_kernel(w_gen_one, channels, channels)
    kernel_two = volume_kernel(w_disc_two, disc_width, disc_width)
    gen_pad = slab_rim(gen_in)
    hidden = squash(conv_plane(gen_pad, kernel_gen)).astype(jnp.bfloat16)
    hidden_pad = slab_rim(hidden)
    colour = conv_plane(hidden_pad, w_gen_rgb).astype(jnp.bfloat16)
    colour_pad = volume_rim(colour)
    feat_one = squash(conv_volume(colour_pad, w_disc_one)).astype(jnp.bfloat16)
    feat_pad = volume_rim(feat_one)
    feat_two = squash(conv_volume(feat_pad, kernel_two)).astype(jnp.bfloat16)
    part_score = jnp.einsum("cfhw,fhw->c", feat_two.astype(jnp.float32), score_grad)
    dz_two = (
        w_score.astype(jnp.float32)[:, None, None, None] * score_grad[None] * slope(feat_two)
    ).astype(jnp.bfloat16)
    part_two = volume_flat(wgrad_volume(feat_pad, dz_two))
    dz_one = (back_volume(volume_rim(dz_two), kernel_two) * slope(feat_one)).astype(jnp.bfloat16)
    part_one = wgrad_volume(colour_pad, dz_one)
    d_colour = back_volume(volume_rim(dz_one), w_disc_one).astype(jnp.bfloat16)
    part_rgb = wgrad_plane(hidden_pad, d_colour)
    dz_hidden = (back_plane(slab_rim(d_colour), w_gen_rgb) * slope(hidden)).astype(jnp.bfloat16)
    part_gen = plane_flat(wgrad_plane(gen_pad, dz_hidden))
    grad_in = back_plane(slab_rim(dz_hidden), kernel_gen).astype(jnp.bfloat16)
    gen_one, gen_rgb, disc_one, disc_two, disc_score = lax.psum(
        (part_gen, part_rgb, part_one, part_two, part_score), ("section", "frame")
    )
    return (
        grad_in,
        gen_one * factor,
        gen_rgb * factor,
        disc_one * factor,
        disc_two * factor,
        disc_score * factor,
    )


def solution(mesh):
    in_specs = (
        P(None, "frame", "section", None),
        P(),
        P(),
        P(),
        P(),
        P(),
        P("frame", "section", None),
    )
    out_specs = (P(None, "frame", "section", None), P(), P(), P(), P(), P())
    return jax.shard_map(local, mesh=mesh, in_specs=in_specs, out_specs=out_specs, check_vma=False)
```

profile of v0, /device:TPU:1, one launch (start us, length us, event | category | flops | bytes accessed | tf_op | source)
XLA Modules:
  0.0 615.9 jit_solution(366871063907782256)
XLA Ops:
  8.4 4.9 collective-permute-start
  16.4 2.5 collective-permute-done.1
  26.8 2.9 collective-permute-start.3
  37.2 6.6 %fusion.75 = bf16[8,16,17,3]{1,3,2,0:T(4,128)(2,1)S(1)} fusion(bf16[64,10,2,7,2]{0,3,2,4,1:T(8,128)(2,1)S(1)} %slice.132, bf16[64,10,2,8,17]{0,3,2,4,1:T(8,128)(2,1)S(1)} %copy.257, bf16[3,64,3,3]{1,3,2,0:T(4,128)(2,1)S(1)} %copy-done.39), kind=kOutput, calls=%fused_computation.89 | convolution fusion | flops 8687616 | bytes 400512 | tf_op jit(solution)/shard_map/conv_general_dilated | solution.py:50
  44.3 4.9 collective-permute-start.4
  50.5 2.4 fusion.137
  52.9 2.7 collective-permute-done.5
  55.6 5.4 collective-permute-start.6
  67.9 3.4 convert_multiply_fusion.1
  72.4 6.4 %collective-permute-start.8 = (bf16[64,1,8,128]{0,2,3,1:T(8,128)(2,1)}, bf16[64,1,8,128]{0,2,3,1:T(8,128)(2,1)}, u32[]{:S(2)}, u32[]{:S(2)}) collective-permute-start(bf16[64,1,8,128]{0,2,3,1:T(8,128)(2,1)} %get-tuple-element.63), channel_id=1, source_target_pairs={{0,1},{1,2},{2,3},{3,4},{4,5},{5,6},{6,7},{7,8},{8,9},{9,10},{10,1... | collective-permute-start | bytes 393224 | tf_op jit(solution)/shard_map/ppermute | solution.py:18
  88.8 5.6 collective-permute-done.9
  98.0 2.4 collective-permute-start.11
  100.6 5.3 copy.312
  114.3 4.3 convert_multiply_fusion
  119.8 3.7 collective-permute-start.12
  126.4 4.8 copy.316
  131.2 17.3 %fusion.66 = f32[3,3,3,64,64]{4,3,2,1,0:T(8,128)S(1)} fusion(bf16[64,1,4,10,130]{0,1,4,3,2:T(2,128)(2,1)} %copy.316, bf16[64,1,2,8,128]{0,3,4,2,1:T(8,128)(2,1)} %fusion.61), kind=kOutput, calls=%fused_computation.81 | convolution fusion | flops 452984832 | bytes 1370112 | tf_op jit(solution)/shard_map/transpose;transpose | solution.py:46
  153.0 3.0 collective-permute-start.15
  159.0 5.6 collective-permute-done.15
  165.5 2.3 copy.337
  169.6 2.3 fusion.37
  172.4 4.8 collective-permute-start.16
  180.5 10.3 %collective-permute-done.17 = bf16[64,1,8,128]{0,2,3,1:T(8,128)(2,1)S(1)} collective-permute-done((bf16[64,1,8,128]{0,2,3,1:T(8,128)(2,1)S(1)}, bf16[64,1,8,128]{0,2,3,1:T(8,128)(2,1)S(1)}, u32[]{:S(2)}, u32[]{:S(2)}) %collective-permute-start.17) | collective-permute-done | bytes 131104 | tf_op jit(solution)/shard_map/ppermute | solution.py:19
  193.3 2.6 collective-permute-start.19
  195.9 14.8 %fusion.68 = f32[64,3,3,3,3]{0,1,4,3,2:T(4,128)S(1)} fusion(bf16[3,1,4,10,130]{0,1,4,3,2:T(2,128)(2,1)S(1)} %copy-done.4, bf16[64,1,2,8,128]{0,3,4,2,1:T(8,128)(2,1)S(1)} %fusion.97), kind=kOutput, calls=%fused_computation.83 | convolution fusion | flops 21233664 | bytes 314080 | tf_op jit(solution)/shard_map/transpose | solution.py:100
  212.4 2.3 copy.338
  215.7 34.6 %fusion.20 = bf16[2,8,8,17,3]{2,4,3,1,0:T(4,128)(2,1)S(1)} fusion(bf16[64,4,10,1,7,2]{0,4,5,2,1,3:T(8,128)(2,1)S(1)} %slice.154, bf16[64,4,10,1,8,17]{0,4,5,2,1,3:T(8,128)(2,1)S(1)} %copy.284, bf16[64,3,3,3,3]{0,4,3,2,1:T(4,128)(2,1)S(1)} %copy-done), kind=kOutput, calls=%fused_computation.23 | convolution fusion | flops 24895488 | bytes 791424 | tf_op jit(solution)/shard_map/conv_general_dilated | solution.py:61
  252.2 3.2 fusion.147
  255.4 81.0 %all-reduce.4 = (f32[3,64,3,3]{1,0,3,2:T(4,128)S(1)}, f32[64,3,3,3,3]{0,1,4,3,2:T(4,128)S(1)}, f32[64]{0:T(128)S(1)}) all-reduce(f32[3,64,3,3]{1,0,3,2:T(4,128)S(1)} %fusion.147, f32[64,3,3,3,3]{0,1,4,3,2:T(4,128)S(1)} %fusion.68, f32[64]{0:T(128)S(1)} %convolution_bitcast_fusion), channel_id=1, replica_groups=mesh['section'=16,'frame'=16] {'section','frame'}, use_global_device_ids=true, to_apply=%region_1.2 | all-reduce | flops 6976 | bytes 55808 | tf_op jit(solution)/shard_map/psum | solution.py:147
  336.5 2.9 collective-permute-start.20
  346.9 2.3 collective-permute-start.22
  360.5 244.8 %all-reduce.8.cloned.1.call-done = (f32[9,4096]{1,0:T(8,128)}, f32[27,4096]{1,0:T(8,128)}) async-done(((f32[9,4096]{1,0:T(8,128)}, f32[27,4096]{1,0:T(8,128)}), (f32[9,4096]{1,0:T(8,128)}, f32[27,4096]{1,0:T(8,128)})) %all-reduce.8.cloned.1.call-update) | async-done | bytes 589840 | tf_op jit(solution)/shard_map/psum | solution.py:147
  (262 shorter events, 97.4 us)
Async XLA Ops:
  7.2 60.7 %copy-start = (bf16[64,3,3,3,3]{0,4,3,2,1:T(4,128)(2,1)S(1)}, bf16[64,3,3,3,3]{0,4,3,2,1:T(4,128)(2,1)}, u32[]{:S(2)}) copy-start(bf16[64,3,3,3,3]{0,4,3,2,1:T(4,128)(2,1)} %param.10) | copy-start | bytes 31108
  7.2 598.1 %all-reduce.8.cloned.1.call-start = ((), (), s32[]{:S(2)}) async-start(), calls=%async_computation | async-start | bytes 1572864 | tf_op jit(solution)/shard_map/psum | solution.py:147
  8.4 8.0 %collective-permute-start = (bf16[64,2,1,128]{3,2,1,0:T(2,128)(2,1)S(1)}, bf16[64,2,1,128]{3,2,1,0:T(2,128)(2,1)S(1)}, u32[]{:S(2)}, u32[]{:S(2)}) collective-permute-start(bf16[64,2,1,128]{3,2,1,0:T(2,128)(2,1)S(1)} %get-tuple-element.65), channel_id=1, source_target_pairs={{0,16},{16,32},{32,48},{48,64},{64,80},{80,96},{96,112},{112,128},... | collective-permute-start | bytes 98312 | tf_op jit(solution)/shard_map/ppermute | solution.py:18
  13.3 5.6 collective-permute-start.1
  24.5 10.5 %collective-permute-start.2 = (bf16[64,2,1,128]{0,1,3,2:T(2,128)(2,1)S(1)}, bf16[64,2,1,128]{0,1,3,2:T(2,128)(2,1)S(1)}, u32[]{:S(2)}, u32[]{:S(2)}) collective-permute-start(bf16[64,2,1,128]{0,1,3,2:T(2,128)(2,1)S(1)} %bitcast.205), channel_id=1, source_target_pairs={{0,16},{16,32},{32,48},{48,64},{64,80},{80,96},{96,112},{112,128},... | collective-permute-start | bytes 98312 | tf_op jit(solution)/shard_map/ppermute | solution.py:18
  26.8 8.3 %collective-permute-start.3 = (bf16[64,2,1,128]{0,1,3,2:T(2,128)(2,1)S(1)}, bf16[64,2,1,128]{0,1,3,2:T(2,128)(2,1)S(1)}, u32[]{:S(2)}, u32[]{:S(2)}) collective-permute-start(bf16[64,2,1,128]{0,1,3,2:T(2,128)(2,1)S(1)} %bitcast.206), channel_id=1, source_target_pairs={{16,0},{32,16},{48,32},{64,48},{80,64},{96,80},{112,96},{128,112},... | collective-permute-start | bytes 98312 | tf_op jit(solution)/shard_map/ppermute | solution.py:19
  44.2 21.8 %copy-start.15 = (bf16[3,2,8,128]{3,1,0,2:T(2,128)(2,1)}, bf16[3,2,8,128]{3,1,0,2:T(2,128)(2,1)S(1)}, u32[]{:S(2)}) copy-start(bf16[3,2,8,128]{3,1,0,2:T(2,128)(2,1)S(1)} %slice_bitcast_fusion.7) | copy-start | bytes 36868
  44.3 8.6 %collective-permute-start.4 = (bf16[3,1,8,128]{3,1,0,2:T(2,128)(2,1)S(1)}, bf16[3,1,8,128]{3,1,0,2:T(2,128)(2,1)S(1)}, u32[]{:S(2)}, u32[]{:S(2)}) collective-permute-start(bf16[3,1,8,128]{3,1,0,2:T(2,128)(2,1)S(1)} %get-tuple-element.69), channel_id=1, source_target_pairs={{0,1},{1,2},{2,3},{3,4},{4,5},{5,6},{6,7},{7,8},{8,9},{9,10},{10,1... | collective-permute-start | bytes 18440 | tf_op jit(solution)/shard_map/ppermute | solution.py:18
  49.2 6.4 %collective-permute-start.5 = (bf16[3,1,8,128]{3,1,0,2:T(2,128)(2,1)S(1)}, bf16[3,1,8,128]{3,1,0,2:T(2,128)(2,1)S(1)}, u32[]{:S(2)}, u32[]{:S(2)}) collective-permute-start(bf16[3,1,8,128]{3,1,0,2:T(2,128)(2,1)S(1)} %get-tuple-element.70), channel_id=1, source_target_pairs={{1,0},{2,1},{3,2},{4,3},{5,4},{6,5},{7,6},{8,7},{9,8},{10,9},{11,1... | collective-permute-start | bytes 18440 | tf_op jit(solution)/shard_map/ppermute | solution.py:19
  52.9 18.5 %copy-start.24 = (bf16[3,1,8,128]{3,1,0,2:T(2,128)(2,1)}, bf16[3,1,8,128]{3,1,0,2:T(2,128)(2,1)S(1)}, u32[]{:S(2)}) copy-start(bf16[3,1,8,128]{3,1,0,2:T(2,128)(2,1)S(1)} %collective-permute-done.4) | copy-start | bytes 18436
  55.6 8.1 %collective-permute-start.6 = (bf16[3,4,1,128]{3,1,0,2:T(4,128)(2,1)S(1)}, bf16[3,4,1,128]{3,1,0,2:T(4,128)(2,1)S(1)}, u32[]{:S(2)}, u32[]{:S(2)}) collective-permute-start(bf16[3,4,1,128]{3,1,0,2:T(4,128)(2,1)S(1)} %get-tuple-element.67), channel_id=1, source_target_pairs={{0,16},{16,32},{32,48},{48,64},{64,80},{80,96},{96,112},{112,128},... | collective-permute-start | bytes 9224 | tf_op jit(solution)/shard_map/ppermute | solution.py:18
  61.1 4.9 collective-permute-start.7
  72.4 16.5 %collective-permute-start.8 = (bf16[64,1,8,128]{0,2,3,1:T(8,128)(2,1)}, bf16[64,1,8,128]{0,2,3,1:T(8,128)(2,1)}, u32[]{:S(2)}, u32[]{:S(2)}) collective-permute-start(bf16[64,1,8,128]{0,2,3,1:T(8,128)(2,1)} %get-tuple-element.63), channel_id=1, source_target_pairs={{0,1},{1,2},{2,3},{3,4},{4,5},{5,6},{6,7},{7,8},{8,9},{9,10},{10,1... | collective-permute-start | bytes 393224 | tf_op jit(solution)/shard_map/ppermute | solution.py:18
  78.8 15.6 %collective-permute-start.9 = (bf16[64,1,8,128]{0,2,3,1:T(8,128)(2,1)}, bf16[64,1,8,128]{0,2,3,1:T(8,128)(2,1)}, u32[]{:S(2)}, u32[]{:S(2)}) collective-permute-start(bf16[64,1,8,128]{0,2,3,1:T(8,128)(2,1)} %get-tuple-element.64), channel_id=1, source_target_pairs={{1,0},{2,1},{3,2},{4,3},{5,4},{6,5},{7,6},{8,7},{9,8},{10,9},{11,1... | collective-permute-start | bytes 393224 | tf_op jit(solution)/shard_map/ppermute | solution.py:19
  96.1 10.6 %collective-permute-start.10 = (bf16[64,4,1,128]{0,2,3,1:T(2,128)(2,1)S(1)}, bf16[64,4,1,128]{0,2,3,1:T(2,128)(2,1)S(1)}, u32[]{:S(2)}, u32[]{:S(2)}) collective-permute-start(bf16[64,4,1,128]{0,2,3,1:T(2,128)(2,1)S(1)} %get-tuple-element.45), channel_id=1, source_target_pairs={{0,16},{16,32},{32,48},{48,64},{64,80},{80,96},{96,112},{112,128},... | collective-permute-start | bytes 196616 | tf_op jit(solution)/shard_map/ppermute | solution.py:18
  98.0 10.3 %collective-permute-start.11 = (bf16[64,4,1,128]{0,2,3,1:T(2,128)(2,1)S(1)}, bf16[64,4,1,128]{0,2,3,1:T(2,128)(2,1)S(1)}, u32[]{:S(2)}, u32[]{:S(2)}) collective-permute-start(bf16[64,4,1,128]{0,2,3,1:T(2,128)(2,1)S(1)} %get-tuple-element.46), channel_id=1, source_target_pairs={{16,0},{32,16},{48,32},{64,48},{80,64},{96,80},{112,96},{128,112},... | collective-permute-start | bytes 196616 | tf_op jit(solution)/shard_map/ppermute | solution.py:19
  119.8 28.7 %collective-permute-start.12 = (bf16[64,1,8,128]{0,2,3,1:T(8,128)(2,1)}, bf16[64,1,8,128]{0,2,3,1:T(8,128)(2,1)}, u32[]{:S(2)}, u32[]{:S(2)}) collective-permute-start(bf16[64,1,8,128]{0,2,3,1:T(8,128)(2,1)} %get-tuple-element.61), channel_id=1, source_target_pairs={{0,1},{1,2},{2,3},{3,4},{4,5},{5,6},{6,7},{7,8},{8,9},{9,10},{10,1... | collective-permute-start | bytes 393224 | tf_op jit(solution)/shard_map/ppermute | solution.py:18
  123.5 25.0 %collective-permute-start.13 = (bf16[64,1,8,128]{0,2,3,1:T(8,128)(2,1)S(1)}, bf16[64,1,8,128]{0,2,3,1:T(8,128)(2,1)}, u32[]{:S(2)}, u32[]{:S(2)}) collective-permute-start(bf16[64,1,8,128]{0,2,3,1:T(8,128)(2,1)S(1)} %get-tuple-element.62), channel_id=1, source_target_pairs={{1,0},{2,1},{3,2},{4,3},{5,4},{6,5},{7,6},{8,7},{9,8},{10,9},{11,1... | collective-permute-start | bytes 393224 | tf_op jit(solution)/shard_map/ppermute | solution.py:19
  151.0 7.0 %collective-permute-start.14 = (bf16[64,4,1,128]{0,2,3,1:T(2,128)(2,1)}, bf16[64,4,1,128]{0,2,3,1:T(2,128)(2,1)}, u32[]{:S(2)}, u32[]{:S(2)}) collective-permute-start(bf16[64,4,1,128]{0,2,3,1:T(2,128)(2,1)} %get-tuple-element.43), channel_id=1, source_target_pairs={{0,16},{16,32},{32,48},{48,64},{64,80},{80,96},{96,112},{112,128},... | collective-permute-start | bytes 196616 | tf_op jit(solution)/shard_map/ppermute | solution.py:18
  153.0 11.7 %collective-permute-start.15 = (bf16[64,4,1,128]{0,2,3,1:T(2,128)(2,1)}, bf16[64,4,1,128]{0,2,3,1:T(2,128)(2,1)S(1)}, u32[]{:S(2)}, u32[]{:S(2)}) collective-permute-start(bf16[64,4,1,128]{0,2,3,1:T(2,128)(2,1)} %get-tuple-element.44), channel_id=1, source_target_pairs={{16,0},{32,16},{48,32},{64,48},{80,64},{96,80},{112,96},{128,112},... | collective-permute-start | bytes 196616 | tf_op jit(solution)/shard_map/ppermute | solution.py:19
  172.4 8.1 %collective-permute-start.16 = (bf16[64,1,8,128]{0,2,3,1:T(8,128)(2,1)S(1)}, bf16[64,1,8,128]{0,2,3,1:T(8,128)(2,1)S(1)}, u32[]{:S(2)}, u32[]{:S(2)}) collective-permute-start(bf16[64,1,8,128]{0,2,3,1:T(8,128)(2,1)S(1)} %get-tuple-element.59), channel_id=1, source_target_pairs={{0,1},{1,2},{2,3},{3,4},{4,5},{5,6},{6,7},{7,8},{8,9},{9,10},{10,1... | collective-permute-start | bytes 393224 | tf_op jit(solution)/shard_map/ppermute | solution.py:18
  177.1 13.6 %collective-permute-start.17 = (bf16[64,1,8,128]{0,2,3,1:T(8,128)(2,1)S(1)}, bf16[64,1,8,128]{0,2,3,1:T(8,128)(2,1)S(1)}, u32[]{:S(2)}, u32[]{:S(2)}) collective-permute-start(bf16[64,1,8,128]{0,2,3,1:T(8,128)(2,1)S(1)} %get-tuple-element.60), channel_id=1, source_target_pairs={{1,0},{2,1},{3,2},{4,3},{5,4},{6,5},{7,6},{8,7},{9,8},{10,9},{11,1... | collective-permute-start | bytes 393224 | tf_op jit(solution)/shard_map/ppermute | solution.py:19
  191.4 20.0 %collective-permute-start.18 = (bf16[64,4,1,128]{0,2,3,1:T(2,128)(2,1)S(1)}, bf16[64,4,1,128]{0,2,3,1:T(2,128)(2,1)S(1)}, u32[]{:S(2)}, u32[]{:S(2)}) collective-permute-start(bf16[64,4,1,128]{0,2,3,1:T(2,128)(2,1)S(1)} %get-tuple-element.41), channel_id=1, source_target_pairs={{0,16},{16,32},{32,48},{48,64},{64,80},{80,96},{96,112},{112,128},... | collective-permute-start | bytes 196616 | tf_op jit(solution)/shard_map/ppermute | solution.py:18
  193.3 18.2 %collective-permute-start.19 = (bf16[64,4,1,128]{0,2,3,1:T(2,128)(2,1)S(1)}, bf16[64,4,1,128]{0,2,3,1:T(2,128)(2,1)S(1)}, u32[]{:S(2)}, u32[]{:S(2)}) collective-permute-start(bf16[64,4,1,128]{0,2,3,1:T(2,128)(2,1)S(1)} %get-tuple-element.42), channel_id=1, source_target_pairs={{16,0},{32,16},{48,32},{64,48},{80,64},{96,80},{112,96},{128,112},... | collective-permute-start | bytes 196616 | tf_op jit(solution)/shard_map/ppermute | solution.py:19
  215.6 35.0 %copy-start.38 = (pred[8,17]{1,0:T(8,128)(4,1)S(1)}, pred[8,17]{1,0:T(8,128)(4,1)}, u32[]{:S(2)}) copy-start(pred[8,17]{1,0:T(8,128)(4,1)} %constant.60) | copy-start | bytes 412
  255.4 90.5 %copy-start.12 = (bf16[8,16,17,64]{3,1,2,0:T(8,128)(2,1)S(1)}, bf16[8,16,17,64]{3,1,2,0:T(8,128)(2,1)}, u32[]{:S(2)}) copy-start(bf16[8,16,17,64]{3,1,2,0:T(8,128)(2,1)} %copy-done.11) | copy-start | bytes 835588
  255.4 90.5 %copy-start.40 = (bf16[3,64,3,3]{1,3,2,0:T(4,128)(2,1)S(1)}, bf16[3,64,3,3]{1,3,2,0:T(4,128)(2,1)}, u32[]{:S(2)}) copy-start(bf16[3,64,3,3]{1,3,2,0:T(4,128)(2,1)} %param.9) | copy-start | bytes 10372
  255.4 90.5 %copy-start.43 = (pred[16,17]{0,1:T(8,128)(4,1)S(1)}, pred[16,17]{0,1:T(8,128)(4,1)}, u32[]{:S(2)}) copy-start(pred[16,17]{0,1:T(8,128)(4,1)} %constant.67) | copy-start | bytes 820
  336.5 7.0 %collective-permute-start.20 = (bf16[3,2,1,128]{0,1,3,2:T(2,128)(2,1)S(1)}, bf16[3,2,1,128]{0,1,3,2:T(2,128)(2,1)S(1)}, u32[]{:S(2)}, u32[]{:S(2)}) collective-permute-start(bf16[3,2,1,128]{0,1,3,2:T(2,128)(2,1)S(1)} %get-tuple-element.57), channel_id=1, source_target_pairs={{0,16},{16,32},{32,48},{48,64},{64,80},{80,96},{96,112},{112,128},... | collective-permute-start | bytes 4616 | tf_op jit(solution)/shard_map/ppermute | solution.py:18
  339.4 5.6 collective-permute-start.21
  346.9 8.6 %collective-permute-start.22 = (bf16[64,2,1,128]{0,3,1,2:T(8,128)(2,1)S(1)}, bf16[64,2,1,128]{0,3,1,2:T(8,128)(2,1)S(1)}, u32[]{:S(2)}, u32[]{:S(2)}) collective-permute-start(bf16[64,2,1,128]{0,3,1,2:T(8,128)(2,1)S(1)} %slice_bitcast_fusion.6), channel_id=1, source_target_pairs={{0,16},{16,32},{32,48},{48,64},{64,80},{80,96},{96,112},{112,128},... | collective-permute-start | bytes 98312 | tf_op jit(solution)/shard_map/ppermute | solution.py:18
  350.0 5.8 collective-permute-start.23
  (39 other events, 229.3 us)
Sparse Core Ops, SparseCore 0:
  355.6 249.6 all-reduce.7
where the time goes:
time: 622 us; the launch traced here: 616 us
  waiting for transfers between devices  279 us (45%)
  matrix products  92 us (15%)
  blocking collectives  81 us (13%)
  starting transfers between devices  67.5 us (11%)
  local copies, waits for them, and re-layouts  62.1 us (10%)
  other arithmetic  18.7 us (3%)
  between operations  15.7 us (3%)
    psum x1, waiting for transfers between devices, local(): lax.psum((part_gen, part_rgb, part_one, part_two, part_score), ('section'...  245 us
    psum x1, blocking collectives, local(): lax.psum((part_gen, part_rgb, part_one, part_two, part_score), ('section'...  81 us
    conv_general_dilated x4, matrix products, conv_volume(): lax.conv_general_dilated(xp[None], w, (1, 1, 1), 'VALID', dimension_numbe...  44.7 us
    ppermute x12, starting transfers between devices, padded(): before = lax.ppermute(last, axis, up)  43.3 us
    ppermute x12, waiting for transfers between devices, padded(): after = lax.ppermute(first, axis, down)  32.2 us
    ppermute x12, starting transfers between devices, padded(): after = lax.ppermute(first, axis, down)  24.1 us
    another operation x1, matrix products, volume_flat(): return jnp.transpose(kernel, (2, 3, 4, 0, 1)).reshape(27, -1)  17.3 us
    unnamed x104, local copies, waits for them, and re-layouts  15.4 us
  transfers between devices with their start and end apart: 25, of which 11 were waited for; matrix products, arithmetic and copies ran while one was open for 12% of the time, Pallas kernels for 0%

commit v1 on v0

v1 whole, which is shorter than its diff:
```python
import jax
import jax.numpy as jnp
from jax import lax
from jax.experimental import pallas as pl
from jax.experimental.pallas import tpu as pltpu
from jax.sharding import PartitionSpec as P

BF = jnp.bfloat16
F32 = jnp.float32
C = 64
C3 = 3 * C
L = 128
BOTH = ("section", "frame")


def span(row, rows=1):
    return slice(row * L, (row + rows) * L)


def lanes():
    return lax.broadcasted_iota(jnp.int32, (1, L), 1)


def sides(value):
    at = lanes()
    left = jnp.where(at == 0, 0.0, pltpu.roll(value, 1, 1))
    right = jnp.where(at == L - 1, 0.0, pltpu.roll(value, L - 1, 1))
    return left, right


def put(ref, row, value):
    left, right = sides(value)
    ref[0:C, span(row)] = left.astype(BF)
    ref[C : 2 * C, span(row)] = value.astype(BF)
    ref[2 * C : C3, span(row)] = right.astype(BF)


def inside(index, size):
    return jnp.where(jnp.logical_and(index >= 0, index < size), 1.0, 0.0).astype(F32)


def product(out, weight, block, rows, step=4):
    for row in range(0, rows, step):
        part = span(row, min(step, rows - row))
        out[:, part] = jnp.dot(weight[...], block(part), preferred_element_type=F32)


def tap_rows(part, row, outs):
    return (
        part[0:outs, span(row)]
        + part[outs : 2 * outs, span(row + 1)]
        + part[2 * outs : 3 * outs, span(row + 2)]
    )


def along_lanes(a, b):
    return lax.dot_general(a, b, (((1,), (1,)), ((), ())), preferred_element_type=F32)


def three_rows(value):
    blank = jnp.zeros((value.shape[0], L), BF)
    return jnp.concatenate(
        [
            jnp.concatenate([value, blank, blank], axis=1),
            jnp.concatenate([blank, value, blank], axis=1),
            jnp.concatenate([blank, blank, value], axis=1),
        ],
        axis=0,
    )


def gen_kernel(up, mid, down, w_gen, w_rgb, edge, hid, gen, gs, hs, part, part_rgb):
    section = lax.axis_index("section")
    rows_all = 8 * lax.axis_size("section")
    base = section * 8

    for f in range(2):
        for row in range(24):
            source = (up, mid, down)[row // 8]
            keep = inside(base + row - 8, rows_all)
            value = source[0:C, span(f * 8 + row % 8)].astype(F32) * keep
            put(gs, row, value)
        product(part, w_gen, lambda s: gs[:, s], 24)
        gen[f] = gs[:, span(7, 10)]
        for row in range(22):
            keep = inside(base + row - 7, rows_all)
            put(hs, row, jnp.tanh(tap_rows(part, row, C)) * keep)
        product(part_rgb, w_rgb, lambda s: hs[:, s], 22)
        hid[f] = hs[:, span(6, 10)]
        for row in range(20):
            at = row + 2
            source = (up, mid, down)[at // 8]
            score = source[C : C + 16, span(f * 8 + at % 8)].astype(F32)[0:8]
            keep = inside(base + row - 6, rows_all)
            value = (tap_rows(part_rgb, row, 8) + score) * keep
            edge[:, span(f * 20 + row)] = value.astype(BF)


def disc_kernel(
    e0, e1, e2, e3, e4, w_one, w_two, w_two_back, w_one_back, w_rgb_back, w_gen_back, w_score, hid, gen,
    grad_in, pack,
    es, cs, sg, fs, ds, zs, dcs, hzs, part, part_one, part_col, acc_two, acc_gen, acc_one, acc_rgb, acc_score,
):
    section = lax.axis_index("section")
    frame = lax.axis_index("frame")
    rows_all = 8 * lax.axis_size("section")
    frames_all = 2 * lax.axis_size("frame")
    base = section * 8
    first = frame * 2
    sub = lax.broadcasted_iota(jnp.int32, (8, L), 0)

    for k, e in enumerate((e0, e1, e2, e3, e4)):
        for j in range(2):
            es[2 * k + j] = e[:, span(20 * j, 20)].astype(F32)

    def colour_step(e, carry):
        keep = inside(first + e - 4, frames_all)
        for row in range(20):
            value = es[e, :, span(row)] * keep
            sg[e, row : row + 1, :] = value[3:4] + value[4:5]
            value = jnp.where(sub < 3, value, 0.0)
            left, right = sides(value)
            block = jnp.concatenate([left + pltpu.roll(value, 4, 0), right], axis=0).astype(BF)
            for dr in range(3):
                if 0 <= row - dr < 18:
                    cs[e, dr * 16 : (dr + 1) * 16, span(row - dr)] = block
        return carry

    lax.fori_loop(0, 10, colour_step, 0)

    def feat_step(p, carry):
        product(part_one, w_one, lambda s: cs[pl.ds(2 * p, 4), :, s].reshape(192, -1), 18)
        for j in range(2):
            u = 2 * p + j
            keep_frame = inside(first + u - 3, frames_all)
            for row in range(18):
                keep = inside(base + row - 5, rows_all) * keep_frame
                put(fs.at[u], row, jnp.tanh(part_one[j * C : (j + 1) * C, span(row)]) * keep)
        return carry

    lax.fori_loop(0, 4, feat_step, 0)

    acc_score[...] = jnp.zeros_like(acc_score)

    def score_step(g, carry):
        product(part, w_two, lambda s: fs[pl.ds(g, 3), :, s].reshape(3 * C3, -1), 18)
        own = inside(g - 2, 2)
        for row in range(16):
            value = jnp.tanh(tap_rows(part, row, C)).astype(BF).astype(F32)
            score = sg[g + 2, row + 2 : row + 3, :]
            if 4 <= row < 12:
                acc_score[...] += value * (score * own)
            put(ds.at[g], row, w_score[...] * score * (1.0 - value * value))
        return carry

    lax.fori_loop(0, 6, score_step, 0)

    def back_step(h, carry):
        product(part, w_two_back, lambda s: ds[pl.ds(h, 3), :, s].reshape(3 * C3, -1), 16)
        keep_frame = inside(first + h - 1, frames_all)
        for row in range(14):
            keep = inside(base + row - 3, rows_all) * keep_frame
            value = fs[h + 2, C : 2 * C, span(row + 2)].astype(F32)
            put(zs.at[h], row, tap_rows(part, row, C) * ((1.0 - value * value) * keep))
        return carry

    lax.fori_loop(0, 4, back_step, 0)

    for f in range(2):
        feat = fs[f + 2 : f + 5, :, span(4, 10)].reshape(3 * C3, 10 * L)
        grad = along_lanes(three_rows(ds[f + 2, C : 2 * C, span(4, 8)]), feat)
        acc_two[...] = grad if f == 0 else acc_two[...] + grad
        colours = cs[f + 3 : f + 6, :, span(5, 8)].reshape(144, 8 * L)
        grad = along_lanes(colours, zs[f + 1, C : 2 * C, span(3, 8)])
        acc_one[...] = grad if f == 0 else acc_one[...] + grad

        product(part_col, w_one_back, lambda s: zs[f : f + 3, :, s].reshape(3 * C3, -1), 14)
        colour_rows = []
        for row in range(12):
            keep = inside(base + row - 2, rows_all)
            value = (tap_rows(part_col, row, 8) * keep).astype(BF).astype(F32)
            colour_rows.append(value)
            left, right = sides(value)
            block = jnp.concatenate([left + pltpu.roll(value, 4, 0), right], axis=0)
            dcs[:, span(row)] = block.astype(BF)
        own = jnp.concatenate(colour_rows[2:10], axis=1)
        blank = jnp.zeros((8, L), F32)
        own3 = jnp.concatenate(
            [
                jnp.concatenate([own, blank, blank], axis=1),
                jnp.concatenate([blank, own, blank], axis=1),
                jnp.concatenate([blank, blank, own], axis=1),
                jnp.zeros((8, 10 * L), F32),
            ],
            axis=0,
        ).astype(BF)
        grad = along_lanes(hid[f], own3)
        acc_rgb[...] = grad if f == 0 else acc_rgb[...] + grad

        product(part, w_rgb_back, lambda s: dcs[:, s], 12)
        for row in range(10):
            keep = inside(base + row - 1, rows_all)
            value = hid[f, C : 2 * C, span(row)].astype(F32)
            put(hzs, row, tap_rows(part, row, C) * ((1.0 - value * value) * keep))
        grad = along_lanes(three_rows(hzs[C : 2 * C, span(1, 8)]), gen[f])
        acc_gen[...] = grad if f == 0 else acc_gen[...] + grad
        product(part, w_gen_back, lambda s: hzs[:, s], 10)
        for row in range(8):
            grad_in[:, span(f * 8 + row)] = tap_rows(part, row, C).astype(BF)

    score = jnp.sum(acc_score[...], axis=1, keepdims=True)
    tail = jnp.concatenate(
        [jnp.broadcast_to(score, (C, 32)), jnp.zeros((C3 - C, 32), F32)], axis=0
    )
    ones = jnp.concatenate([acc_one[...], jnp.zeros((C3 - 144, C), F32)], axis=0)
    whole = jnp.concatenate([acc_two[...], acc_gen[...], ones, acc_rgb[...], tail], axis=1)
    for k in range(8):
        pack[k] = whole[24 * k : 24 * (k + 1)].astype(BF)


def call(kernel, outs, scratch, name):
    return pl.pallas_call(
        kernel,
        out_shape=outs,
        scratch_shapes=scratch,
        compiler_params=pltpu.CompilerParams(vmem_limit_bytes=50 << 20),
        name=name,
    )


def cyclic(value, axis, step):
    size = lax.axis_size(axis)
    return lax.ppermute(value, axis, [(i, (i + step) % size) for i in range(size)])


def swapped(value, axis, mask):
    return lax.ppermute(value, axis, [(i, i ^ mask) for i in range(lax.axis_size(axis))])


def pick(value, at):
    return lax.dynamic_index_in_dim(value, at, 0, keepdims=False)


def plus(values):
    total = values[0].astype(F32)
    for value in values[1:]:
        total = total + value.astype(F32)
    return total.astype(BF)


def all_sum4(value, axis, low):
    one, two, three = (swapped(value, axis, m * low).astype(F32) for m in (1, 2, 3))
    return ((value.astype(F32) + one) + (two + three)).astype(BF)


def gathered(value, axis, low, count, me):
    parts = jnp.stack([value] + [swapped(value, axis, m * low) for m in range(1, count)])
    return jnp.stack([pick(parts, me ^ k) for k in range(count)])


def summed(value):
    section = lax.axis_index("section")
    core = section & 1
    y = (section >> 2) & 3
    halves = value.reshape((2, 4) + value.shape[1:])
    mine = plus([pick(halves, core), swapped(pick(halves, 1 - core), "section", 1)])
    own = plus([pick(mine, y)] + [swapped(pick(mine, y ^ m), "section", 4 * m) for m in (1, 2, 3)])
    own = all_sum4(own, "frame", 4)
    own = plus([own, swapped(own, "section", 2)])
    own = all_sum4(own, "frame", 1)
    mine = gathered(own, "section", 4, 4, y)
    both = gathered(mine, "section", 1, 2, core)
    return both.reshape(value.shape)


def local(gen_in, w_gen_one, w_gen_rgb, w_disc_one, w_disc_two, w_score, score_grad):
    cells = 2048 * lax.axis_size("frame") * lax.axis_size("section")
    factor = 1.0 / cells**0.5

    gen = w_gen_one.reshape(3, 3, C, C)
    w_gen = jnp.transpose(gen, (0, 2, 1, 3)).reshape(C3, C3)
    w_gen_back = jnp.transpose(jnp.flip(gen, (0, 1)), (0, 3, 1, 2)).reshape(C3, C3)
    rgb = jnp.pad(jnp.transpose(w_gen_rgb, (2, 0, 3, 1)), ((0, 0), (0, 5), (0, 0), (0, 0)))
    w_rgb = rgb.reshape(24, C3)
    rgb_back = jnp.transpose(jnp.flip(w_gen_rgb, (2, 3)), (2, 1, 3, 0))
    w_rgb_back = jnp.pad(rgb_back, ((0, 0), (0, 0), (0, 1), (0, 1))).reshape(C3, 16)
    two = w_disc_two.reshape(3, 3, 3, C, C)
    w_two = jnp.transpose(two, (1, 3, 0, 2, 4)).reshape(C3, 3 * C3)
    w_two_back = jnp.transpose(jnp.flip(two, (0, 1, 2)), (1, 4, 0, 2, 3)).reshape(C3, 3 * C3)
    one = jnp.transpose(w_disc_one, (0, 2, 3, 4, 1))
    one = jnp.pad(one, ((0, 0), (0, 0), (0, 0), (0, 1), (0, 1))).reshape(C, 144)
    w_one = jnp.concatenate(
        [jnp.pad(one, ((0, 0), (0, 48))), jnp.pad(one, ((0, 0), (48, 0)))], axis=0
    )
    one_back = jnp.transpose(jnp.flip(w_disc_one, (2, 3, 4)), (3, 1, 2, 4, 0))
    w_one_back = jnp.pad(one_back, ((0, 0), (0, 5), (0, 0), (0, 0), (0, 0))).reshape(24, 3 * C3)
    score_w = jnp.broadcast_to(w_score.astype(F32)[:, None], (C, L))

    score = score_grad.reshape(1, 2048)
    high = score.astype(BF)
    low = (score - high.astype(F32)).astype(BF)
    mid = jnp.concatenate(
        [gen_in.reshape(C, 2048), jnp.zeros((3, 2048), BF), high, low, jnp.zeros((11, 2048), BF)],
        axis=0,
    )
    up = cyclic(mid, "section", 1)
    down = cyclic(mid, "section", -1)

    edge, hid, gen_pad = call(
        gen_kernel,
        (
            jax.ShapeDtypeStruct((8, 40 * L), BF),
            jax.ShapeDtypeStruct((2, C3, 10 * L), BF),
            jax.ShapeDtypeStruct((2, C3, 10 * L), BF),
        ),
        [
            pltpu.VMEM((C3, 24 * L), BF),
            pltpu.VMEM((C3, 22 * L), BF),
            pltpu.VMEM((C3, 24 * L), F32),
            pltpu.VMEM((24, 22 * L), F32),
        ],
        "generator",
    )(up, mid, down, w_gen, w_rgb)

    edges = [cyclic(edge, "frame", s) for s in (2, -2, 1, -1)]
    grad_in, pack = call(
        disc_kernel,
        (jax.ShapeDtypeStruct((C, 2048), BF), jax.ShapeDtypeStruct((8, 24, 896), BF)),
        [
            pltpu.VMEM((10, 8, 20 * L), F32),
            pltpu.VMEM((10, 48, 18 * L), BF),
            pltpu.VMEM((10, 24, L), F32),
            pltpu.VMEM((8, C3, 18 * L), BF),
            pltpu.VMEM((6, C3, 16 * L), BF),
            pltpu.VMEM((4, C3, 14 * L), BF),
            pltpu.VMEM((16, 12 * L), BF),
            pltpu.VMEM((C3, 10 * L), BF),
            pltpu.VMEM((C3, 18 * L), F32),
            pltpu.VMEM((2 * C, 18 * L), F32),
            pltpu.VMEM((24, 14 * L), F32),
            pltpu.VMEM((C3, 3 * C3), F32),
            pltpu.VMEM((C3, C3), F32),
            pltpu.VMEM((144, C), F32),
            pltpu.VMEM((C3, 32), F32),
            pltpu.VMEM((C, L), F32),
        ],
        "discriminator",
    )(
        edges[0], edges[2], edge, edges[3], edges[1],
        w_one, w_two, w_two_back, w_one_back, w_rgb_back, w_gen_back, score_w, hid, gen_pad,
    )

    total = summed(pack).reshape(C3, 896).astype(F32) * factor
    disc_two = jnp.transpose(total[:, : 3 * C3].reshape(3, C, 3, 3, C), (2, 0, 3, 1, 4)).reshape(27, C * C)
    gen_one = jnp.transpose(total[:, 576:768].reshape(3, C, 3, C), (0, 2, 1, 3)).reshape(9, C * C)
    disc_one = total[:144, 768:832].reshape(3, 3, 4, 4, C)[:, :, :3, :3]
    disc_one = jnp.transpose(disc_one, (4, 3, 0, 1, 2))
    gen_rgb = total[:, 832:856].reshape(3, C, 3, 8)[..., :3]
    gen_rgb = jnp.transpose(gen_rgb, (3, 1, 2, 0))
    disc_score = total[:C, 864]
    return (grad_in.reshape(gen_in.shape), gen_one, gen_rgb, disc_one, disc_two, disc_score)


def solution(mesh):
    in_specs = (
        P(None, "frame", "section", None),
        P(),
        P(),
        P(),
        P(),
        P(),
        P("frame", "section", None),
    )
    out_specs = (P(None, "frame", "section", None), P(), P(), P(), P(), P())
    return jax.shard_map(local, mesh=mesh, in_specs=in_specs, out_specs=out_specs, check_vma=False)
```

time: 622 us -> 105 us (0.17)
  waiting for transfers between devices: 279 us -> 23.5 us
  matrix products: 92 us -> 0 us
  blocking collectives: 81 us -> 0 us
  local copies, waits for them, and re-layouts: 62.1 us -> 15.1 us
  starting transfers between devices: 67.5 us -> 44.3 us
  Pallas kernels: 0 us -> 18.5 us
  other arithmetic: 18.7 us -> 1.99 us
  between operations: 15.7 us -> 1.07 us
    psum x1 -> x0, waiting for transfers between devices: 245 us -> none  [local(): lax.psum((part_gen, part_rgb, part_one, part_two, part_score), ('section'...]
    psum x1 -> x0, blocking collectives: 81 us -> none  [local(): lax.psum((part_gen, part_rgb, part_one, part_two, part_score), ('section'...]
    conv_general_dilated x8 -> x0, matrix products: 54.3 us -> none  [the longest x4 44.7 us: conv_volume(): lax.conv_general_dilated(xp[None], w, (1, 1, 1), 'VALID', dimension_numbe...]
    ppermute x24 -> x21, starting transfers between devices: 67.4 us -> 44.3 us  [the longest x15 27.9 us: swapped(): lax.ppermute(value, axis, [(i, i ^ mask) for i in range(lax.axis_size(axi...]
    another operation x2 -> x0, matrix products: 19.5 us -> none  [the longest x1 17.3 us: volume_flat(): return jnp.transpose(kernel, (2, 3, 4, 0, 1)).reshape(27, -1)]
    pallas_call x0 -> x2, Pallas kernels: none -> 18.5 us  [the longest x1 16.6 us: local(): call(disc_kernel, (jax.ShapeDtypeStruct((C, 2048), BF), jax.ShapeDtypeStr...]
    transpose x2 -> x0, matrix products: 18 us -> none  [the longest x1 14.8 us: wgrad_volume(): return jnp.swapaxes(out, 0, 1)]
    concatenate x16 -> x1, local copies, waits for them, and re-layouts: 14.2 us -> 0.33 us  [local(): jnp.concatenate([gen_in.reshape(C, 2048), jnp.zeros((3, 2048), BF), high,...]
  transfers between devices with their start and end apart: 25 -> 21, of which waited for: 11 -> 15; matrix products, arithmetic and copies ran while one was open for 12% -> 8% of each run, Pallas kernels for 0% -> 0%
where the time goes in v1:
time: 105 us; the launch traced here: 104 us
  starting transfers between devices  44.3 us (42%)
  waiting for transfers between devices  23.5 us (22%)
  Pallas kernels  18.5 us (18%)
  local copies, waits for them, and re-layouts  15.1 us (14%)
  other arithmetic  1.99 us (2%)
  between operations  1.07 us (1%)
    ppermute x15, starting transfers between devices, swapped(): lax.ppermute(value, axis, [(i, i ^ mask) for i in range(lax.axis_size(axi...  27.9 us
    pallas_call x1, Pallas kernels, local(): call(disc_kernel, (jax.ShapeDtypeStruct((C, 2048), BF), jax.ShapeDtypeStr...  16.6 us
    ppermute x6, starting transfers between devices, cyclic(): lax.ppermute(value, axis, [(i, (i + step) % size) for i in range(size)])  16.3 us
    ppermute x15, waiting for transfers between devices, swapped(): lax.ppermute(value, axis, [(i, i ^ mask) for i in range(lax.axis_size(axi...  15.5 us
    ppermute x6, waiting for transfers between devices, cyclic(): lax.ppermute(value, axis, [(i, (i + step) % size) for i in range(size)])  7.99 us
    unnamed x20, local copies, waits for them, and re-layouts  3.08 us
    rev x1, local copies, waits for them, and re-layouts, local(): jnp.flip(two, (0, 1, 2))  2.35 us
  transfers between devices with their start and end apart: 21, of which 15 were waited for; matrix products, arithmetic and copies ran while one was open for 8% of the time, Pallas kernels for 0%

profile of v1, /device:TPU:1, one launch (start us, length us, event | category | flops | bytes accessed | tf_op | source)
XLA Modules:
  0.0 104.5 jit_solution(4108473749042877649)
XLA Ops:
  2.1 1.0 copy.64
  3.5 3.3 %collective-permute-start.1 = (bf16[80,2048]{1,0:T(8,128)(2,1)S(1)}, bf16[80,2048]{1,0:T(8,128)(2,1)S(1)}, u32[]{:S(2)}, u32[]{:S(2)}) collective-permute-start(bf16[80,2048]{1,0:T(8,128)(2,1)S(1)} %concatenate.6.mid), channel_id=1, source_target_pairs={{0,240},{16,0},{32,16},{48,32},{64,48},{80,64},{96,80},{112,96},{1... | collective-permute-start | bytes 983048 | tf_op jit(solution)/shard_map/ppermute | solution.py:233
  7.8 0.9 copy.44
  10.5 0.8 rev.19
  11.6 2.4 %rev.16 = bf16[3,3,3,64,64]{3,2,0,4,1:T(4,128)(2,1)S(1)} reverse(bf16[3,3,3,64,64]{3,2,0,4,1:T(4,128)(2,1)S(1)} %copy.44), dimensions={0,1,2} | reverse | bytes 442368 | tf_op jit(solution)/shard_map/jit(_flip)/rev | solution.py:289
  14.8 1.9 %generator.1 = (bf16[8,5120]{1,0:T(8,128)(2,1)S(1)}, bf16[2,192,1280]{2,1,0:T(8,128)(2,1)S(1)}, bf16[2,192,1280]{2,1,0:T(8,128)(2,1)S(1)}) custom-call(bf16[80,2048]{1,0:T(8,128)(2,1)S(1)} %collective-permute-done.up, bf16[80,2048]{1,0:T(8,128)(2,1)S(1)} %concatenate.6.mid, bf16[80,2048]{1,0:T(8,128)(2,1)S(1)} %collective-permute-done.1.down, ...), custom_call_target="tpu_custom_call" | custom-call | tf_op jit(solution)/shard_map/generator/pallas_call | solution.py:309
  16.8 8.5 %collective-permute-start.5 = (bf16[8,5120]{1,0:T(8,128)(2,1)S(1)}, bf16[8,5120]{1,0:T(8,128)(2,1)S(1)}, u32[]{:S(2)}, u32[]{:S(2)}) collective-permute-start(bf16[8,5120]{1,0:T(8,128)(2,1)S(1)} %get-tuple-element.11.e2), channel_id=1, source_target_pairs={{0,14},{1,15},{2,0},{3,1},{4,2},{5,3},{6,4},{7,5},{8,6},{9,7},{10,... | collective-permute-start | bytes 245768 | tf_op jit(solution)/shard_map/ppermute | solution.py:233
  25.3 2.4 %collective-permute-start.3 = (bf16[8,5120]{1,0:T(8,128)(2,1)S(1)}, bf16[8,5120]{1,0:T(8,128)(2,1)S(1)}, u32[]{:S(2)}, u32[]{:S(2)}) collective-permute-start(bf16[8,5120]{1,0:T(8,128)(2,1)S(1)} %get-tuple-element.11.e2), channel_id=1, source_target_pairs={{0,1},{1,2},{2,3},{3,4},{4,5},{5,6},{6,7},{7,8},{8,9},{9,10},{10,1... | collective-permute-start | bytes 245768 | tf_op jit(solution)/shard_map/ppermute | solution.py:233
  27.6 2.1 %collective-permute-start.2 = (bf16[8,5120]{1,0:T(8,128)(2,1)S(1)}, bf16[8,5120]{1,0:T(8,128)(2,1)S(1)}, u32[]{:S(2)}, u32[]{:S(2)}) collective-permute-start(bf16[8,5120]{1,0:T(8,128)(2,1)S(1)} %get-tuple-element.11.e2), channel_id=1, source_target_pairs={{0,2},{1,3},{2,4},{3,5},{4,6},{5,7},{6,8},{7,9},{8,10},{9,11},{10,... | collective-permute-start | bytes 245768 | tf_op jit(solution)/shard_map/ppermute | solution.py:233
  29.8 1.9 %collective-permute-done.4.e3 = bf16[8,5120]{1,0:T(8,128)(2,1)S(1)} collective-permute-done((bf16[8,5120]{1,0:T(8,128)(2,1)S(1)}, bf16[8,5120]{1,0:T(8,128)(2,1)S(1)}, u32[]{:S(2)}, u32[]{:S(2)}) %collective-permute-start.4) | collective-permute-done | bytes 81952 | tf_op jit(solution)/shard_map/ppermute | solution.py:233
  31.7 2.8 %collective-permute-done.3.e1 = bf16[8,5120]{1,0:T(8,128)(2,1)S(1)} collective-permute-done((bf16[8,5120]{1,0:T(8,128)(2,1)S(1)}, bf16[8,5120]{1,0:T(8,128)(2,1)S(1)}, u32[]{:S(2)}, u32[]{:S(2)}) %collective-permute-start.3) | collective-permute-done | bytes 81952 | tf_op jit(solution)/shard_map/ppermute | solution.py:233
  34.5 3.3 %collective-permute-done.2.e0 = bf16[8,5120]{1,0:T(8,128)(2,1)S(1)} collective-permute-done((bf16[8,5120]{1,0:T(8,128)(2,1)S(1)}, bf16[8,5120]{1,0:T(8,128)(2,1)S(1)}, u32[]{:S(2)}, u32[]{:S(2)}) %collective-permute-start.2) | collective-permute-done | bytes 81952 | tf_op jit(solution)/shard_map/ppermute | solution.py:233
  37.9 16.6 %discriminator.1 = (bf16[64,2048]{1,0:T(8,128)(2,1)S(1)}, bf16[8,24,896]{2,1,0:T(8,128)(2,1)S(1)}) custom-call(bf16[8,5120]{1,0:T(8,128)(2,1)S(1)} %collective-permute-done.2.e0, bf16[8,5120]{1,0:T(8,128)(2,1)S(1)} %collective-permute-done.3.e1, bf16[8,5120]{1,0:T(8,128)(2,1)S(1)} %get-tuple-element.11.e2, bf16[8,5120]{1,0:T(8,128)(2,1)S(1)} %collective-permute-done.4.e3, ...), custom_call_target="tpu_custom_call" | custom-call | tf_op jit(solution)/shard_map/discriminator/pallas_call | solution.py:326
  54.5 4.6 %collective-permute-start.6 = (bf16[4,24,896]{2,1,0:T(8,128)(2,1)S(1)}, bf16[4,24,896]{2,1,0:T(8,128)(2,1)S(1)}, u32[]{:S(2)}, u32[]{:S(2)}) collective-permute-start(bf16[4,24,896]{2,1,0:T(8,128)(2,1)S(1)} %dynamic-slice_bitcast_fusion), channel_id=1, source_target_pairs={{0,16},{16,0},{32,48},{48,32},{64,80},{80,64},{96,112},{112,96},{1... | collective-permute-start | bytes 516104 | tf_op jit(solution)/shard_map/ppermute | solution.py:237
  59.2 1.0 collective-permute-done.6
  60.4 1.7 %collective-permute-start.9 = (bf16[24,896]{1,0:T(8,128)(2,1)S(1)}, bf16[24,896]{1,0:T(8,128)(2,1)S(1)}, u32[]{:S(2)}, u32[]{:S(2)}) collective-permute-start(bf16[24,896]{1,0:T(8,128)(2,1)S(1)} %get-tuple-element.37), channel_id=1, source_target_pairs={{0,192},{16,208},{32,224},{48,240},{64,128},{80,144},{96,160},{112... | collective-permute-start | bytes 129032 | tf_op jit(solution)/shard_map/ppermute | solution.py:237
  62.1 1.5 %collective-permute-start.8 = (bf16[24,896]{1,0:T(8,128)(2,1)S(1)}, bf16[24,896]{1,0:T(8,128)(2,1)S(1)}, u32[]{:S(2)}, u32[]{:S(2)}) collective-permute-start(bf16[24,896]{1,0:T(8,128)(2,1)S(1)} %get-tuple-element.38), channel_id=1, source_target_pairs={{0,128},{16,144},{32,160},{48,176},{64,192},{80,208},{96,224},{112... | collective-permute-start | bytes 129032 | tf_op jit(solution)/shard_map/ppermute | solution.py:237
  63.6 0.9 collective-permute-done.9
  64.6 1.9 %collective-permute-done.8 = bf16[24,896]{1,0:T(8,128)(2,1)S(1)} collective-permute-done((bf16[24,896]{1,0:T(8,128)(2,1)S(1)}, bf16[24,896]{1,0:T(8,128)(2,1)S(1)}, u32[]{:S(2)}, u32[]{:S(2)}) %collective-permute-start.8) | collective-permute-done | bytes 43040 | tf_op jit(solution)/shard_map/ppermute | solution.py:237
  66.9 3.0 %collective-permute-start.10 = (bf16[24,896]{1,0:T(8,128)(2,1)S(1)}, bf16[24,896]{1,0:T(8,128)(2,1)S(1)}, u32[]{:S(2)}, u32[]{:S(2)}) collective-permute-start(bf16[24,896]{1,0:T(8,128)(2,1)S(1)} %fusion.7), channel_id=1, source_target_pairs={{0,4},{1,5},{2,6},{3,7},{4,0},{5,1},{6,2},{7,3},{8,12},{9,13},{10,... | collective-permute-start | bytes 129032 | tf_op jit(solution)/shard_map/ppermute | solution.py:237
  69.9 0.8 collective-permute-done.12
  71.9 2.9 %collective-permute-done.13 = bf16[24,896]{1,0:T(8,128)(2,1)S(1)} collective-permute-done((bf16[24,896]{1,0:T(8,128)(2,1)S(1)}, bf16[24,896]{1,0:T(8,128)(2,1)S(1)}, u32[]{:S(2)}, u32[]{:S(2)}) %collective-permute-start.13) | collective-permute-done | bytes 43040 | tf_op jit(solution)/shard_map/ppermute | solution.py:237
  74.9 1.8 %collective-permute-start.16 = (bf16[24,896]{1,0:T(8,128)(2,1)S(1)}, bf16[24,896]{1,0:T(8,128)(2,1)S(1)}, u32[]{:S(2)}, u32[]{:S(2)}) collective-permute-start(bf16[24,896]{1,0:T(8,128)(2,1)S(1)} %add_convert_fusion.1), channel_id=1, source_target_pairs={{0,3},{1,2},{2,1},{3,0},{4,7},{5,6},{6,5},{7,4},{8,11},{9,10},{10,... | collective-permute-start | bytes 129032 | tf_op jit(solution)/shard_map/ppermute | solution.py:237
  76.7 3.6 %collective-permute-start.15 = (bf16[24,896]{1,0:T(8,128)(2,1)S(1)}, bf16[24,896]{1,0:T(8,128)(2,1)S(1)}, u32[]{:S(2)}, u32[]{:S(2)}) collective-permute-start(bf16[24,896]{1,0:T(8,128)(2,1)S(1)} %add_convert_fusion.1), channel_id=1, source_target_pairs={{0,2},{1,3},{2,0},{3,1},{4,6},{5,7},{6,4},{7,5},{8,10},{9,11},{10,... | collective-permute-start | bytes 129032 | tf_op jit(solution)/shard_map/ppermute | solution.py:237
  80.6 2.9 %collective-permute-done.15 = bf16[24,896]{1,0:T(8,128)(2,1)S(1)} collective-permute-done((bf16[24,896]{1,0:T(8,128)(2,1)S(1)}, bf16[24,896]{1,0:T(8,128)(2,1)S(1)}, u32[]{:S(2)}, u32[]{:S(2)}) %collective-permute-start.15) | collective-permute-done | bytes 43040 | tf_op jit(solution)/shard_map/ppermute | solution.py:237
  84.1 2.1 %collective-permute-start.19 = (bf16[24,896]{1,0:T(8,128)(2,1)S(1)}, bf16[24,896]{1,0:T(8,128)(2,1)S(1)}, u32[]{:S(2)}, u32[]{:S(2)}) collective-permute-start(bf16[24,896]{1,0:T(8,128)(2,1)S(1)} %add_convert_fusion), channel_id=1, source_target_pairs={{0,192},{16,208},{32,224},{48,240},{64,128},{80,144},{96,160},{112... | collective-permute-start | bytes 129032 | tf_op jit(solution)/shard_map/ppermute | solution.py:237
  86.1 1.0 collective-permute-start.18
  87.4 1.1 %collective-permute-done.19 = bf16[24,896]{1,0:T(8,128)(2,1)S(1)} collective-permute-done((bf16[24,896]{1,0:T(8,128)(2,1)S(1)}, bf16[24,896]{1,0:T(8,128)(2,1)S(1)}, u32[]{:S(2)}, u32[]{:S(2)}) %collective-permute-start.19) | collective-permute-done | bytes 43040 | tf_op jit(solution)/shard_map/ppermute | solution.py:237
  88.5 2.0 %collective-permute-done.18 = bf16[24,896]{1,0:T(8,128)(2,1)S(1)} collective-permute-done((bf16[24,896]{1,0:T(8,128)(2,1)S(1)}, bf16[24,896]{1,0:T(8,128)(2,1)S(1)}, u32[]{:S(2)}, u32[]{:S(2)}) %collective-permute-start.18) | collective-permute-done | bytes 43040 | tf_op jit(solution)/shard_map/ppermute | solution.py:237
  90.6 7.4 %collective-permute-start.20 = (bf16[4,24,896]{2,1,0:T(8,128)(2,1)S(1)}, bf16[4,24,896]{2,1,0:T(8,128)(2,1)S(1)}, u32[]{:S(2)}, u32[]{:S(2)}) collective-permute-start(bf16[4,24,896]{2,1,0:T(8,128)(2,1)S(1)} %get-tuple-element.30), channel_id=1, source_target_pairs={{0,16},{16,0},{32,48},{48,32},{64,80},{80,64},{96,112},{112,96},{1... | collective-permute-start | bytes 516104 | tf_op jit(solution)/shard_map/ppermute | solution.py:237
  101.9 0.8 reshape.131
  103.4 1.1 %reshape.135 = f32[27,4096]{1,0:T(8,128)} reshape(f32[3,3,3,64,64]{4,3,2,1,0:T(8,128)S(1)} %copy.51) | data formatting | bytes 884736 | tf_op jit(solution)/shard_map/reshape | solution.py:354
  (89 shorter events, 13.1 us)
Async XLA Ops:
  0.6 6.2 %copy-start.2 = (bf16[9,4096]{1,0:T(8,128)(2,1)S(1)}, bf16[9,4096]{1,0:T(8,128)(2,1)}, u32[]{:S(2)}) copy-start(bf16[9,4096]{1,0:T(8,128)(2,1)} %param.8) | copy-start | bytes 221188
  0.6 6.7 %copy-start = (bf16[27,4096]{1,0:T(8,128)(2,1)S(1)}, bf16[27,4096]{1,0:T(8,128)(2,1)}, u32[]{:S(2)}) copy-start(bf16[27,4096]{1,0:T(8,128)(2,1)} %param.11) | copy-start | bytes 663556
  3.5 11.3 %collective-permute-start.1 = (bf16[80,2048]{1,0:T(8,128)(2,1)S(1)}, bf16[80,2048]{1,0:T(8,128)(2,1)S(1)}, u32[]{:S(2)}, u32[]{:S(2)}) collective-permute-start(bf16[80,2048]{1,0:T(8,128)(2,1)S(1)} %concatenate.6.mid), channel_id=1, source_target_pairs={{0,240},{16,0},{32,16},{48,32},{64,48},{80,64},{96,80},{112,96},{1... | collective-permute-start | bytes 983048 | tf_op jit(solution)/shard_map/ppermute | solution.py:233
  6.8 8.0 %collective-permute-start = (bf16[80,2048]{1,0:T(8,128)(2,1)S(1)}, bf16[80,2048]{1,0:T(8,128)(2,1)S(1)}, u32[]{:S(2)}, u32[]{:S(2)}) collective-permute-start(bf16[80,2048]{1,0:T(8,128)(2,1)S(1)} %concatenate.6.mid), channel_id=1, source_target_pairs={{0,16},{16,32},{32,48},{48,64},{64,80},{80,96},{96,112},{112,128},... | collective-permute-start | bytes 983048 | tf_op jit(solution)/shard_map/ppermute | solution.py:233
  7.8 1.3 %copy-start.4 = (bf16[3,64,3,3]{1,3,2,0:T(4,128)(2,1)S(1)}, bf16[3,64,3,3]{1,3,2,0:T(4,128)(2,1)}, u32[]{:S(2)}) copy-start(bf16[3,64,3,3]{1,3,2,0:T(4,128)(2,1)} %param.9) | copy-start | bytes 10372
  7.8 1.6 %copy-start.3 = (bf16[64,3,3,3,3]{0,4,3,2,1:T(4,128)(2,1)S(1)}, bf16[64,3,3,3,3]{0,4,3,2,1:T(4,128)(2,1)}, u32[]{:S(2)}) copy-start(bf16[64,3,3,3,3]{0,4,3,2,1:T(4,128)(2,1)} %param.10) | copy-start | bytes 31108
  14.0 15.8 %copy-start.1 = (bf16[64,144]{1,0:T(8,128)(2,1)S(1)}, bf16[64,144]{1,0:T(8,128)(2,1)}, u32[]{:S(2)}) copy-start(bf16[64,144]{1,0:T(8,128)(2,1)} %copy.41) | copy-start | bytes 55300
  14.4 23.4 %copy-start.5 = (bf16[64]{0:T(256)(128)(2,1)S(1)}, bf16[64]{0:T(256)(128)(2,1)}, u32[]{:S(2)}) copy-start(bf16[64]{0:T(256)(128)(2,1)} %param.12) | copy-start | bytes 388
  16.8 13.1 %collective-permute-start.5 = (bf16[8,5120]{1,0:T(8,128)(2,1)S(1)}, bf16[8,5120]{1,0:T(8,128)(2,1)S(1)}, u32[]{:S(2)}, u32[]{:S(2)}) collective-permute-start(bf16[8,5120]{1,0:T(8,128)(2,1)S(1)} %get-tuple-element.11.e2), channel_id=1, source_target_pairs={{0,14},{1,15},{2,0},{3,1},{4,2},{5,3},{6,4},{7,5},{8,6},{9,7},{10,... | collective-permute-start | bytes 245768 | tf_op jit(solution)/shard_map/ppermute | solution.py:233
  25.3 6.5 %collective-permute-start.4 = (bf16[8,5120]{1,0:T(8,128)(2,1)S(1)}, bf16[8,5120]{1,0:T(8,128)(2,1)S(1)}, u32[]{:S(2)}, u32[]{:S(2)}) collective-permute-start(bf16[8,5120]{1,0:T(8,128)(2,1)S(1)} %get-tuple-element.11.e2), channel_id=1, source_target_pairs={{0,15},{1,0},{2,1},{3,2},{4,3},{5,4},{6,5},{7,6},{8,7},{9,8},{10,9... | collective-permute-start | bytes 245768 | tf_op jit(solution)/shard_map/ppermute | solution.py:233
  25.3 9.3 %collective-permute-start.3 = (bf16[8,5120]{1,0:T(8,128)(2,1)S(1)}, bf16[8,5120]{1,0:T(8,128)(2,1)S(1)}, u32[]{:S(2)}, u32[]{:S(2)}) collective-permute-start(bf16[8,5120]{1,0:T(8,128)(2,1)S(1)} %get-tuple-element.11.e2), channel_id=1, source_target_pairs={{0,1},{1,2},{2,3},{3,4},{4,5},{5,6},{6,7},{7,8},{8,9},{9,10},{10,1... | collective-permute-start | bytes 245768 | tf_op jit(solution)/shard_map/ppermute | solution.py:233
  27.6 10.2 %collective-permute-start.2 = (bf16[8,5120]{1,0:T(8,128)(2,1)S(1)}, bf16[8,5120]{1,0:T(8,128)(2,1)S(1)}, u32[]{:S(2)}, u32[]{:S(2)}) collective-permute-start(bf16[8,5120]{1,0:T(8,128)(2,1)S(1)} %get-tuple-element.11.e2), channel_id=1, source_target_pairs={{0,2},{1,3},{2,4},{3,5},{4,6},{5,7},{6,8},{7,9},{8,10},{9,11},{10,... | collective-permute-start | bytes 245768 | tf_op jit(solution)/shard_map/ppermute | solution.py:233
  54.5 5.7 %collective-permute-start.6 = (bf16[4,24,896]{2,1,0:T(8,128)(2,1)S(1)}, bf16[4,24,896]{2,1,0:T(8,128)(2,1)S(1)}, u32[]{:S(2)}, u32[]{:S(2)}) collective-permute-start(bf16[4,24,896]{2,1,0:T(8,128)(2,1)S(1)} %dynamic-slice_bitcast_fusion), channel_id=1, source_target_pairs={{0,16},{16,0},{32,48},{48,32},{64,80},{80,64},{96,112},{112,96},{1... | collective-permute-start | bytes 516104 | tf_op jit(solution)/shard_map/ppermute | solution.py:237
  60.3 3.3 %collective-permute-start.7 = (bf16[24,896]{1,0:T(8,128)(2,1)S(1)}, bf16[24,896]{1,0:T(8,128)(2,1)S(1)}, u32[]{:S(2)}, u32[]{:S(2)}) collective-permute-start(bf16[24,896]{1,0:T(8,128)(2,1)S(1)} %get-tuple-element.36), channel_id=1, source_target_pairs={{0,64},{16,80},{32,96},{48,112},{64,0},{80,16},{96,32},{112,48},{1... | collective-permute-start | bytes 129032 | tf_op jit(solution)/shard_map/ppermute | solution.py:237
  60.4 4.2 %collective-permute-start.9 = (bf16[24,896]{1,0:T(8,128)(2,1)S(1)}, bf16[24,896]{1,0:T(8,128)(2,1)S(1)}, u32[]{:S(2)}, u32[]{:S(2)}) collective-permute-start(bf16[24,896]{1,0:T(8,128)(2,1)S(1)} %get-tuple-element.37), channel_id=1, source_target_pairs={{0,192},{16,208},{32,224},{48,240},{64,128},{80,144},{96,160},{112... | collective-permute-start | bytes 129032 | tf_op jit(solution)/shard_map/ppermute | solution.py:237
  62.1 4.4 %collective-permute-start.8 = (bf16[24,896]{1,0:T(8,128)(2,1)S(1)}, bf16[24,896]{1,0:T(8,128)(2,1)S(1)}, u32[]{:S(2)}, u32[]{:S(2)}) collective-permute-start(bf16[24,896]{1,0:T(8,128)(2,1)S(1)} %get-tuple-element.38), channel_id=1, source_target_pairs={{0,128},{16,144},{32,160},{48,176},{64,192},{80,208},{96,224},{112... | collective-permute-start | bytes 129032 | tf_op jit(solution)/shard_map/ppermute | solution.py:237
  66.5 4.2 %collective-permute-start.12 = (bf16[24,896]{1,0:T(8,128)(2,1)S(1)}, bf16[24,896]{1,0:T(8,128)(2,1)S(1)}, u32[]{:S(2)}, u32[]{:S(2)}) collective-permute-start(bf16[24,896]{1,0:T(8,128)(2,1)S(1)} %fusion.7), channel_id=1, source_target_pairs={{0,12},{1,13},{2,14},{3,15},{4,8},{5,9},{6,10},{7,11},{8,4},{9,5},... | collective-permute-start | bytes 129032 | tf_op jit(solution)/shard_map/ppermute | solution.py:237
  66.6 4.5 %collective-permute-start.11 = (bf16[24,896]{1,0:T(8,128)(2,1)S(1)}, bf16[24,896]{1,0:T(8,128)(2,1)S(1)}, u32[]{:S(2)}, u32[]{:S(2)}) collective-permute-start(bf16[24,896]{1,0:T(8,128)(2,1)S(1)} %fusion.7), channel_id=1, source_target_pairs={{0,8},{1,9},{2,10},{3,11},{4,12},{5,13},{6,14},{7,15},{8,0},{9,1},... | collective-permute-start | bytes 129032 | tf_op jit(solution)/shard_map/ppermute | solution.py:237
  66.9 4.9 %collective-permute-start.10 = (bf16[24,896]{1,0:T(8,128)(2,1)S(1)}, bf16[24,896]{1,0:T(8,128)(2,1)S(1)}, u32[]{:S(2)}, u32[]{:S(2)}) collective-permute-start(bf16[24,896]{1,0:T(8,128)(2,1)S(1)} %fusion.7), channel_id=1, source_target_pairs={{0,4},{1,5},{2,6},{3,7},{4,0},{5,1},{6,2},{7,3},{8,12},{9,13},{10,... | collective-permute-start | bytes 129032 | tf_op jit(solution)/shard_map/ppermute | solution.py:237
  71.8 3.1 %collective-permute-start.13 = (bf16[24,896]{1,0:T(8,128)(2,1)S(1)}, bf16[24,896]{1,0:T(8,128)(2,1)S(1)}, u32[]{:S(2)}, u32[]{:S(2)}) collective-permute-start(bf16[24,896]{1,0:T(8,128)(2,1)S(1)} %add_convert_fusion.2), channel_id=1, source_target_pairs={{0,32},{16,48},{32,0},{48,16},{64,96},{80,112},{96,64},{112,80},{1... | collective-permute-start | bytes 129032 | tf_op jit(solution)/shard_map/ppermute | solution.py:237
  74.9 5.7 %collective-permute-start.16 = (bf16[24,896]{1,0:T(8,128)(2,1)S(1)}, bf16[24,896]{1,0:T(8,128)(2,1)S(1)}, u32[]{:S(2)}, u32[]{:S(2)}) collective-permute-start(bf16[24,896]{1,0:T(8,128)(2,1)S(1)} %add_convert_fusion.1), channel_id=1, source_target_pairs={{0,3},{1,2},{2,1},{3,0},{4,7},{5,6},{6,5},{7,4},{8,11},{9,10},{10,... | collective-permute-start | bytes 129032 | tf_op jit(solution)/shard_map/ppermute | solution.py:237
  76.7 6.8 %collective-permute-start.15 = (bf16[24,896]{1,0:T(8,128)(2,1)S(1)}, bf16[24,896]{1,0:T(8,128)(2,1)S(1)}, u32[]{:S(2)}, u32[]{:S(2)}) collective-permute-start(bf16[24,896]{1,0:T(8,128)(2,1)S(1)} %add_convert_fusion.1), channel_id=1, source_target_pairs={{0,2},{1,3},{2,0},{3,1},{4,6},{5,7},{6,4},{7,5},{8,10},{9,11},{10,... | collective-permute-start | bytes 129032 | tf_op jit(solution)/shard_map/ppermute | solution.py:237
  80.3 3.8 %collective-permute-start.14 = (bf16[24,896]{1,0:T(8,128)(2,1)S(1)}, bf16[24,896]{1,0:T(8,128)(2,1)S(1)}, u32[]{:S(2)}, u32[]{:S(2)}) collective-permute-start(bf16[24,896]{1,0:T(8,128)(2,1)S(1)} %add_convert_fusion.1), channel_id=1, source_target_pairs={{0,1},{1,0},{2,3},{3,2},{4,5},{5,4},{6,7},{7,6},{8,9},{9,8},{10,11... | collective-permute-start | bytes 129032 | tf_op jit(solution)/shard_map/ppermute | solution.py:237
  84.1 4.5 %collective-permute-start.19 = (bf16[24,896]{1,0:T(8,128)(2,1)S(1)}, bf16[24,896]{1,0:T(8,128)(2,1)S(1)}, u32[]{:S(2)}, u32[]{:S(2)}) collective-permute-start(bf16[24,896]{1,0:T(8,128)(2,1)S(1)} %add_convert_fusion), channel_id=1, source_target_pairs={{0,192},{16,208},{32,224},{48,240},{64,128},{80,144},{96,160},{112... | collective-permute-start | bytes 129032 | tf_op jit(solution)/shard_map/ppermute | solution.py:237
  86.1 4.4 %collective-permute-start.18 = (bf16[24,896]{1,0:T(8,128)(2,1)S(1)}, bf16[24,896]{1,0:T(8,128)(2,1)S(1)}, u32[]{:S(2)}, u32[]{:S(2)}) collective-permute-start(bf16[24,896]{1,0:T(8,128)(2,1)S(1)} %add_convert_fusion), channel_id=1, source_target_pairs={{0,128},{16,144},{32,160},{48,176},{64,192},{80,208},{96,224},{112... | collective-permute-start | bytes 129032 | tf_op jit(solution)/shard_map/ppermute | solution.py:237
  87.2 3.3 %collective-permute-start.17 = (bf16[24,896]{1,0:T(8,128)(2,1)S(1)}, bf16[24,896]{1,0:T(8,128)(2,1)S(1)}, u32[]{:S(2)}, u32[]{:S(2)}) collective-permute-start(bf16[24,896]{1,0:T(8,128)(2,1)S(1)} %add_convert_fusion), channel_id=1, source_target_pairs={{0,64},{16,80},{32,96},{48,112},{64,0},{80,16},{96,32},{112,48},{1... | collective-permute-start | bytes 129032 | tf_op jit(solution)/shard_map/ppermute | solution.py:237
  90.6 8.5 %collective-permute-start.20 = (bf16[4,24,896]{2,1,0:T(8,128)(2,1)S(1)}, bf16[4,24,896]{2,1,0:T(8,128)(2,1)S(1)}, u32[]{:S(2)}, u32[]{:S(2)}) collective-permute-start(bf16[4,24,896]{2,1,0:T(8,128)(2,1)S(1)} %get-tuple-element.30), channel_id=1, source_target_pairs={{0,16},{16,0},{32,48},{48,32},{64,80},{80,64},{96,112},{112,96},{1... | collective-permute-start | bytes 516104 | tf_op jit(solution)/shard_map/ppermute | solution.py:237

commit v2 on v1

v2 whole, which is shorter than its diff:
```python
import functools

import jax
import jax.numpy as jnp
from jax import lax
from jax.experimental import pallas as pl
from jax.experimental.pallas import tpu as pltpu
from jax.sharding import PartitionSpec as P

BF = jnp.bfloat16
F32 = jnp.float32
C = 64
C3 = 3 * C
L = 128
BOTH = ("section", "frame")


def span(row, rows=1):
    return slice(row * L, (row + rows) * L)


def lanes():
    return lax.broadcasted_iota(jnp.int32, (1, L), 1)


def sides(value):
    at = lanes()
    left = jnp.where(at == 0, 0.0, pltpu.roll(value, 1, 1))
    right = jnp.where(at == L - 1, 0.0, pltpu.roll(value, L - 1, 1))
    return left, right


def put(ref, row, value):
    left, right = sides(value)
    ref[0:C, span(row)] = left.astype(BF)
    ref[C : 2 * C, span(row)] = value.astype(BF)
    ref[2 * C : C3, span(row)] = right.astype(BF)


def inside(index, size):
    return jnp.where(jnp.logical_and(index >= 0, index < size), 1.0, 0.0).astype(F32)


def staged(out, weight, block, rows, outs, lag, finish, step=2):
    done = 0
    for row in range(0, rows, step):
        part = span(row, min(step, rows - row))
        out[:, part] = jnp.dot(weight[...], block(part), preferred_element_type=F32)
        while done < min(row - lag, outs):
            finish(done)
            done += 1
    for row in range(done, outs):
        finish(row)


def tap_rows(part, row, outs):
    return (
        part[0:outs, span(row)]
        + part[outs : 2 * outs, span(row + 1)]
        + part[2 * outs : 3 * outs, span(row + 2)]
    )


def along_lanes(a, b):
    return lax.dot_general(a, b, (((1,), (1,)), ((), ())), preferred_element_type=F32)


def three_rows(value):
    blank = jnp.zeros((value.shape[0], L), BF)
    return jnp.concatenate(
        [
            jnp.concatenate([value, blank, blank], axis=1),
            jnp.concatenate([blank, value, blank], axis=1),
            jnp.concatenate([blank, blank, value], axis=1),
        ],
        axis=0,
    )


def pack_kernel(features, scores, mid, wide):
    wide[...] = features[...].astype(F32)
    sub = lax.broadcasted_iota(jnp.int32, (16, L), 0)
    for k in range(16):
        mid[0:C, span(k)] = wide[pl.ds(k, C, stride=16), :].astype(BF)
        score = scores[k : k + 1, :]
        high = score.astype(BF).astype(F32)
        both = jnp.where(sub == 0, high, jnp.where(sub == 1, score - high, 0.0))
        mid[C : C + 16, span(k)] = both.astype(BF)


def weight_kernel(
    flat_two, flat_gen, two, two_back, gen, gen_back, taps, blocks,
):
    for j in range(32):
        taps[pl.ds(j, 27, stride=32), :] = flat_two[:, span(j)].astype(F32)
        taps[pl.ds(27 * 32 + j, 9, stride=32), :] = flat_gen[:, span(j)].astype(F32)
    for dr in range(3):
        for b in range(6):
            pair = []
            for tap in (2 * b, 2 * b + 1):
                at = (tap // 3) * 9 + dr * 3 + tap % 3 if tap < 9 else 27 + dr * 3 + tap - 9
                pair.append(taps[32 * at : 32 * at + 32, :])
            for odd in range(2):
                half = slice(C * odd, C * odd + C)
                blocks[b, pl.ds(C * dr + odd, 32, stride=2), :] = jnp.concatenate(
                    [pair[0][:, half], pair[1][:, half]], axis=1
                )
    for dr in range(3):
        rows = slice(C * dr, C * dr + C)
        mirror = slice(C * (2 - dr), C * (2 - dr) + C)
        ahead = [blocks[b, rows, :] for b in range(6)]
        ahead = [block[:, C * h : C * h + C] for block in ahead for h in range(2)]
        two[rows, :] = jnp.concatenate(ahead[:9], axis=1).astype(BF)
        gen[rows, :] = jnp.concatenate(ahead[9:], axis=1).astype(BF)
        back = [jnp.transpose(blocks[b, rows, :]) for b in range(6)]
        back = [block[C * h : C * h + C, :] for block in back for h in range(2)]
        two_back[mirror, :] = jnp.concatenate(back[8::-1], axis=1).astype(BF)
        gen_back[mirror, :] = jnp.concatenate(back[:8:-1], axis=1).astype(BF)


def gen_kernel(up, mid, down, w_gen, w_rgb, near, far, hid, gen, gs, hs, part, part_rgb, rows):
    section = lax.axis_index("section")
    rows_all = 8 * lax.axis_size("section")
    base = section * 8

    rows[...] = jnp.zeros_like(rows)
    for f in range(2):
        for row in range(24):
            source = (up, mid, down)[row // 8]
            keep = inside(base + row - 8, rows_all)
            value = source[0:C, span(f * 8 + row % 8)].astype(F32) * keep
            put(gs, row, value)
        def hidden_row(row):
            keep = inside(base + row - 7, rows_all)
            put(hs, row, jnp.tanh(tap_rows(part, row, C)) * keep)

        def colour_row(row):
            keep = inside(base + row - 6, rows_all)
            rows[3 * row : 3 * row + 3, span(f)] = (tap_rows(part_rgb, row, 8) * keep)[0:3]

        staged(part, w_gen, lambda s: gs[:, s], 24, 22, 2, hidden_row)
        gen[f] = gs[:, span(7, 10)]
        staged(part_rgb, w_rgb, lambda s: hs[:, s], 22, 20, 2, colour_row)
        hid[f] = hs[:, span(6, 10)]
        for row in range(16):
            at = row + 4
            source = (up, mid, down)[at // 8]
            keep = inside(base + row - 4, rows_all)
            score = source[C : C + 16, span(f * 8 + at % 8)].astype(F32) * keep
            rows[C + row : C + row + 1, span(f)] = score[0:1]
            rows[C + 16 + row : C + 17 + row, span(f)] = score[1:2]
    near[...] = rows[...].astype(BF)
    far[...] = rows[0:C, :].astype(BF)


def disc_kernel(
    far_a, far_b, near_a, near_b, home, w_one, w_two, w_two_back, w_one_back, w_rgb_back, w_gen_back, w_score, hid, gen,
    grad_in, pack,
    es, cs, sg, fs, ds, zs, dcs, hzs, part, part_one, part_col, acc, acc_one, acc_rgb, acc_score,
):
    section = lax.axis_index("section")
    frame = lax.axis_index("frame")
    rows_all = 8 * lax.axis_size("section")
    frames_all = 2 * lax.axis_size("frame")
    base = section * 8
    first = frame * 2
    sub = lax.broadcasted_iota(jnp.int32, (8, L), 0)

    turn_far, turn_near = (frame >> 1) & 1, frame & 1
    blocks = (
        (far_a, jnp.where(turn_far == 0, 8, 0), C),
        (far_b, jnp.where(turn_far == 0, 0, 8), C),
        (near_a, jnp.where(turn_near == 0, 6, 2), C + 32),
        (near_b, jnp.where(turn_near == 0, 2, 6), C + 32),
        (home, 4, C + 32),
    )
    es[...] = jnp.zeros_like(es)
    for block, at, size in blocks:
        for j in range(2):
            es[at + j, 0:size, :] = block[:, span(j)].astype(F32)

    def colour_step(e, carry):
        keep = inside(first + e - 4, frames_all)
        sg[e] = (es[e, C : C + 16, :] + es[e, C + 16 : C + 32, :]) * keep
        for row in range(20):
            value = jnp.where(sub < 3, es[e, 3 * row : 3 * row + 8, :] * keep, 0.0)
            left, right = sides(value)
            block = jnp.concatenate([left + pltpu.roll(value, 4, 0), right], axis=0).astype(BF)
            for dr in range(3):
                if 0 <= row - dr < 18:
                    cs[e, dr * 16 : (dr + 1) * 16, span(row - dr)] = block
        return carry

    lax.fori_loop(0, 10, colour_step, 0)

    def feat_step(p, carry):
        def feat_row(row):
            keep_row = inside(base + row - 5, rows_all)
            for j in range(2):
                keep = keep_row * inside(first + 2 * p + j - 3, frames_all)
                put(fs.at[2 * p + j], row, jnp.tanh(part_one[j * C : (j + 1) * C, span(row)]) * keep)

        staged(part_one, w_one, lambda s: cs[pl.ds(2 * p, 4), :, s].reshape(192, -1), 18, 18, 0, feat_row)
        return carry

    lax.fori_loop(0, 4, feat_step, 0)

    acc_score[...] = jnp.zeros_like(acc_score)

    def score_step(g, carry):
        own = inside(g - 2, 2)

        def score_row(row):
            value = jnp.tanh(tap_rows(part, row, C)).astype(BF).astype(F32)
            score = sg[g + 2, row : row + 1, :]
            if 4 <= row < 12:
                acc_score[...] += value * (score * own)
            put(ds.at[g], row, w_score[...] * score * (1.0 - value * value))

        staged(part, w_two, lambda s: fs[pl.ds(g, 3), :, s].reshape(3 * C3, -1), 18, 16, 2, score_row)
        return carry

    lax.fori_loop(0, 6, score_step, 0)

    def back_step(h, carry):
        keep_frame = inside(first + h - 1, frames_all)

        def back_row(row):
            keep = inside(base + row - 3, rows_all) * keep_frame
            value = fs[h + 2, C : 2 * C, span(row + 2)].astype(F32)
            put(zs.at[h], row, tap_rows(part, row, C) * ((1.0 - value * value) * keep))

        staged(part, w_two_back, lambda s: ds[pl.ds(h, 3), :, s].reshape(3 * C3, -1), 16, 14, 2, back_row)
        return carry

    lax.fori_loop(0, 4, back_step, 0)

    for f in range(2):
        feat = fs[f + 2 : f + 5, :, span(4, 10)].reshape(3 * C3, 10 * L)
        grad = along_lanes(three_rows(ds[f + 2, C : 2 * C, span(4, 8)]), feat)
        acc[:, : 3 * C3] = grad if f == 0 else acc[:, : 3 * C3] + grad
        colours = cs[f + 3 : f + 6, :, span(5, 8)].reshape(144, 8 * L)
        grad = along_lanes(colours, zs[f + 1, C : 2 * C, span(3, 8)])
        acc_one[...] = grad if f == 0 else acc_one[...] + grad

        colour_rows = []

        def colour_row(row):
            keep = inside(base + row - 2, rows_all)
            value = (tap_rows(part_col, row, 8) * keep).astype(BF).astype(F32)
            colour_rows.append(value)
            left, right = sides(value)
            block = jnp.concatenate([left + pltpu.roll(value, 4, 0), right], axis=0)
            dcs[:, span(row)] = block.astype(BF)

        staged(part_col, w_one_back, lambda s: zs[f : f + 3, :, s].reshape(3 * C3, -1), 14, 12, 2, colour_row)
        own = jnp.concatenate(colour_rows[2:10], axis=1)
        blank = jnp.zeros((8, L), F32)
        own3 = jnp.concatenate(
            [
                jnp.concatenate([own, blank, blank], axis=1),
                jnp.concatenate([blank, own, blank], axis=1),
                jnp.concatenate([blank, blank, own], axis=1),
                jnp.zeros((8, 10 * L), F32),
            ],
            axis=0,
        ).astype(BF)
        grad = along_lanes(own3, hid[f])
        acc_rgb[...] = grad if f == 0 else acc_rgb[...] + grad

        def hidden_row(row):
            keep = inside(base + row - 1, rows_all)
            value = hid[f, C : 2 * C, span(row)].astype(F32)
            put(hzs, row, tap_rows(part, row, C) * ((1.0 - value * value) * keep))

        def input_row(row):
            grad_in[:, span(f * 8 + row)] = tap_rows(part, row, C).astype(BF)

        staged(part, w_rgb_back, lambda s: dcs[:, s], 12, 10, 2, hidden_row)
        grad = along_lanes(three_rows(hzs[C : 2 * C, span(1, 8)]), gen[f])
        acc[:, 3 * C3 :] = grad if f == 0 else acc[:, 3 * C3 :] + grad
        staged(part, w_gen_back, lambda s: hzs[:, s], 10, 8, 2, input_row)

    score = jnp.sum(jnp.transpose(acc_score[...]), axis=0, keepdims=True)
    ones = jnp.concatenate([acc_one[...], jnp.zeros((C3 - 144, C), F32)], axis=0)
    colours = [acc_rgb[0:24, C * k : C * k + C] for k in range(3)]
    colours = jnp.concatenate(colours + [score, jnp.zeros((C3 - 73, C), F32)], axis=0)
    tail = jnp.concatenate([ones, colours], axis=1)
    for k in range(8):
        block = [acc[C * dr + 8 * k : C * dr + 8 * k + 8, :] for dr in range(3)]
        whole = jnp.concatenate([jnp.concatenate(block, axis=0), tail[24 * k : 24 * k + 24]], axis=1)
        pack[k] = whole.astype(BF)


def finish_kernel(factor, own, three, two, one, other, gen_one, gen_rgb, disc_one, disc_two, disc_score, total, taps):
    section = lax.axis_index("section")
    core, y = section & 1, (section >> 2) & 3
    for at, (k, block) in enumerate(((0, own), (3, three), (2, two), (1, one))):
        rows = pl.ds(pl.multiple_of((core * 4 + (y ^ k)) * 24, 8), 24)
        others = pl.ds(pl.multiple_of(((1 - core) * 4 + (y ^ k)) * 24, 8), 24)
        for b in range(7):
            total[b, rows, :] = block[:, span(b)].astype(F32) * factor
            total[b, others, :] = other[at, :, span(b)].astype(F32) * factor
    for c in range(3):
        for dr in range(3):
            for df in range(3):
                disc_one[c, df, dr] = total[6, pl.ds(48 * df + 16 * dr + c, 3, stride=4), :][:, 0:C]
            for dw in range(3):
                at = 24 * dw + 8 * dr + c
                gen_rgb[c, dr, dw : dw + 1, :] = total[6, at : at + 1, :][:, C:]
    disc_score[...] = total[6, 72:73, :][:, C:]
    for dr in range(3):
        for b in range(6):
            for pair in range(4):
                first, second = (
                    total[b, pl.ds(8 * dr + 2 * pair + odd, 8, stride=24), :] for odd in range(2)
                )
                for h in range(2):
                    half = slice(C * h, C * h + C)
                    tap = 2 * b + h
                    at = (tap // 3) * 9 + dr * 3 + tap % 3 if tap < 9 else 27 + dr * 3 + tap - 9
                    taps[pl.ds(32 * at + pair, 8, stride=4), :] = jnp.concatenate(
                        [first[:, half], second[:, half]], axis=1
                    )
    for j in range(32):
        disc_two[:, span(j)] = taps[pl.ds(j, 27, stride=32), :]
        gen_one[:, span(j)] = taps[pl.ds(27 * 32 + j, 9, stride=32), :]


def call(kernel, outs, scratch, name):
    return pl.pallas_call(
        kernel,
        out_shape=outs,
        scratch_shapes=scratch,
        compiler_params=pltpu.CompilerParams(vmem_limit_bytes=50 << 20),
        name=name,
    )


def cyclic(value, axis, step):
    size = lax.axis_size(axis)
    return lax.ppermute(value, axis, [(i, (i + step) % size) for i in range(size)])


def swapped(value, axis, mask):
    return lax.ppermute(value, axis, [(i, i ^ mask) for i in range(lax.axis_size(axis))])


def neighbours(value, axis, step):
    size = lax.axis_size(axis)
    found = []
    for turn in range(2):
        pairs = [(i, (i + step) % size) for i in range(size) if (i // step) % 2 == turn]
        found.append(lax.ppermute(value, axis, pairs + [(j, i) for i, j in pairs]))
    return found


def pick(value, at):
    return lax.dynamic_index_in_dim(value, at, 0, keepdims=False)


def plus(values):
    total = values[0].astype(F32)
    for value in values[1:]:
        total = total + value.astype(F32)
    return total.astype(BF)


def all_sum4(value, axis, low):
    three, two, one = (swapped(value, axis, m * low).astype(F32) for m in (3, 2, 1))
    return ((three + two) + (one + value.astype(F32))).astype(BF)


def summed(value):
    section = lax.axis_index("section")
    core, y = section & 1, (section >> 2) & 3
    halves = value.reshape((2, 4) + value.shape[1:])
    mine = plus([pick(halves, core), swapped(pick(halves, 1 - core), "section", 1)])
    own = plus([pick(mine, y)] + [swapped(pick(mine, y ^ m), "section", 4 * m) for m in (1, 3, 2)])
    own = all_sum4(own, "frame", 4)
    own = plus([own, swapped(own, "section", 2)])
    own = all_sum4(own, "frame", 1)
    three, two, one = (swapped(own, "section", 4 * m) for m in (3, 2, 1))
    blocks = [own, three, two, one]
    return blocks + [swapped(jnp.stack(blocks), "section", 1)]


def local(gen_in, w_gen_one, w_gen_rgb, w_disc_one, w_disc_two, w_score, score_grad):
    cells = 2048 * lax.axis_size("frame") * lax.axis_size("section")
    factor = 1.0 / cells**0.5

    rgb = jnp.pad(jnp.transpose(w_gen_rgb, (2, 0, 3, 1)), ((0, 0), (0, 5), (0, 0), (0, 0)))
    w_rgb = rgb.reshape(24, C3)
    rgb_back = jnp.transpose(jnp.flip(w_gen_rgb, (2, 3)), (2, 1, 3, 0))
    w_rgb_back = jnp.pad(rgb_back, ((0, 0), (0, 0), (0, 1), (0, 1))).reshape(C3, 16)
    one = jnp.transpose(w_disc_one, (0, 2, 3, 4, 1))
    one = jnp.pad(one, ((0, 0), (0, 0), (0, 0), (0, 1), (0, 1))).reshape(C, 144)
    w_one = jnp.concatenate(
        [jnp.pad(one, ((0, 0), (0, 48))), jnp.pad(one, ((0, 0), (48, 0)))], axis=0
    )
    one_back = jnp.transpose(jnp.flip(w_disc_one, (2, 3, 4)), (3, 1, 2, 4, 0))
    w_one_back = jnp.pad(one_back, ((0, 0), (0, 5), (0, 0), (0, 0), (0, 0))).reshape(24, 3 * C3)
    w_two, w_two_back, w_gen, w_gen_back = call(
        weight_kernel,
        (
            jax.ShapeDtypeStruct((C3, 3 * C3), BF),
            jax.ShapeDtypeStruct((C3, 3 * C3), BF),
            jax.ShapeDtypeStruct((C3, C3), BF),
            jax.ShapeDtypeStruct((C3, C3), BF),
        ),
        [pltpu.VMEM((36 * 32, L), F32), pltpu.VMEM((6, C3, L), F32)],
        "weights",
    )(w_disc_two, w_gen_one)
    score_w = jnp.broadcast_to(w_score.astype(F32)[:, None], (C, L))

    mid = call(
        pack_kernel,
        jax.ShapeDtypeStruct((C + 16, 2048), BF),
        [pltpu.VMEM((16 * C, L), F32)],
        "pack",
    )(gen_in.reshape(16 * C, L), score_grad.reshape(16, L))
    up = cyclic(mid, "section", 1)
    down = cyclic(mid, "section", -1)

    near, far, hid, gen_pad = call(
        gen_kernel,
        (
            jax.ShapeDtypeStruct((C + 32, 2 * L), BF),
            jax.ShapeDtypeStruct((C, 2 * L), BF),
            jax.ShapeDtypeStruct((2, C3, 10 * L), BF),
            jax.ShapeDtypeStruct((2, C3, 10 * L), BF),
        ),
        [
            pltpu.VMEM((C3, 24 * L), BF),
            pltpu.VMEM((C3, 22 * L), BF),
            pltpu.VMEM((C3, 24 * L), F32),
            pltpu.VMEM((24, 22 * L), F32),
            pltpu.VMEM((C + 32, 2 * L), F32),
        ],
        "generator",
    )(up, mid, down, w_gen, w_rgb)

    edges = neighbours(far, "frame", 2) + neighbours(near, "frame", 1) + [near]
    grad_in, pack = call(
        disc_kernel,
        (jax.ShapeDtypeStruct((C, 2048), BF), jax.ShapeDtypeStruct((8, 24, 14 * C), BF)),
        [
            pltpu.VMEM((10, C + 32, L), F32),
            pltpu.VMEM((10, 48, 18 * L), BF),
            pltpu.VMEM((10, 16, L), F32),
            pltpu.VMEM((8, C3, 18 * L), BF),
            pltpu.VMEM((6, C3, 16 * L), BF),
            pltpu.VMEM((4, C3, 14 * L), BF),
            pltpu.VMEM((16, 12 * L), BF),
            pltpu.VMEM((C3, 10 * L), BF),
            pltpu.VMEM((C3, 18 * L), F32),
            pltpu.VMEM((2 * C, 18 * L), F32),
            pltpu.VMEM((24, 14 * L), F32),
            pltpu.VMEM((C3, 12 * C), F32),
            pltpu.VMEM((144, C), F32),
            pltpu.VMEM((32, C3), F32),
            pltpu.VMEM((C, L), F32),
        ],
        "discriminator",
    )(
        *edges,
        w_one, w_two, w_two_back, w_one_back, w_rgb_back, w_gen_back, score_w, hid, gen_pad,
    )

    gen_one, gen_rgb, disc_one, disc_two, disc_score = call(
        functools.partial(finish_kernel, factor),
        (
            jax.ShapeDtypeStruct((9, C * C), F32),
            jax.ShapeDtypeStruct((3, 3, 3, C), F32),
            jax.ShapeDtypeStruct((3, 3, 3, 3, C), F32),
            jax.ShapeDtypeStruct((27, C * C), F32),
            jax.ShapeDtypeStruct((1, C), F32),
        ),
        [
            pltpu.VMEM((7, C3, L), F32),
            pltpu.VMEM((36 * 32, L), F32),
        ],
        "finish",
    )(*summed(pack))
    gen_rgb = jnp.transpose(gen_rgb, (0, 3, 1, 2))
    disc_one = jnp.transpose(disc_one, (4, 0, 1, 2, 3))
    return (grad_in.reshape(gen_in.shape), gen_one, gen_rgb, disc_one, disc_two, disc_score.reshape(C))


def solution(mesh):
    in_specs = (
        P(None, "frame", "section", None),
        P(),
        P(),
        P(),
        P(),
        P(),
        P("frame", "section", None),
    )
    out_specs = (P(None, "frame", "section", None), P(), P(), P(), P(), P())
    return jax.shard_map(local, mesh=mesh, in_specs=in_specs, out_specs=out_specs, check_vma=False)
```

time: 105 us -> 99.3 us (0.946)
  local copies, waits for them, and re-layouts: 15.1 us -> 5.15 us
  Pallas kernels: 18.5 us -> 22 us
  other arithmetic: 1.99 us -> 0.25 us
  waiting for transfers between devices: 23.5 us -> 25.1 us
  starting transfers between devices: 44.3 us -> 45.7 us
    ppermute x0 -> x4, starting transfers between devices: none -> 14.7 us  [neighbours(): found.append(lax.ppermute(value, axis, pairs + [(j, i) for i, j in pairs]))]
    ppermute x6 -> x2, starting transfers between devices: 16.3 us -> 3.41 us  [cyclic(): lax.ppermute(value, axis, [(i, (i + step) % size) for i in range(size)])]
    reshape x15 -> x0, local copies, waits for them, and re-layouts: 5.99 us -> none  [the longest x3 1.68 us: local(): two = w_disc_two.reshape(3, 3, 3, C, C)]
    pallas_call x1 -> x4, Pallas kernels: 1.9 us -> 5.11 us  [the longest x1 2.53 us: local(): call(gen_kernel, (jax.ShapeDtypeStruct((C + 32, 2 * L), BF), jax.ShapeDty...]
    rev x2 -> x0, local copies, waits for them, and re-layouts: 3.16 us -> none  [the longest x1 2.35 us: local(): jnp.flip(two, (0, 1, 2))]
    ppermute x0 -> x4, waiting for transfers between devices: none -> 2.12 us  [neighbours(): found.append(lax.ppermute(value, axis, pairs + [(j, i) for i, j in pairs]))]
    convert_element_type x4 -> x2, other arithmetic: 1.54 us -> 0.05 us  [all_sum4(): return (three + two + (one + value.astype(F32))).astype(BF)]
    ppermute x6 -> x2, waiting for transfers between devices: 7.99 us -> 7.11 us  [cyclic(): lax.ppermute(value, axis, [(i, (i + step) % size) for i in range(size)])]
  transfers between devices with their start and end apart: 21 -> 21, of which waited for: 15 -> 15; matrix products, arithmetic and copies ran while one was open for 8% -> 2% of each run, Pallas kernels for 0% -> 1%
where the time goes in v2:
time: 99.3 us; the launch traced here: 99.1 us
  starting transfers between devices  45.7 us (46%)
  waiting for transfers between devices  25.1 us (25%)
  Pallas kernels  22 us (22%)
  local copies, waits for them, and re-layouts  5.15 us (5%)
    ppermute x15, starting transfers between devices, swapped(): lax.ppermute(value, axis, [(i, i ^ mask) for i in range(lax.axis_size(axi...  27.6 us
    pallas_call x1, Pallas kernels, local(): call(disc_kernel, (jax.ShapeDtypeStruct((C, 2048), BF), jax.ShapeDtypeStr...  16.9 us
    ppermute x15, waiting for transfers between devices, swapped(): lax.ppermute(value, axis, [(i, i ^ mask) for i in range(lax.axis_size(axi...  15.9 us
    ppermute x4, starting transfers between devices, neighbours(): found.append(lax.ppermute(value, axis, pairs + [(j, i) for i, j in pairs]))  14.7 us
    ppermute x2, waiting for transfers between devices, cyclic(): lax.ppermute(value, axis, [(i, (i + step) % size) for i in range(size)])  7.11 us
    unnamed x25, local copies, waits for them, and re-layouts  3.74 us
    ppermute x2, starting transfers between devices, cyclic(): lax.ppermute(value, axis, [(i, (i + step) % size) for i in range(size)])  3.41 us
    pallas_call x1, Pallas kernels, local(): call(gen_kernel, (jax.ShapeDtypeStruct((C + 32, 2 * L), BF), jax.ShapeDty...  2.53 us
  transfers between devices with their start and end apart: 21, of which 15 were waited for; matrix products, arithmetic and copies ran while one was open for 2% of the time, Pallas kernels for 1%

profile of v2, /device:TPU:1, one launch (start us, length us, event | category | flops | bytes accessed | tf_op | source)
XLA Modules:
  0.0 99.1 jit_solution(8556692625313904238)
XLA Ops:
  0.6 0.9 copy-done
  2.5 3.1 %collective-permute-start = (bf16[80,2048]{1,0:T(8,128)(2,1)S(1)}, bf16[80,2048]{1,0:T(8,128)(2,1)S(1)}, u32[]{:S(2)}, u32[]{:S(2)}) collective-permute-start(bf16[80,2048]{1,0:T(8,128)(2,1)S(1)} %pack.1.mid), channel_id=1, source_target_pairs={{0,16},{16,32},{32,48},{48,64},{64,80},{80,96},{96,112},{112,128},... | collective-permute-start | bytes 983048 | tf_op jit(solution)/shard_map/ppermute | solution.py:342
  6.8 0.8 weights.1
  7.6 2.0 %collective-permute-done.up = bf16[80,2048]{1,0:T(8,128)(2,1)S(1)} collective-permute-done((bf16[80,2048]{1,0:T(8,128)(2,1)S(1)}, bf16[80,2048]{1,0:T(8,128)(2,1)S(1)}, u32[]{:S(2)}, u32[]{:S(2)}) %collective-permute-start) | collective-permute-done | bytes 327712 | tf_op jit(solution)/shard_map/ppermute | solution.py:342
  9.7 5.1 %collective-permute-done.1.down = bf16[80,2048]{1,0:T(8,128)(2,1)S(1)} collective-permute-done((bf16[80,2048]{1,0:T(8,128)(2,1)S(1)}, bf16[80,2048]{1,0:T(8,128)(2,1)S(1)}, u32[]{:S(2)}, u32[]{:S(2)}) %collective-permute-start.1) | collective-permute-done | bytes 327712 | tf_op jit(solution)/shard_map/ppermute | solution.py:342
  14.7 2.5 %generator.1 = (bf16[96,256]{1,0:T(8,128)(2,1)}, bf16[64,256]{1,0:T(8,128)(2,1)}, bf16[2,192,1280]{2,1,0:T(8,128)(2,1)S(1)}, bf16[2,192,1280]{2,1,0:T(8,128)(2,1)S(1)}) custom-call(bf16[80,2048]{1,0:T(8,128)(2,1)S(1)} %collective-permute-done.up, bf16[80,2048]{1,0:T(8,128)(2,1)S(1)} %pack.1.mid, bf16[80,2048]{1,0:T(8,128)(2,1)S(1)} %collective-permute-done.1.down, ...), custom_call_target="tpu_custom_call" | custom-call | tf_op jit(solution)/shard_map/generator/pallas_call | solution.py:425
  17.3 2.7 %collective-permute-start.4 = (bf16[96,256]{1,0:T(8,128)(2,1)}, bf16[96,256]{1,0:T(8,128)(2,1)S(1)}, u32[]{:S(2)}, u32[]{:S(2)}) collective-permute-start(bf16[96,256]{1,0:T(8,128)(2,1)} %get-tuple-element.23.home), channel_id=1, source_target_pairs={{0,1},{2,3},{4,5},{6,7},{8,9},{10,11},{12,13},{14,15},{1,0},{3,2},... | collective-permute-start | bytes 147464 | tf_op jit(solution)/shard_map/ppermute | solution.py:354
  20.0 6.4 %collective-permute-start.5 = (bf16[96,256]{1,0:T(8,128)(2,1)}, bf16[96,256]{1,0:T(8,128)(2,1)S(1)}, u32[]{:S(2)}, u32[]{:S(2)}) collective-permute-start(bf16[96,256]{1,0:T(8,128)(2,1)} %get-tuple-element.23.home), channel_id=1, source_target_pairs={{1,2},{3,4},{5,6},{7,8},{9,10},{11,12},{13,14},{15,0},{2,1},{4,3},... | collective-permute-start | bytes 147464 | tf_op jit(solution)/shard_map/ppermute | solution.py:354
  26.4 5.6 %collective-permute-start.3 = (bf16[64,256]{1,0:T(8,128)(2,1)}, bf16[64,256]{1,0:T(8,128)(2,1)S(1)}, u32[]{:S(2)}, u32[]{:S(2)}) collective-permute-start(bf16[64,256]{1,0:T(8,128)(2,1)} %get-tuple-element.22), channel_id=1, source_target_pairs={{2,4},{3,5},{6,8},{7,9},{10,12},{11,13},{14,0},{15,1},{4,2},{5,3},... | collective-permute-start | bytes 98312 | tf_op jit(solution)/shard_map/ppermute | solution.py:354
  33.4 2.0 %collective-permute-done.3.far_b = bf16[64,256]{1,0:T(8,128)(2,1)S(1)} collective-permute-done((bf16[64,256]{1,0:T(8,128)(2,1)}, bf16[64,256]{1,0:T(8,128)(2,1)S(1)}, u32[]{:S(2)}, u32[]{:S(2)}) %collective-permute-start.3) | collective-permute-done | bytes 32800 | tf_op jit(solution)/shard_map/ppermute | solution.py:354
  36.1 16.9 %discriminator.1 = (bf16[64,2048]{1,0:T(8,128)(2,1)S(1)}, bf16[8,24,896]{2,1,0:T(8,128)(2,1)S(1)}) custom-call(bf16[64,256]{1,0:T(8,128)(2,1)S(1)} %collective-permute-done.2.far_a, bf16[64,256]{1,0:T(8,128)(2,1)S(1)} %collective-permute-done.3.far_b, bf16[96,256]{1,0:T(8,128)(2,1)S(1)} %collective-permute-done.4.near_a, ...), custom_call_target="tpu_custom_call" | custom-call | tf_op jit(solution)/shard_map/discriminator/pallas_call | solution.py:444
  53.0 2.0 %collective-permute-start.6 = (bf16[4,24,896]{2,1,0:T(8,128)(2,1)S(1)}, bf16[4,24,896]{2,1,0:T(8,128)(2,1)S(1)}, u32[]{:S(2)}, u32[]{:S(2)}) collective-permute-start(bf16[4,24,896]{2,1,0:T(8,128)(2,1)S(1)} %dynamic-slice_bitcast_fusion), channel_id=1, source_target_pairs={{0,16},{16,0},{32,48},{48,32},{64,80},{80,64},{96,112},{112,96},{1... | collective-permute-start | bytes 516104 | tf_op jit(solution)/shard_map/ppermute | solution.py:346
  55.1 1.0 %collective-permute-done.6 = bf16[4,24,896]{2,1,0:T(8,128)(2,1)S(1)} collective-permute-done((bf16[4,24,896]{2,1,0:T(8,128)(2,1)S(1)}, bf16[4,24,896]{2,1,0:T(8,128)(2,1)S(1)}, u32[]{:S(2)}, u32[]{:S(2)}) %collective-permute-start.6) | collective-permute-done | bytes 172064 | tf_op jit(solution)/shard_map/ppermute | solution.py:346
  56.2 1.6 %collective-permute-start.7 = (bf16[24,896]{1,0:T(8,128)(2,1)S(1)}, bf16[24,896]{1,0:T(8,128)(2,1)S(1)}, u32[]{:S(2)}, u32[]{:S(2)}) collective-permute-start(bf16[24,896]{1,0:T(8,128)(2,1)S(1)} %get-tuple-element.36), channel_id=1, source_target_pairs={{0,64},{16,80},{32,96},{48,112},{64,0},{80,16},{96,32},{112,48},{1... | collective-permute-start | bytes 129032 | tf_op jit(solution)/shard_map/ppermute | solution.py:346
  57.8 1.9 %collective-permute-start.8 = (bf16[24,896]{1,0:T(8,128)(2,1)S(1)}, bf16[24,896]{1,0:T(8,128)(2,1)S(1)}, u32[]{:S(2)}, u32[]{:S(2)}) collective-permute-start(bf16[24,896]{1,0:T(8,128)(2,1)S(1)} %get-tuple-element.38), channel_id=1, source_target_pairs={{0,192},{16,208},{32,224},{48,240},{64,128},{80,144},{96,160},{112... | collective-permute-start | bytes 129032 | tf_op jit(solution)/shard_map/ppermute | solution.py:346
  59.7 0.9 collective-permute-start.9
  60.5 1.3 %collective-permute-done.8 = bf16[24,896]{1,0:T(8,128)(2,1)S(1)} collective-permute-done((bf16[24,896]{1,0:T(8,128)(2,1)S(1)}, bf16[24,896]{1,0:T(8,128)(2,1)S(1)}, u32[]{:S(2)}, u32[]{:S(2)}) %collective-permute-start.8) | collective-permute-done | bytes 43040 | tf_op jit(solution)/shard_map/ppermute | solution.py:346
  61.9 2.2 %collective-permute-done.9 = bf16[24,896]{1,0:T(8,128)(2,1)S(1)} collective-permute-done((bf16[24,896]{1,0:T(8,128)(2,1)S(1)}, bf16[24,896]{1,0:T(8,128)(2,1)S(1)}, u32[]{:S(2)}, u32[]{:S(2)}) %collective-permute-start.9) | collective-permute-done | bytes 43040 | tf_op jit(solution)/shard_map/ppermute | solution.py:346
  64.2 1.2 %collective-permute-start.11 = (bf16[24,896]{1,0:T(8,128)(2,1)S(1)}, bf16[24,896]{1,0:T(8,128)(2,1)S(1)}, u32[]{:S(2)}, u32[]{:S(2)}) collective-permute-start(bf16[24,896]{1,0:T(8,128)(2,1)S(1)} %fusion.5), channel_id=1, source_target_pairs={{0,8},{1,9},{2,10},{3,11},{4,12},{5,13},{6,14},{7,15},{8,0},{9,1},... | collective-permute-start | bytes 129032 | tf_op jit(solution)/shard_map/ppermute | solution.py:346
  65.4 2.0 %collective-permute-start.12 = (bf16[24,896]{1,0:T(8,128)(2,1)S(1)}, bf16[24,896]{1,0:T(8,128)(2,1)S(1)}, u32[]{:S(2)}, u32[]{:S(2)}) collective-permute-start(bf16[24,896]{1,0:T(8,128)(2,1)S(1)} %fusion.5), channel_id=1, source_target_pairs={{0,4},{1,5},{2,6},{3,7},{4,0},{5,1},{6,2},{7,3},{8,12},{9,13},{10,... | collective-permute-start | bytes 129032 | tf_op jit(solution)/shard_map/ppermute | solution.py:346
  67.4 0.8 collective-permute-done.10
  70.0 2.4 %collective-permute-done.13 = bf16[24,896]{1,0:T(8,128)(2,1)S(1)} collective-permute-done((bf16[24,896]{1,0:T(8,128)(2,1)S(1)}, bf16[24,896]{1,0:T(8,128)(2,1)S(1)}, u32[]{:S(2)}, u32[]{:S(2)}) %collective-permute-start.13) | collective-permute-done | bytes 43040 | tf_op jit(solution)/shard_map/ppermute | solution.py:346
  72.4 4.5 %collective-permute-start.14 = (bf16[24,896]{1,0:T(8,128)(2,1)S(1)}, bf16[24,896]{1,0:T(8,128)(2,1)S(1)}, u32[]{:S(2)}, u32[]{:S(2)}) collective-permute-start(bf16[24,896]{1,0:T(8,128)(2,1)S(1)} %add_convert_fusion.1), channel_id=1, source_target_pairs={{0,3},{1,2},{2,1},{3,0},{4,7},{5,6},{6,5},{7,4},{8,11},{9,10},{10,... | collective-permute-start | bytes 129032 | tf_op jit(solution)/shard_map/ppermute | solution.py:346
  76.9 1.2 %collective-permute-start.15 = (bf16[24,896]{1,0:T(8,128)(2,1)S(1)}, bf16[24,896]{1,0:T(8,128)(2,1)S(1)}, u32[]{:S(2)}, u32[]{:S(2)}) collective-permute-start(bf16[24,896]{1,0:T(8,128)(2,1)S(1)} %add_convert_fusion.1), channel_id=1, source_target_pairs={{0,2},{1,3},{2,0},{3,1},{4,6},{5,7},{6,4},{7,5},{8,10},{9,11},{10,... | collective-permute-start | bytes 129032 | tf_op jit(solution)/shard_map/ppermute | solution.py:346
  78.1 1.0 %collective-permute-start.16 = (bf16[24,896]{1,0:T(8,128)(2,1)S(1)}, bf16[24,896]{1,0:T(8,128)(2,1)S(1)}, u32[]{:S(2)}, u32[]{:S(2)}) collective-permute-start(bf16[24,896]{1,0:T(8,128)(2,1)S(1)} %add_convert_fusion.1), channel_id=1, source_target_pairs={{0,1},{1,0},{2,3},{3,2},{4,5},{5,4},{6,7},{7,6},{8,9},{9,8},{10,11... | collective-permute-start | bytes 129032 | tf_op jit(solution)/shard_map/ppermute | solution.py:346
  79.1 4.9 %collective-permute-done.15 = bf16[24,896]{1,0:T(8,128)(2,1)S(1)} collective-permute-done((bf16[24,896]{1,0:T(8,128)(2,1)S(1)}, bf16[24,896]{1,0:T(8,128)(2,1)S(1)}, u32[]{:S(2)}, u32[]{:S(2)}) %collective-permute-start.15) | collective-permute-done | bytes 43040 | tf_op jit(solution)/shard_map/ppermute | solution.py:346
  84.1 0.8 collective-permute-start.17
  84.9 1.1 %collective-permute-start.18 = (bf16[24,896]{1,0:T(8,128)(2,1)S(1)}, bf16[24,896]{1,0:T(8,128)(2,1)S(1)}, u32[]{:S(2)}, u32[]{:S(2)}) collective-permute-start(bf16[24,896]{1,0:T(8,128)(2,1)S(1)} %add_convert_fusion.own), channel_id=1, source_target_pairs={{0,128},{16,144},{32,160},{48,176},{64,192},{80,208},{96,224},{112... | collective-permute-start | bytes 129032 | tf_op jit(solution)/shard_map/ppermute | solution.py:346
  86.0 1.4 %collective-permute-start.19 = (bf16[24,896]{1,0:T(8,128)(2,1)S(1)}, bf16[24,896]{1,0:T(8,128)(2,1)S(1)}, u32[]{:S(2)}, u32[]{:S(2)}) collective-permute-start(bf16[24,896]{1,0:T(8,128)(2,1)S(1)} %add_convert_fusion.own), channel_id=1, source_target_pairs={{0,64},{16,80},{32,96},{48,112},{64,0},{80,16},{96,32},{112,48},{1... | collective-permute-start | bytes 129032 | tf_op jit(solution)/shard_map/ppermute | solution.py:346
  87.4 1.1 %collective-permute-done.17.three = bf16[24,896]{1,0:T(8,128)(2,1)S(1)} collective-permute-done((bf16[24,896]{1,0:T(8,128)(2,1)S(1)}, bf16[24,896]{1,0:T(8,128)(2,1)S(1)}, u32[]{:S(2)}, u32[]{:S(2)}) %collective-permute-start.17) | collective-permute-done | bytes 43040 | tf_op jit(solution)/shard_map/ppermute | solution.py:346
  89.3 7.2 %collective-permute-start.20 = (bf16[4,24,896]{2,1,0:T(8,128)(2,1)S(1)}, bf16[4,24,896]{2,1,0:T(8,128)(2,1)S(1)}, u32[]{:S(2)}, u32[]{:S(2)}) collective-permute-start(bf16[4,24,896]{2,1,0:T(8,128)(2,1)S(1)} %pad_maximum_fusion), channel_id=1, source_target_pairs={{0,16},{16,0},{32,48},{48,32},{64,80},{80,64},{96,112},{112,96},{1... | collective-permute-start | bytes 516104 | tf_op jit(solution)/shard_map/ppermute | solution.py:346
  97.5 1.6 %finish.1 = (f32[9,4096]{1,0:T(8,128)}, f32[3,3,3,64]{3,2,1,0:T(4,128)}, f32[3,3,3,3,64]{4,3,2,1,0:T(4,128)}, f32[27,4096]{1,0:T(8,128)}, f32[1,64]{1,0:T(1,128)}) custom-call(bf16[24,896]{1,0:T(8,128)(2,1)S(1)} %add_convert_fusion.own, bf16[24,896]{1,0:T(8,128)(2,1)S(1)} %collective-permute-done.17.three, bf16[24,896]{1,0:T(8,128)(2,1)S(1)} %collective-permute-done.18.two, ...), custom_call_target="tpu_custom_call" | custom-call | tf_op jit(solution)/shard_map/finish/pallas_call | solution.py:470
  (61 shorter events, 8.0 us)
Async XLA Ops:
  0.6 1.0 copy-start
  1.6 0.7 copy-start.3
  2.3 3.7 %copy-start.7 = (bf16[3,64,3,3]{1,3,2,0:T(4,128)(2,1)S(1)}, bf16[3,64,3,3]{1,3,2,0:T(4,128)(2,1)}, u32[]{:S(2)}) copy-start(bf16[3,64,3,3]{1,3,2,0:T(4,128)(2,1)} %param.9) | copy-start | bytes 10372
  2.3 3.8 %copy-start.5 = (bf16[64,3,3,3,3]{0,4,3,2,1:T(4,128)(2,1)S(1)}, bf16[64,3,3,3,3]{0,4,3,2,1:T(4,128)(2,1)}, u32[]{:S(2)}) copy-start(bf16[64,3,3,3,3]{0,4,3,2,1:T(4,128)(2,1)} %param.10) | copy-start | bytes 31108
  2.3 4.5 %copy-start.2 = (bf16[9,4096]{1,0:T(8,128)(2,1)S(1)}, bf16[9,4096]{1,0:T(8,128)(2,1)}, u32[]{:S(2)}) copy-start(bf16[9,4096]{1,0:T(8,128)(2,1)} %flat_gen.1) | copy-start | bytes 221188
  2.5 4.3 %copy-start.1 = (bf16[27,4096]{1,0:T(8,128)(2,1)S(1)}, bf16[27,4096]{1,0:T(8,128)(2,1)}, u32[]{:S(2)}) copy-start(bf16[27,4096]{1,0:T(8,128)(2,1)} %flat_two.1) | copy-start | bytes 663556
  2.5 7.1 %collective-permute-start = (bf16[80,2048]{1,0:T(8,128)(2,1)S(1)}, bf16[80,2048]{1,0:T(8,128)(2,1)S(1)}, u32[]{:S(2)}, u32[]{:S(2)}) collective-permute-start(bf16[80,2048]{1,0:T(8,128)(2,1)S(1)} %pack.1.mid), channel_id=1, source_target_pairs={{0,16},{16,32},{32,48},{48,64},{64,80},{80,96},{96,112},{112,128},... | collective-permute-start | bytes 983048 | tf_op jit(solution)/shard_map/ppermute | solution.py:342
  5.6 9.1 %collective-permute-start.1 = (bf16[80,2048]{1,0:T(8,128)(2,1)S(1)}, bf16[80,2048]{1,0:T(8,128)(2,1)S(1)}, u32[]{:S(2)}, u32[]{:S(2)}) collective-permute-start(bf16[80,2048]{1,0:T(8,128)(2,1)S(1)} %pack.1.mid), channel_id=1, source_target_pairs={{0,240},{16,0},{32,16},{48,32},{64,48},{80,64},{96,80},{112,96},{1... | collective-permute-start | bytes 983048 | tf_op jit(solution)/shard_map/ppermute | solution.py:342
  14.7 17.3 %copy-start.4 = (bf16[64,144]{1,0:T(8,128)(2,1)S(1)}, bf16[64,144]{1,0:T(8,128)(2,1)}, u32[]{:S(2)}) copy-start(bf16[64,144]{1,0:T(8,128)(2,1)} %copy.19) | copy-start | bytes 55300
  17.3 18.1 %collective-permute-start.4 = (bf16[96,256]{1,0:T(8,128)(2,1)}, bf16[96,256]{1,0:T(8,128)(2,1)S(1)}, u32[]{:S(2)}, u32[]{:S(2)}) collective-permute-start(bf16[96,256]{1,0:T(8,128)(2,1)} %get-tuple-element.23.home), channel_id=1, source_target_pairs={{0,1},{2,3},{4,5},{6,7},{8,9},{10,11},{12,13},{14,15},{1,0},{3,2},... | collective-permute-start | bytes 147464 | tf_op jit(solution)/shard_map/ppermute | solution.py:354
  20.0 15.4 %collective-permute-start.5 = (bf16[96,256]{1,0:T(8,128)(2,1)}, bf16[96,256]{1,0:T(8,128)(2,1)S(1)}, u32[]{:S(2)}, u32[]{:S(2)}) collective-permute-start(bf16[96,256]{1,0:T(8,128)(2,1)} %get-tuple-element.23.home), channel_id=1, source_target_pairs={{1,2},{3,4},{5,6},{7,8},{9,10},{11,12},{13,14},{15,0},{2,1},{4,3},... | collective-permute-start | bytes 147464 | tf_op jit(solution)/shard_map/ppermute | solution.py:354
  26.4 5.7 %copy-start.6 = (bf16[64,3,3,3,3]{0,4,3,2,1:T(4,128)(2,1)S(1)}, bf16[64,3,3,3,3]{0,4,3,2,1:T(4,128)(2,1)}, u32[]{:S(2)}) copy-start(bf16[64,3,3,3,3]{0,4,3,2,1:T(4,128)(2,1)} %param.10) | copy-start | bytes 31108
  26.4 7.0 %collective-permute-start.2 = (bf16[64,256]{1,0:T(8,128)(2,1)}, bf16[64,256]{1,0:T(8,128)(2,1)S(1)}, u32[]{:S(2)}, u32[]{:S(2)}) collective-permute-start(bf16[64,256]{1,0:T(8,128)(2,1)} %get-tuple-element.22), channel_id=1, source_target_pairs={{0,2},{1,3},{4,6},{5,7},{8,10},{9,11},{12,14},{13,15},{2,0},{3,1},... | collective-permute-start | bytes 98312 | tf_op jit(solution)/shard_map/ppermute | solution.py:354
  26.4 9.0 %collective-permute-start.3 = (bf16[64,256]{1,0:T(8,128)(2,1)}, bf16[64,256]{1,0:T(8,128)(2,1)S(1)}, u32[]{:S(2)}, u32[]{:S(2)}) collective-permute-start(bf16[64,256]{1,0:T(8,128)(2,1)} %get-tuple-element.22), channel_id=1, source_target_pairs={{2,4},{3,5},{6,8},{7,9},{10,12},{11,13},{14,0},{15,1},{4,2},{5,3},... | collective-permute-start | bytes 98312 | tf_op jit(solution)/shard_map/ppermute | solution.py:354
  32.1 0.7 copy-start.8
  35.4 0.7 copy-start.9
  53.0 3.1 %collective-permute-start.6 = (bf16[4,24,896]{2,1,0:T(8,128)(2,1)S(1)}, bf16[4,24,896]{2,1,0:T(8,128)(2,1)S(1)}, u32[]{:S(2)}, u32[]{:S(2)}) collective-permute-start(bf16[4,24,896]{2,1,0:T(8,128)(2,1)S(1)} %dynamic-slice_bitcast_fusion), channel_id=1, source_target_pairs={{0,16},{16,0},{32,48},{48,32},{64,80},{80,64},{96,112},{112,96},{1... | collective-permute-start | bytes 516104 | tf_op jit(solution)/shard_map/ppermute | solution.py:346
  56.2 4.3 %collective-permute-start.7 = (bf16[24,896]{1,0:T(8,128)(2,1)S(1)}, bf16[24,896]{1,0:T(8,128)(2,1)S(1)}, u32[]{:S(2)}, u32[]{:S(2)}) collective-permute-start(bf16[24,896]{1,0:T(8,128)(2,1)S(1)} %get-tuple-element.36), channel_id=1, source_target_pairs={{0,64},{16,80},{32,96},{48,112},{64,0},{80,16},{96,32},{112,48},{1... | collective-permute-start | bytes 129032 | tf_op jit(solution)/shard_map/ppermute | solution.py:346
  57.8 4.1 %collective-permute-start.8 = (bf16[24,896]{1,0:T(8,128)(2,1)S(1)}, bf16[24,896]{1,0:T(8,128)(2,1)S(1)}, u32[]{:S(2)}, u32[]{:S(2)}) collective-permute-start(bf16[24,896]{1,0:T(8,128)(2,1)S(1)} %get-tuple-element.38), channel_id=1, source_target_pairs={{0,192},{16,208},{32,224},{48,240},{64,128},{80,144},{96,160},{112... | collective-permute-start | bytes 129032 | tf_op jit(solution)/shard_map/ppermute | solution.py:346
  59.7 4.4 %collective-permute-start.9 = (bf16[24,896]{1,0:T(8,128)(2,1)S(1)}, bf16[24,896]{1,0:T(8,128)(2,1)S(1)}, u32[]{:S(2)}, u32[]{:S(2)}) collective-permute-start(bf16[24,896]{1,0:T(8,128)(2,1)S(1)} %get-tuple-element.37), channel_id=1, source_target_pairs={{0,128},{16,144},{32,160},{48,176},{64,192},{80,208},{96,224},{112... | collective-permute-start | bytes 129032 | tf_op jit(solution)/shard_map/ppermute | solution.py:346
  64.1 4.2 %collective-permute-start.10 = (bf16[24,896]{1,0:T(8,128)(2,1)S(1)}, bf16[24,896]{1,0:T(8,128)(2,1)S(1)}, u32[]{:S(2)}, u32[]{:S(2)}) collective-permute-start(bf16[24,896]{1,0:T(8,128)(2,1)S(1)} %fusion.5), channel_id=1, source_target_pairs={{0,12},{1,13},{2,14},{3,15},{4,8},{5,9},{6,10},{7,11},{8,4},{9,5},... | collective-permute-start | bytes 129032 | tf_op jit(solution)/shard_map/ppermute | solution.py:346
  64.2 4.5 %collective-permute-start.11 = (bf16[24,896]{1,0:T(8,128)(2,1)S(1)}, bf16[24,896]{1,0:T(8,128)(2,1)S(1)}, u32[]{:S(2)}, u32[]{:S(2)}) collective-permute-start(bf16[24,896]{1,0:T(8,128)(2,1)S(1)} %fusion.5), channel_id=1, source_target_pairs={{0,8},{1,9},{2,10},{3,11},{4,12},{5,13},{6,14},{7,15},{8,0},{9,1},... | collective-permute-start | bytes 129032 | tf_op jit(solution)/shard_map/ppermute | solution.py:346
  65.4 3.9 %collective-permute-start.12 = (bf16[24,896]{1,0:T(8,128)(2,1)S(1)}, bf16[24,896]{1,0:T(8,128)(2,1)S(1)}, u32[]{:S(2)}, u32[]{:S(2)}) collective-permute-start(bf16[24,896]{1,0:T(8,128)(2,1)S(1)} %fusion.5), channel_id=1, source_target_pairs={{0,4},{1,5},{2,6},{3,7},{4,0},{5,1},{6,2},{7,3},{8,12},{9,13},{10,... | collective-permute-start | bytes 129032 | tf_op jit(solution)/shard_map/ppermute | solution.py:346
  69.3 3.1 %collective-permute-start.13 = (bf16[24,896]{1,0:T(8,128)(2,1)S(1)}, bf16[24,896]{1,0:T(8,128)(2,1)S(1)}, u32[]{:S(2)}, u32[]{:S(2)}) collective-permute-start(bf16[24,896]{1,0:T(8,128)(2,1)S(1)} %add_convert_fusion.2), channel_id=1, source_target_pairs={{0,32},{16,48},{32,0},{48,16},{64,96},{80,112},{96,64},{112,80},{1... | collective-permute-start | bytes 129032 | tf_op jit(solution)/shard_map/ppermute | solution.py:346
  72.4 6.7 %collective-permute-start.14 = (bf16[24,896]{1,0:T(8,128)(2,1)S(1)}, bf16[24,896]{1,0:T(8,128)(2,1)S(1)}, u32[]{:S(2)}, u32[]{:S(2)}) collective-permute-start(bf16[24,896]{1,0:T(8,128)(2,1)S(1)} %add_convert_fusion.1), channel_id=1, source_target_pairs={{0,3},{1,2},{2,1},{3,0},{4,7},{5,6},{6,5},{7,4},{8,11},{9,10},{10,... | collective-permute-start | bytes 129032 | tf_op jit(solution)/shard_map/ppermute | solution.py:346
  76.9 7.1 %collective-permute-start.15 = (bf16[24,896]{1,0:T(8,128)(2,1)S(1)}, bf16[24,896]{1,0:T(8,128)(2,1)S(1)}, u32[]{:S(2)}, u32[]{:S(2)}) collective-permute-start(bf16[24,896]{1,0:T(8,128)(2,1)S(1)} %add_convert_fusion.1), channel_id=1, source_target_pairs={{0,2},{1,3},{2,0},{3,1},{4,6},{5,7},{6,4},{7,5},{8,10},{9,11},{10,... | collective-permute-start | bytes 129032 | tf_op jit(solution)/shard_map/ppermute | solution.py:346
  78.1 5.9 %collective-permute-start.16 = (bf16[24,896]{1,0:T(8,128)(2,1)S(1)}, bf16[24,896]{1,0:T(8,128)(2,1)S(1)}, u32[]{:S(2)}, u32[]{:S(2)}) collective-permute-start(bf16[24,896]{1,0:T(8,128)(2,1)S(1)} %add_convert_fusion.1), channel_id=1, source_target_pairs={{0,1},{1,0},{2,3},{3,2},{4,5},{5,4},{6,7},{7,6},{8,9},{9,8},{10,11... | collective-permute-start | bytes 129032 | tf_op jit(solution)/shard_map/ppermute | solution.py:346
  84.1 4.5 %collective-permute-start.17 = (bf16[24,896]{1,0:T(8,128)(2,1)S(1)}, bf16[24,896]{1,0:T(8,128)(2,1)S(1)}, u32[]{:S(2)}, u32[]{:S(2)}) collective-permute-start(bf16[24,896]{1,0:T(8,128)(2,1)S(1)} %add_convert_fusion.own), channel_id=1, source_target_pairs={{0,192},{16,208},{32,224},{48,240},{64,128},{80,144},{96,160},{112... | collective-permute-start | bytes 129032 | tf_op jit(solution)/shard_map/ppermute | solution.py:346
  84.9 4.4 %collective-permute-start.18 = (bf16[24,896]{1,0:T(8,128)(2,1)S(1)}, bf16[24,896]{1,0:T(8,128)(2,1)S(1)}, u32[]{:S(2)}, u32[]{:S(2)}) collective-permute-start(bf16[24,896]{1,0:T(8,128)(2,1)S(1)} %add_convert_fusion.own), channel_id=1, source_target_pairs={{0,128},{16,144},{32,160},{48,176},{64,192},{80,208},{96,224},{112... | collective-permute-start | bytes 129032 | tf_op jit(solution)/shard_map/ppermute | solution.py:346
  86.0 3.3 %collective-permute-start.19 = (bf16[24,896]{1,0:T(8,128)(2,1)S(1)}, bf16[24,896]{1,0:T(8,128)(2,1)S(1)}, u32[]{:S(2)}, u32[]{:S(2)}) collective-permute-start(bf16[24,896]{1,0:T(8,128)(2,1)S(1)} %add_convert_fusion.own), channel_id=1, source_target_pairs={{0,64},{16,80},{32,96},{48,112},{64,0},{80,16},{96,32},{112,48},{1... | collective-permute-start | bytes 129032 | tf_op jit(solution)/shard_map/ppermute | solution.py:346
  89.3 8.2 %collective-permute-start.20 = (bf16[4,24,896]{2,1,0:T(8,128)(2,1)S(1)}, bf16[4,24,896]{2,1,0:T(8,128)(2,1)S(1)}, u32[]{:S(2)}, u32[]{:S(2)}) collective-permute-start(bf16[4,24,896]{2,1,0:T(8,128)(2,1)S(1)} %pad_maximum_fusion), channel_id=1, source_target_pairs={{0,16},{16,0},{32,48},{48,32},{64,80},{80,64},{96,112},{112,96},{1... | collective-permute-start | bytes 516104 | tf_op jit(solution)/shard_map/ppermute | solution.py:346

commit v3 on v2

--- a/solution.py
+++ b/solution.py
@@ -53,11 +53,12 @@
         finish(row)
 
 
-def tap_rows(part, row, outs):
+def tap_rows(part, row, outs, first=0, pitch=None):
+    pitch = pitch or outs
     return (
-        part[0:outs, span(row)]
-        + part[outs : 2 * outs, span(row + 1)]
-        + part[2 * outs : 3 * outs, span(row + 2)]
+        part[first : first + outs, span(row)]
+        + part[first + pitch : first + pitch + outs, span(row + 1)]
+        + part[first + 2 * pitch : first + 2 * pitch + outs, span(row + 2)]
     )
 
 
@@ -156,7 +157,7 @@
 def disc_kernel(
     far_a, far_b, near_a, near_b, home, w_one, w_two, w_two_back, w_one_back, w_rgb_back, w_gen_back, w_score, hid, gen,
     grad_in, pack,
-    es, cs, sg, fs, ds, zs, dcs, hzs, part, part_one, part_col, acc, acc_one, acc_rgb, acc_score,
+    es, cs, sg, fs, ds, zs, dcs, hzs, wide, wide_back, part, part_two, part_one, part_col, acc, acc_one, acc_rgb, acc_score,
 ):
     section = lax.axis_index("section")
     frame = lax.axis_index("frame")
@@ -165,6 +166,14 @@
     base = section * 8
     first = frame * 2
     sub = lax.broadcasted_iota(jnp.int32, (8, L), 0)
+
+    blank = jnp.zeros((C, C3), BF)
+    for once, twice in ((w_two, wide), (w_two_back, wide_back)):
+        for dr in range(3):
+            rows = once[C * dr : C * dr + C, :]
+            at = 2 * C * dr
+            twice[at : at + C, :] = jnp.concatenate([rows, blank], axis=1)
+            twice[at + C : at + 2 * C, :] = jnp.concatenate([blank, rows], axis=1)
 
     turn_far, turn_near = (frame >> 1) & 1, frame & 1
     blocks = (
@@ -207,33 +216,33 @@
 
     acc_score[...] = jnp.zeros_like(acc_score)
 
-    def score_step(g, carry):
-        own = inside(g - 2, 2)
-
+    def score_step(p, carry):
         def score_row(row):
-            value = jnp.tanh(tap_rows(part, row, C)).astype(BF).astype(F32)
-            score = sg[g + 2, row : row + 1, :]
-            if 4 <= row < 12:
-                acc_score[...] += value * (score * own)
-            put(ds.at[g], row, w_score[...] * score * (1.0 - value * value))
-
-        staged(part, w_two, lambda s: fs[pl.ds(g, 3), :, s].reshape(3 * C3, -1), 18, 16, 2, score_row)
+            for j in range(2):
+                value = jnp.tanh(tap_rows(part_two, row, C, j * C, 2 * C)).astype(BF).astype(F32)
+                score = sg[2 * p + j + 2, row : row + 1, :]
+                if 4 <= row < 12:
+                    acc_score[...] += value * (score * inside(p - 1, 1))
+                put(ds.at[2 * p + j], row, w_score[...] * score * (1.0 - value * value))
+
+        staged(part_two, wide, lambda s: fs[pl.ds(2 * p, 4), :, s].reshape(4 * C3, -1), 18, 16, 2, score_row)
         return carry
 
-    lax.fori_loop(0, 6, score_step, 0)
-
-    def back_step(h, carry):
-        keep_frame = inside(first + h - 1, frames_all)
-
+    lax.fori_loop(0, 3, score_step, 0)
+
+    def back_step(p, carry):
         def back_row(row):
-            keep = inside(base + row - 3, rows_all) * keep_frame
-            value = fs[h + 2, C : 2 * C, span(row + 2)].astype(F32)
-            put(zs.at[h], row, tap_rows(part, row, C) * ((1.0 - value * value) * keep))
-
-        staged(part, w_two_back, lambda s: ds[pl.ds(h, 3), :, s].reshape(3 * C3, -1), 16, 14, 2, back_row)
+            keep_row = inside(base + row - 3, rows_all)
+            for j in range(2):
+                keep = keep_row * inside(first + 2 * p + j - 1, frames_all)
+                value = fs[2 * p + j + 2, C : 2 * C, span(row + 2)].astype(F32)
+                total = tap_rows(part_two, row, C, j * C, 2 * C)
+                put(zs.at[2 * p + j], row, total * ((1.0 - value * value) * keep))
+
+        staged(part_two, wide_back, lambda s: ds[pl.ds(2 * p, 4), :, s].reshape(4 * C3, -1), 16, 14, 2, back_row)
         return carry
 
-    lax.fori_loop(0, 4, back_step, 0)
+    lax.fori_loop(0, 2, back_step, 0)
 
     for f in range(2):
         feat = fs[f + 2 : f + 5, :, span(4, 10)].reshape(3 * C3, 10 * L)
@@ -332,7 +341,7 @@
         kernel,
         out_shape=outs,
         scratch_shapes=scratch,
-        compiler_params=pltpu.CompilerParams(vmem_limit_bytes=50 << 20),
+        compiler_params=pltpu.CompilerParams(vmem_limit_bytes=52 << 20),
         name=name,
     )
 
@@ -411,7 +420,6 @@
         [pltpu.VMEM((36 * 32, L), F32), pltpu.VMEM((6, C3, L), F32)],
         "weights",
     )(w_disc_two, w_gen_one)
-    score_w = jnp.broadcast_to(w_score.astype(F32)[:, None], (C, L))
 
     mid = call(
         pack_kernel,
@@ -422,6 +430,10 @@
     up = cyclic(mid, "section", 1)
     down = cyclic(mid, "section", -1)
 
+    score_w = jnp.broadcast_to(w_score.astype(F32)[:, None], (C, L))
+    w_rgb, w_one, w_one_back, w_rgb_back, score_w = lax.optimization_barrier(
+        (w_rgb, w_one, w_one_back, w_rgb_back, score_w)
+    )
     near, far, hid, gen_pad = call(
         gen_kernel,
         (
@@ -453,7 +465,10 @@
             pltpu.VMEM((4, C3, 14 * L), BF),
             pltpu.VMEM((16, 12 * L), BF),
             pltpu.VMEM((C3, 10 * L), BF),
+            pltpu.VMEM((2 * C3, 4 * C3), BF),
+            pltpu.VMEM((2 * C3, 4 * C3), BF),
             pltpu.VMEM((C3, 18 * L), F32),
+            pltpu.VMEM((2 * C3, 18 * L), F32),
             pltpu.VMEM((2 * C, 18 * L), F32),
             pltpu.VMEM((24, 14 * L), F32),
             pltpu.VMEM((C3, 12 * C), F32),

time: 99.3 us -> 98.5 us (level)
    ppermute x2, waiting for transfers between devices: 7.11 us -> 6.06 us  [cyclic(): lax.ppermute(value, axis, [(i, (i + step) % size) for i in range(size)])]
    unnamed x25 -> x19, local copies, waits for them, and re-layouts: 3.74 us -> 3.52 us
where the time goes in v3:
time: 98.5 us; the launch traced here: 98.3 us
  starting transfers between devices  45.5 us (46%)
  waiting for transfers between devices  25.1 us (25%)
  Pallas kernels  22.3 us (23%)
  local copies, waits for them, and re-layouts  4.31 us (4%)
    ppermute x15, starting transfers between devices, swapped(): lax.ppermute(value, axis, [(i, i ^ mask) for i in range(lax.axis_size(axi...  27.4 us
    pallas_call x1, Pallas kernels, local(): call(disc_kernel, (jax.ShapeDtypeStruct((C, 2048), BF), jax.ShapeDtypeStr...  16.7 us
    ppermute x15, waiting for transfers between devices, swapped(): lax.ppermute(value, axis, [(i, i ^ mask) for i in range(lax.axis_size(axi...  16 us
    ppermute x4, starting transfers between devices, neighbours(): found.append(lax.ppermute(value, axis, pairs + [(j, i) for i, j in pairs]))  14.7 us
    ppermute x2, waiting for transfers between devices, cyclic(): lax.ppermute(value, axis, [(i, (i + step) % size) for i in range(size)])  6.06 us
    unnamed x19, local copies, waits for them, and re-layouts  3.52 us
    ppermute x2, starting transfers between devices, cyclic(): lax.ppermute(value, axis, [(i, (i + step) % size) for i in range(size)])  3.41 us
    pallas_call x1, Pallas kernels, local(): call(gen_kernel, (jax.ShapeDtypeStruct((C + 32, 2 * L), BF), jax.ShapeDty...  3.07 us
  transfers between devices with their start and end apart: 21, of which 15 were waited for; matrix products, arithmetic and copies ran while one was open for 2% of the time, Pallas kernels for 1%

profile of v3, /device:TPU:1, one launch (start us, length us, event | category | flops | bytes accessed | tf_op | source)
XLA Modules:
  0.0 98.3 jit_solution(2817401815603997057)
XLA Ops:
  0.6 0.9 copy-done
  2.5 3.1 %collective-permute-start = (bf16[80,2048]{1,0:T(8,128)(2,1)S(1)}, bf16[80,2048]{1,0:T(8,128)(2,1)S(1)}, u32[]{:S(2)}, u32[]{:S(2)}) collective-permute-start(bf16[80,2048]{1,0:T(8,128)(2,1)S(1)} %pack.1.mid), channel_id=1, source_target_pairs={{0,16},{16,32},{32,48},{48,64},{64,80},{80,96},{96,112},{112,128},... | collective-permute-start | bytes 983048 | tf_op jit(solution)/shard_map/ppermute | solution.py:351
  8.7 1.0 collective-permute-done.up
  9.6 5.1 %collective-permute-done.1.down = bf16[80,2048]{1,0:T(8,128)(2,1)S(1)} collective-permute-done((bf16[80,2048]{1,0:T(8,128)(2,1)S(1)}, bf16[80,2048]{1,0:T(8,128)(2,1)S(1)}, u32[]{:S(2)}, u32[]{:S(2)}) %collective-permute-start.1) | collective-permute-done | bytes 327712 | tf_op jit(solution)/shard_map/ppermute | solution.py:351
  14.7 3.1 %generator.1 = (bf16[96,256]{1,0:T(8,128)(2,1)S(1)}, bf16[64,256]{1,0:T(8,128)(2,1)S(1)}, bf16[2,192,1280]{2,1,0:T(8,128)(2,1)}, bf16[2,192,1280]{2,1,0:T(8,128)(2,1)}) custom-call(bf16[80,2048]{1,0:T(8,128)(2,1)S(1)} %collective-permute-done.up, bf16[80,2048]{1,0:T(8,128)(2,1)S(1)} %pack.1.mid, bf16[80,2048]{1,0:T(8,128)(2,1)S(1)} %collective-permute-done.1.down, ...), custom_call_target="tpu_custom_call" | custom-call | tf_op jit(solution)/shard_map/generator/pallas_call | solution.py:437
  17.8 2.7 %collective-permute-start.4 = (bf16[96,256]{1,0:T(8,128)(2,1)S(1)}, bf16[96,256]{1,0:T(8,128)(2,1)S(1)}, u32[]{:S(2)}, u32[]{:S(2)}) collective-permute-start(bf16[96,256]{1,0:T(8,128)(2,1)S(1)} %get-tuple-element.29.home), channel_id=1, source_target_pairs={{0,1},{2,3},{4,5},{6,7},{8,9},{10,11},{12,13},{14,15},{1,0},{3,2},... | collective-permute-start | bytes 147464 | tf_op jit(solution)/shard_map/ppermute | solution.py:363
  20.5 6.4 %collective-permute-start.5 = (bf16[96,256]{1,0:T(8,128)(2,1)S(1)}, bf16[96,256]{1,0:T(8,128)(2,1)S(1)}, u32[]{:S(2)}, u32[]{:S(2)}) collective-permute-start(bf16[96,256]{1,0:T(8,128)(2,1)S(1)} %get-tuple-element.29.home), channel_id=1, source_target_pairs={{1,2},{3,4},{5,6},{7,8},{9,10},{11,12},{13,14},{15,0},{2,1},{4,3},... | collective-permute-start | bytes 147464 | tf_op jit(solution)/shard_map/ppermute | solution.py:363
  26.9 5.6 %collective-permute-start.3 = (bf16[64,256]{1,0:T(8,128)(2,1)S(1)}, bf16[64,256]{1,0:T(8,128)(2,1)S(1)}, u32[]{:S(2)}, u32[]{:S(2)}) collective-permute-start(bf16[64,256]{1,0:T(8,128)(2,1)S(1)} %get-tuple-element.28), channel_id=1, source_target_pairs={{2,4},{3,5},{6,8},{7,9},{10,12},{11,13},{14,0},{15,1},{4,2},{5,3},... | collective-permute-start | bytes 98312 | tf_op jit(solution)/shard_map/ppermute | solution.py:363
  32.6 1.0 %collective-permute-done.2.far_a = bf16[64,256]{1,0:T(8,128)(2,1)S(1)} collective-permute-done((bf16[64,256]{1,0:T(8,128)(2,1)S(1)}, bf16[64,256]{1,0:T(8,128)(2,1)S(1)}, u32[]{:S(2)}, u32[]{:S(2)}) %collective-permute-start.2) | collective-permute-done | bytes 32800 | tf_op jit(solution)/shard_map/ppermute | solution.py:363
  33.7 2.0 %collective-permute-done.3.far_b = bf16[64,256]{1,0:T(8,128)(2,1)S(1)} collective-permute-done((bf16[64,256]{1,0:T(8,128)(2,1)S(1)}, bf16[64,256]{1,0:T(8,128)(2,1)S(1)}, u32[]{:S(2)}, u32[]{:S(2)}) %collective-permute-start.3) | collective-permute-done | bytes 32800 | tf_op jit(solution)/shard_map/ppermute | solution.py:363
  35.7 16.7 %discriminator.1 = (bf16[64,2048]{1,0:T(8,128)(2,1)S(1)}, bf16[8,24,896]{2,1,0:T(8,128)(2,1)S(1)}) custom-call(bf16[64,256]{1,0:T(8,128)(2,1)S(1)} %collective-permute-done.2.far_a, bf16[64,256]{1,0:T(8,128)(2,1)S(1)} %collective-permute-done.3.far_b, bf16[96,256]{1,0:T(8,128)(2,1)S(1)} %collective-permute-done.4.near_a, ...), custom_call_target="tpu_custom_call" | custom-call | tf_op jit(solution)/shard_map/discriminator/pallas_call | solution.py:456
  52.4 1.9 %collective-permute-start.6 = (bf16[4,24,896]{2,1,0:T(8,128)(2,1)S(1)}, bf16[4,24,896]{2,1,0:T(8,128)(2,1)S(1)}, u32[]{:S(2)}, u32[]{:S(2)}) collective-permute-start(bf16[4,24,896]{2,1,0:T(8,128)(2,1)S(1)} %dynamic-slice_bitcast_fusion), channel_id=1, source_target_pairs={{0,16},{16,0},{32,48},{48,32},{64,80},{80,64},{96,112},{112,96},{1... | collective-permute-start | bytes 516104 | tf_op jit(solution)/shard_map/ppermute | solution.py:355
  54.3 1.0 %collective-permute-done.6 = bf16[4,24,896]{2,1,0:T(8,128)(2,1)S(1)} collective-permute-done((bf16[4,24,896]{2,1,0:T(8,128)(2,1)S(1)}, bf16[4,24,896]{2,1,0:T(8,128)(2,1)S(1)}, u32[]{:S(2)}, u32[]{:S(2)}) %collective-permute-start.6) | collective-permute-done | bytes 172064 | tf_op jit(solution)/shard_map/ppermute | solution.py:355
  55.4 1.6 %collective-permute-start.7 = (bf16[24,896]{1,0:T(8,128)(2,1)S(1)}, bf16[24,896]{1,0:T(8,128)(2,1)S(1)}, u32[]{:S(2)}, u32[]{:S(2)}) collective-permute-start(bf16[24,896]{1,0:T(8,128)(2,1)S(1)} %get-tuple-element.46), channel_id=1, source_target_pairs={{0,64},{16,80},{32,96},{48,112},{64,0},{80,16},{96,32},{112,48},{1... | collective-permute-start | bytes 129032 | tf_op jit(solution)/shard_map/ppermute | solution.py:355
  57.0 1.9 %collective-permute-start.8 = (bf16[24,896]{1,0:T(8,128)(2,1)S(1)}, bf16[24,896]{1,0:T(8,128)(2,1)S(1)}, u32[]{:S(2)}, u32[]{:S(2)}) collective-permute-start(bf16[24,896]{1,0:T(8,128)(2,1)S(1)} %get-tuple-element.48), channel_id=1, source_target_pairs={{0,192},{16,208},{32,224},{48,240},{64,128},{80,144},{96,160},{112... | collective-permute-start | bytes 129032 | tf_op jit(solution)/shard_map/ppermute | solution.py:355
  58.9 0.8 collective-permute-start.9
  59.7 1.3 %collective-permute-done.8 = bf16[24,896]{1,0:T(8,128)(2,1)S(1)} collective-permute-done((bf16[24,896]{1,0:T(8,128)(2,1)S(1)}, bf16[24,896]{1,0:T(8,128)(2,1)S(1)}, u32[]{:S(2)}, u32[]{:S(2)}) %collective-permute-start.8) | collective-permute-done | bytes 43040 | tf_op jit(solution)/shard_map/ppermute | solution.py:355
  61.1 2.2 %collective-permute-done.9 = bf16[24,896]{1,0:T(8,128)(2,1)S(1)} collective-permute-done((bf16[24,896]{1,0:T(8,128)(2,1)S(1)}, bf16[24,896]{1,0:T(8,128)(2,1)S(1)}, u32[]{:S(2)}, u32[]{:S(2)}) %collective-permute-start.9) | collective-permute-done | bytes 43040 | tf_op jit(solution)/shard_map/ppermute | solution.py:355
  63.4 1.2 %collective-permute-start.11 = (bf16[24,896]{1,0:T(8,128)(2,1)S(1)}, bf16[24,896]{1,0:T(8,128)(2,1)S(1)}, u32[]{:S(2)}, u32[]{:S(2)}) collective-permute-start(bf16[24,896]{1,0:T(8,128)(2,1)S(1)} %fusion.5), channel_id=1, source_target_pairs={{0,8},{1,9},{2,10},{3,11},{4,12},{5,13},{6,14},{7,15},{8,0},{9,1},... | collective-permute-start | bytes 129032 | tf_op jit(solution)/shard_map/ppermute | solution.py:355
  64.6 2.0 %collective-permute-start.12 = (bf16[24,896]{1,0:T(8,128)(2,1)S(1)}, bf16[24,896]{1,0:T(8,128)(2,1)S(1)}, u32[]{:S(2)}, u32[]{:S(2)}) collective-permute-start(bf16[24,896]{1,0:T(8,128)(2,1)S(1)} %fusion.5), channel_id=1, source_target_pairs={{0,4},{1,5},{2,6},{3,7},{4,0},{5,1},{6,2},{7,3},{8,12},{9,13},{10,... | collective-permute-start | bytes 129032 | tf_op jit(solution)/shard_map/ppermute | solution.py:355
  66.6 0.8 collective-permute-done.10
  69.2 2.4 %collective-permute-done.13 = bf16[24,896]{1,0:T(8,128)(2,1)S(1)} collective-permute-done((bf16[24,896]{1,0:T(8,128)(2,1)S(1)}, bf16[24,896]{1,0:T(8,128)(2,1)S(1)}, u32[]{:S(2)}, u32[]{:S(2)}) %collective-permute-start.13) | collective-permute-done | bytes 43040 | tf_op jit(solution)/shard_map/ppermute | solution.py:355
  71.6 4.4 %collective-permute-start.14 = (bf16[24,896]{1,0:T(8,128)(2,1)S(1)}, bf16[24,896]{1,0:T(8,128)(2,1)S(1)}, u32[]{:S(2)}, u32[]{:S(2)}) collective-permute-start(bf16[24,896]{1,0:T(8,128)(2,1)S(1)} %add_convert_fusion.1), channel_id=1, source_target_pairs={{0,3},{1,2},{2,1},{3,0},{4,7},{5,6},{6,5},{7,4},{8,11},{9,10},{10,... | collective-permute-start | bytes 129032 | tf_op jit(solution)/shard_map/ppermute | solution.py:355
  76.1 1.2 %collective-permute-start.15 = (bf16[24,896]{1,0:T(8,128)(2,1)S(1)}, bf16[24,896]{1,0:T(8,128)(2,1)S(1)}, u32[]{:S(2)}, u32[]{:S(2)}) collective-permute-start(bf16[24,896]{1,0:T(8,128)(2,1)S(1)} %add_convert_fusion.1), channel_id=1, source_target_pairs={{0,2},{1,3},{2,0},{3,1},{4,6},{5,7},{6,4},{7,5},{8,10},{9,11},{10,... | collective-permute-start | bytes 129032 | tf_op jit(solution)/shard_map/ppermute | solution.py:355
  77.3 1.0 collective-permute-start.16
  78.2 4.9 %collective-permute-done.15 = bf16[24,896]{1,0:T(8,128)(2,1)S(1)} collective-permute-done((bf16[24,896]{1,0:T(8,128)(2,1)S(1)}, bf16[24,896]{1,0:T(8,128)(2,1)S(1)}, u32[]{:S(2)}, u32[]{:S(2)}) %collective-permute-start.15) | collective-permute-done | bytes 43040 | tf_op jit(solution)/shard_map/ppermute | solution.py:355
  83.2 0.9 collective-permute-start.17
  84.1 1.1 %collective-permute-start.18 = (bf16[24,896]{1,0:T(8,128)(2,1)S(1)}, bf16[24,896]{1,0:T(8,128)(2,1)S(1)}, u32[]{:S(2)}, u32[]{:S(2)}) collective-permute-start(bf16[24,896]{1,0:T(8,128)(2,1)S(1)} %add_convert_fusion.own), channel_id=1, source_target_pairs={{0,128},{16,144},{32,160},{48,176},{64,192},{80,208},{96,224},{112... | collective-permute-start | bytes 129032 | tf_op jit(solution)/shard_map/ppermute | solution.py:355
  85.2 1.4 %collective-permute-start.19 = (bf16[24,896]{1,0:T(8,128)(2,1)S(1)}, bf16[24,896]{1,0:T(8,128)(2,1)S(1)}, u32[]{:S(2)}, u32[]{:S(2)}) collective-permute-start(bf16[24,896]{1,0:T(8,128)(2,1)S(1)} %add_convert_fusion.own), channel_id=1, source_target_pairs={{0,64},{16,80},{32,96},{48,112},{64,0},{80,16},{96,32},{112,48},{1... | collective-permute-start | bytes 129032 | tf_op jit(solution)/shard_map/ppermute | solution.py:355
  86.6 1.1 %collective-permute-done.17.three = bf16[24,896]{1,0:T(8,128)(2,1)S(1)} collective-permute-done((bf16[24,896]{1,0:T(8,128)(2,1)S(1)}, bf16[24,896]{1,0:T(8,128)(2,1)S(1)}, u32[]{:S(2)}, u32[]{:S(2)}) %collective-permute-start.17) | collective-permute-done | bytes 43040 | tf_op jit(solution)/shard_map/ppermute | solution.py:355
  88.5 7.2 %collective-permute-start.20 = (bf16[4,24,896]{2,1,0:T(8,128)(2,1)S(1)}, bf16[4,24,896]{2,1,0:T(8,128)(2,1)S(1)}, u32[]{:S(2)}, u32[]{:S(2)}) collective-permute-start(bf16[4,24,896]{2,1,0:T(8,128)(2,1)S(1)} %pad_maximum_fusion), channel_id=1, source_target_pairs={{0,16},{16,0},{32,48},{48,32},{64,80},{80,64},{96,112},{112,96},{1... | collective-permute-start | bytes 516104 | tf_op jit(solution)/shard_map/ppermute | solution.py:355
  96.7 1.6 %finish.1 = (f32[9,4096]{1,0:T(8,128)}, f32[3,3,3,64]{3,2,1,0:T(4,128)}, f32[3,3,3,3,64]{4,3,2,1,0:T(4,128)}, f32[27,4096]{1,0:T(8,128)}, f32[1,64]{1,0:T(1,128)}) custom-call(bf16[24,896]{1,0:T(8,128)(2,1)S(1)} %add_convert_fusion.own, bf16[24,896]{1,0:T(8,128)(2,1)S(1)} %collective-permute-done.17.three, bf16[24,896]{1,0:T(8,128)(2,1)S(1)} %collective-permute-done.18.two, ...), custom_call_target="tpu_custom_call" | custom-call | tf_op jit(solution)/shard_map/finish/pallas_call | solution.py:485
  (55 shorter events, 7.9 us)
Async XLA Ops:
  0.6 1.0 copy-start
  1.6 0.7 copy-start.3
  2.3 3.6 %copy-start.4 = (bf16[64,3,3,3,3]{0,4,3,2,1:T(4,128)(2,1)S(1)}, bf16[64,3,3,3,3]{0,4,3,2,1:T(4,128)(2,1)}, u32[]{:S(2)}) copy-start(bf16[64,3,3,3,3]{0,4,3,2,1:T(4,128)(2,1)} %param.10) | copy-start | bytes 31108
  2.5 7.1 %collective-permute-start = (bf16[80,2048]{1,0:T(8,128)(2,1)S(1)}, bf16[80,2048]{1,0:T(8,128)(2,1)S(1)}, u32[]{:S(2)}, u32[]{:S(2)}) collective-permute-start(bf16[80,2048]{1,0:T(8,128)(2,1)S(1)} %pack.1.mid), channel_id=1, source_target_pairs={{0,16},{16,32},{32,48},{48,64},{64,80},{80,96},{96,112},{112,128},... | collective-permute-start | bytes 983048 | tf_op jit(solution)/shard_map/ppermute | solution.py:351
  5.6 9.1 %collective-permute-start.1 = (bf16[80,2048]{1,0:T(8,128)(2,1)S(1)}, bf16[80,2048]{1,0:T(8,128)(2,1)S(1)}, u32[]{:S(2)}, u32[]{:S(2)}) collective-permute-start(bf16[80,2048]{1,0:T(8,128)(2,1)S(1)} %pack.1.mid), channel_id=1, source_target_pairs={{0,240},{16,0},{32,16},{48,32},{64,48},{80,64},{96,80},{112,96},{1... | collective-permute-start | bytes 983048 | tf_op jit(solution)/shard_map/ppermute | solution.py:351
  6.1 0.7 copy-start.5
  6.2 1.7 %copy-start.1 = (bf16[27,4096]{1,0:T(8,128)(2,1)S(1)}, bf16[27,4096]{1,0:T(8,128)(2,1)}, u32[]{:S(2)}) copy-start(bf16[27,4096]{1,0:T(8,128)(2,1)} %flat_two.1) | copy-start | bytes 663556
  6.9 1.0 copy-start.2
  7.1 0.7 copy-start.6
  17.8 17.9 %collective-permute-start.4 = (bf16[96,256]{1,0:T(8,128)(2,1)S(1)}, bf16[96,256]{1,0:T(8,128)(2,1)S(1)}, u32[]{:S(2)}, u32[]{:S(2)}) collective-permute-start(bf16[96,256]{1,0:T(8,128)(2,1)S(1)} %get-tuple-element.29.home), channel_id=1, source_target_pairs={{0,1},{2,3},{4,5},{6,7},{8,9},{10,11},{12,13},{14,15},{1,0},{3,2},... | collective-permute-start | bytes 147464 | tf_op jit(solution)/shard_map/ppermute | solution.py:363
  20.5 15.2 %collective-permute-start.5 = (bf16[96,256]{1,0:T(8,128)(2,1)S(1)}, bf16[96,256]{1,0:T(8,128)(2,1)S(1)}, u32[]{:S(2)}, u32[]{:S(2)}) collective-permute-start(bf16[96,256]{1,0:T(8,128)(2,1)S(1)} %get-tuple-element.29.home), channel_id=1, source_target_pairs={{1,2},{3,4},{5,6},{7,8},{9,10},{11,12},{13,14},{15,0},{2,1},{4,3},... | collective-permute-start | bytes 147464 | tf_op jit(solution)/shard_map/ppermute | solution.py:363
  26.9 6.8 %collective-permute-start.2 = (bf16[64,256]{1,0:T(8,128)(2,1)S(1)}, bf16[64,256]{1,0:T(8,128)(2,1)S(1)}, u32[]{:S(2)}, u32[]{:S(2)}) collective-permute-start(bf16[64,256]{1,0:T(8,128)(2,1)S(1)} %get-tuple-element.28), channel_id=1, source_target_pairs={{0,2},{1,3},{4,6},{5,7},{8,10},{9,11},{12,14},{13,15},{2,0},{3,1},... | collective-permute-start | bytes 98312 | tf_op jit(solution)/shard_map/ppermute | solution.py:363
  26.9 8.8 %collective-permute-start.3 = (bf16[64,256]{1,0:T(8,128)(2,1)S(1)}, bf16[64,256]{1,0:T(8,128)(2,1)S(1)}, u32[]{:S(2)}, u32[]{:S(2)}) collective-permute-start(bf16[64,256]{1,0:T(8,128)(2,1)S(1)} %get-tuple-element.28), channel_id=1, source_target_pairs={{2,4},{3,5},{6,8},{7,9},{10,12},{11,13},{14,0},{15,1},{4,2},{5,3},... | collective-permute-start | bytes 98312 | tf_op jit(solution)/shard_map/ppermute | solution.py:363
  52.4 2.9 %collective-permute-start.6 = (bf16[4,24,896]{2,1,0:T(8,128)(2,1)S(1)}, bf16[4,24,896]{2,1,0:T(8,128)(2,1)S(1)}, u32[]{:S(2)}, u32[]{:S(2)}) collective-permute-start(bf16[4,24,896]{2,1,0:T(8,128)(2,1)S(1)} %dynamic-slice_bitcast_fusion), channel_id=1, source_target_pairs={{0,16},{16,0},{32,48},{48,32},{64,80},{80,64},{96,112},{112,96},{1... | collective-permute-start | bytes 516104 | tf_op jit(solution)/shard_map/ppermute | solution.py:355
  55.4 4.3 %collective-permute-start.7 = (bf16[24,896]{1,0:T(8,128)(2,1)S(1)}, bf16[24,896]{1,0:T(8,128)(2,1)S(1)}, u32[]{:S(2)}, u32[]{:S(2)}) collective-permute-start(bf16[24,896]{1,0:T(8,128)(2,1)S(1)} %get-tuple-element.46), channel_id=1, source_target_pairs={{0,64},{16,80},{32,96},{48,112},{64,0},{80,16},{96,32},{112,48},{1... | collective-permute-start | bytes 129032 | tf_op jit(solution)/shard_map/ppermute | solution.py:355
  57.0 4.1 %collective-permute-start.8 = (bf16[24,896]{1,0:T(8,128)(2,1)S(1)}, bf16[24,896]{1,0:T(8,128)(2,1)S(1)}, u32[]{:S(2)}, u32[]{:S(2)}) collective-permute-start(bf16[24,896]{1,0:T(8,128)(2,1)S(1)} %get-tuple-element.48), channel_id=1, source_target_pairs={{0,192},{16,208},{32,224},{48,240},{64,128},{80,144},{96,160},{112... | collective-permute-start | bytes 129032 | tf_op jit(solution)/shard_map/ppermute | solution.py:355
  58.9 4.4 %collective-permute-start.9 = (bf16[24,896]{1,0:T(8,128)(2,1)S(1)}, bf16[24,896]{1,0:T(8,128)(2,1)S(1)}, u32[]{:S(2)}, u32[]{:S(2)}) collective-permute-start(bf16[24,896]{1,0:T(8,128)(2,1)S(1)} %get-tuple-element.47), channel_id=1, source_target_pairs={{0,128},{16,144},{32,160},{48,176},{64,192},{80,208},{96,224},{112... | collective-permute-start | bytes 129032 | tf_op jit(solution)/shard_map/ppermute | solution.py:355
  63.3 4.2 %collective-permute-start.10 = (bf16[24,896]{1,0:T(8,128)(2,1)S(1)}, bf16[24,896]{1,0:T(8,128)(2,1)S(1)}, u32[]{:S(2)}, u32[]{:S(2)}) collective-permute-start(bf16[24,896]{1,0:T(8,128)(2,1)S(1)} %fusion.5), channel_id=1, source_target_pairs={{0,12},{1,13},{2,14},{3,15},{4,8},{5,9},{6,10},{7,11},{8,4},{9,5},... | collective-permute-start | bytes 129032 | tf_op jit(solution)/shard_map/ppermute | solution.py:355
  63.4 4.5 %collective-permute-start.11 = (bf16[24,896]{1,0:T(8,128)(2,1)S(1)}, bf16[24,896]{1,0:T(8,128)(2,1)S(1)}, u32[]{:S(2)}, u32[]{:S(2)}) collective-permute-start(bf16[24,896]{1,0:T(8,128)(2,1)S(1)} %fusion.5), channel_id=1, source_target_pairs={{0,8},{1,9},{2,10},{3,11},{4,12},{5,13},{6,14},{7,15},{8,0},{9,1},... | collective-permute-start | bytes 129032 | tf_op jit(solution)/shard_map/ppermute | solution.py:355
  64.6 3.9 %collective-permute-start.12 = (bf16[24,896]{1,0:T(8,128)(2,1)S(1)}, bf16[24,896]{1,0:T(8,128)(2,1)S(1)}, u32[]{:S(2)}, u32[]{:S(2)}) collective-permute-start(bf16[24,896]{1,0:T(8,128)(2,1)S(1)} %fusion.5), channel_id=1, source_target_pairs={{0,4},{1,5},{2,6},{3,7},{4,0},{5,1},{6,2},{7,3},{8,12},{9,13},{10,... | collective-permute-start | bytes 129032 | tf_op jit(solution)/shard_map/ppermute | solution.py:355
  68.5 3.1 %collective-permute-start.13 = (bf16[24,896]{1,0:T(8,128)(2,1)S(1)}, bf16[24,896]{1,0:T(8,128)(2,1)S(1)}, u32[]{:S(2)}, u32[]{:S(2)}) collective-permute-start(bf16[24,896]{1,0:T(8,128)(2,1)S(1)} %add_convert_fusion.2), channel_id=1, source_target_pairs={{0,32},{16,48},{32,0},{48,16},{64,96},{80,112},{96,64},{112,80},{1... | collective-permute-start | bytes 129032 | tf_op jit(solution)/shard_map/ppermute | solution.py:355
  71.6 6.6 %collective-permute-start.14 = (bf16[24,896]{1,0:T(8,128)(2,1)S(1)}, bf16[24,896]{1,0:T(8,128)(2,1)S(1)}, u32[]{:S(2)}, u32[]{:S(2)}) collective-permute-start(bf16[24,896]{1,0:T(8,128)(2,1)S(1)} %add_convert_fusion.1), channel_id=1, source_target_pairs={{0,3},{1,2},{2,1},{3,0},{4,7},{5,6},{6,5},{7,4},{8,11},{9,10},{10,... | collective-permute-start | bytes 129032 | tf_op jit(solution)/shard_map/ppermute | solution.py:355
  76.1 7.1 %collective-permute-start.15 = (bf16[24,896]{1,0:T(8,128)(2,1)S(1)}, bf16[24,896]{1,0:T(8,128)(2,1)S(1)}, u32[]{:S(2)}, u32[]{:S(2)}) collective-permute-start(bf16[24,896]{1,0:T(8,128)(2,1)S(1)} %add_convert_fusion.1), channel_id=1, source_target_pairs={{0,2},{1,3},{2,0},{3,1},{4,6},{5,7},{6,4},{7,5},{8,10},{9,11},{10,... | collective-permute-start | bytes 129032 | tf_op jit(solution)/shard_map/ppermute | solution.py:355
  77.3 5.9 %collective-permute-start.16 = (bf16[24,896]{1,0:T(8,128)(2,1)S(1)}, bf16[24,896]{1,0:T(8,128)(2,1)S(1)}, u32[]{:S(2)}, u32[]{:S(2)}) collective-permute-start(bf16[24,896]{1,0:T(8,128)(2,1)S(1)} %add_convert_fusion.1), channel_id=1, source_target_pairs={{0,1},{1,0},{2,3},{3,2},{4,5},{5,4},{6,7},{7,6},{8,9},{9,8},{10,11... | collective-permute-start | bytes 129032 | tf_op jit(solution)/shard_map/ppermute | solution.py:355
  83.2 4.5 %collective-permute-start.17 = (bf16[24,896]{1,0:T(8,128)(2,1)S(1)}, bf16[24,896]{1,0:T(8,128)(2,1)S(1)}, u32[]{:S(2)}, u32[]{:S(2)}) collective-permute-start(bf16[24,896]{1,0:T(8,128)(2,1)S(1)} %add_convert_fusion.own), channel_id=1, source_target_pairs={{0,192},{16,208},{32,224},{48,240},{64,128},{80,144},{96,160},{112... | collective-permute-start | bytes 129032 | tf_op jit(solution)/shard_map/ppermute | solution.py:355
  84.1 4.4 %collective-permute-start.18 = (bf16[24,896]{1,0:T(8,128)(2,1)S(1)}, bf16[24,896]{1,0:T(8,128)(2,1)S(1)}, u32[]{:S(2)}, u32[]{:S(2)}) collective-permute-start(bf16[24,896]{1,0:T(8,128)(2,1)S(1)} %add_convert_fusion.own), channel_id=1, source_target_pairs={{0,128},{16,144},{32,160},{48,176},{64,192},{80,208},{96,224},{112... | collective-permute-start | bytes 129032 | tf_op jit(solution)/shard_map/ppermute | solution.py:355
  85.2 3.3 %collective-permute-start.19 = (bf16[24,896]{1,0:T(8,128)(2,1)S(1)}, bf16[24,896]{1,0:T(8,128)(2,1)S(1)}, u32[]{:S(2)}, u32[]{:S(2)}) collective-permute-start(bf16[24,896]{1,0:T(8,128)(2,1)S(1)} %add_convert_fusion.own), channel_id=1, source_target_pairs={{0,64},{16,80},{32,96},{48,112},{64,0},{80,16},{96,32},{112,48},{1... | collective-permute-start | bytes 129032 | tf_op jit(solution)/shard_map/ppermute | solution.py:355
  88.5 8.2 %collective-permute-start.20 = (bf16[4,24,896]{2,1,0:T(8,128)(2,1)S(1)}, bf16[4,24,896]{2,1,0:T(8,128)(2,1)S(1)}, u32[]{:S(2)}, u32[]{:S(2)}) collective-permute-start(bf16[4,24,896]{2,1,0:T(8,128)(2,1)S(1)} %pad_maximum_fusion), channel_id=1, source_target_pairs={{0,16},{16,0},{32,48},{48,32},{64,80},{80,64},{96,112},{112,96},{1... | collective-permute-start | bytes 516104 | tf_op jit(solution)/shard_map/ppermute | solution.py:355

commit v4 on v3

--- a/solution.py
+++ b/solution.py
@@ -111,11 +111,17 @@
         mirror = slice(C * (2 - dr), C * (2 - dr) + C)
         ahead = [blocks[b, rows, :] for b in range(6)]
         ahead = [block[:, C * h : C * h + C] for block in ahead for h in range(2)]
-        two[rows, :] = jnp.concatenate(ahead[:9], axis=1).astype(BF)
+        once = jnp.concatenate(ahead[:9], axis=1).astype(BF)
+        blank = jnp.zeros((C, C3), BF)
+        two[2 * C * dr : 2 * C * dr + C, :] = jnp.concatenate([once, blank], axis=1)
+        two[2 * C * dr + C : 2 * C * dr + 2 * C, :] = jnp.concatenate([blank, once], axis=1)
         gen[rows, :] = jnp.concatenate(ahead[9:], axis=1).astype(BF)
         back = [jnp.transpose(blocks[b, rows, :]) for b in range(6)]
         back = [block[C * h : C * h + C, :] for block in back for h in range(2)]
-        two_back[mirror, :] = jnp.concatenate(back[8::-1], axis=1).astype(BF)
+        once = jnp.concatenate(back[8::-1], axis=1).astype(BF)
+        at = 2 * C * (2 - dr)
+        two_back[at : at + C, :] = jnp.concatenate([once, blank], axis=1)
+        two_back[at + C : at + 2 * C, :] = jnp.concatenate([blank, once], axis=1)
         gen_back[mirror, :] = jnp.concatenate(back[:8:-1], axis=1).astype(BF)
 
 
@@ -157,7 +163,7 @@
 def disc_kernel(
     far_a, far_b, near_a, near_b, home, w_one, w_two, w_two_back, w_one_back, w_rgb_back, w_gen_back, w_score, hid, gen,
     grad_in, pack,
-    es, cs, sg, fs, ds, zs, dcs, hzs, wide, wide_back, part, part_two, part_one, part_col, acc, acc_one, acc_rgb, acc_score,
+    es, cs, sg, fs, ds, zs, dcs, hzs, part, part_two, part_one, part_col, acc, acc_one, acc_rgb, acc_score,
 ):
     section = lax.axis_index("section")
     frame = lax.axis_index("frame")
@@ -166,14 +172,6 @@
     base = section * 8
     first = frame * 2
     sub = lax.broadcasted_iota(jnp.int32, (8, L), 0)
-
-    blank = jnp.zeros((C, C3), BF)
-    for once, twice in ((w_two, wide), (w_two_back, wide_back)):
-        for dr in range(3):
-            rows = once[C * dr : C * dr + C, :]
-            at = 2 * C * dr
-            twice[at : at + C, :] = jnp.concatenate([rows, blank], axis=1)
-            twice[at + C : at + 2 * C, :] = jnp.concatenate([blank, rows], axis=1)
 
     turn_far, turn_near = (frame >> 1) & 1, frame & 1
     blocks = (
@@ -225,7 +223,7 @@
                     acc_score[...] += value * (score * inside(p - 1, 1))
                 put(ds.at[2 * p + j], row, w_score[...] * score * (1.0 - value * value))
 
-        staged(part_two, wide, lambda s: fs[pl.ds(2 * p, 4), :, s].reshape(4 * C3, -1), 18, 16, 2, score_row)
+        staged(part_two, w_two, lambda s: fs[pl.ds(2 * p, 4), :, s].reshape(4 * C3, -1), 18, 16, 2, score_row)
         return carry
 
     lax.fori_loop(0, 3, score_step, 0)
@@ -239,7 +237,7 @@
                 total = tap_rows(part_two, row, C, j * C, 2 * C)
                 put(zs.at[2 * p + j], row, total * ((1.0 - value * value) * keep))
 
-        staged(part_two, wide_back, lambda s: ds[pl.ds(2 * p, 4), :, s].reshape(4 * C3, -1), 16, 14, 2, back_row)
+        staged(part_two, w_two_back, lambda s: ds[pl.ds(2 * p, 4), :, s].reshape(4 * C3, -1), 16, 14, 2, back_row)
         return carry
 
     lax.fori_loop(0, 2, back_step, 0)
@@ -341,7 +339,7 @@
         kernel,
         out_shape=outs,
         scratch_shapes=scratch,
-        compiler_params=pltpu.CompilerParams(vmem_limit_bytes=52 << 20),
+        compiler_params=pltpu.CompilerParams(vmem_limit_bytes=50 << 20),
         name=name,
     )
 
@@ -412,8 +410,8 @@
     w_two, w_two_back, w_gen, w_gen_back = call(
         weight_kernel,
         (
-            jax.ShapeDtypeStruct((C3, 3 * C3), BF),
-            jax.ShapeDtypeStruct((C3, 3 * C3), BF),
+            jax.ShapeDtypeStruct((2 * C3, 4 * C3), BF),
+            jax.ShapeDtypeStruct((2 * C3, 4 * C3), BF),
             jax.ShapeDtypeStruct((C3, C3), BF),
             jax.ShapeDtypeStruct((C3, C3), BF),
         ),
@@ -465,8 +463,6 @@
             pltpu.VMEM((4, C3, 14 * L), BF),
             pltpu.VMEM((16, 12 * L), BF),
             pltpu.VMEM((C3, 10 * L), BF),
-            pltpu.VMEM((2 * C3, 4 * C3), BF),
-            pltpu.VMEM((2 * C3, 4 * C3), BF),
             pltpu.VMEM((C3, 18 * L), F32),
             pltpu.VMEM((2 * C3, 18 * L), F32),
             pltpu.VMEM((2 * C, 18 * L), F32),

time: 98.5 us -> 97.8 us (level)
  Pallas kernels: 22.3 us -> 20.9 us
    pallas_call x1, Pallas kernels: 3.07 us -> 1.89 us  [local(): call(gen_kernel, (jax.ShapeDtypeStruct((C + 32, 2 * L), BF), jax.ShapeDty...]
    unnamed x19 -> x21, local copies, waits for them, and re-layouts: 3.52 us -> 4.47 us
where the time goes in v4:
time: 97.8 us; the launch traced here: 97.5 us
  starting transfers between devices  45.5 us (47%)
  waiting for transfers between devices  24.8 us (25%)
  Pallas kernels  20.9 us (21%)
  local copies, waits for them, and re-layouts  5.26 us (5%)
    ppermute x15, starting transfers between devices, swapped(): lax.ppermute(value, axis, [(i, i ^ mask) for i in range(lax.axis_size(axi...  27.4 us
    pallas_call x1, Pallas kernels, local(): call(disc_kernel, (jax.ShapeDtypeStruct((C, 2048), BF), jax.ShapeDtypeStr...  16.2 us
    ppermute x15, waiting for transfers between devices, swapped(): lax.ppermute(value, axis, [(i, i ^ mask) for i in range(lax.axis_size(axi...  16 us
    ppermute x4, starting transfers between devices, neighbours(): found.append(lax.ppermute(value, axis, pairs + [(j, i) for i, j in pairs]))  14.7 us
    ppermute x2, waiting for transfers between devices, cyclic(): lax.ppermute(value, axis, [(i, (i + step) % size) for i in range(size)])  5.78 us
    unnamed x21, local copies, waits for them, and re-layouts  4.47 us
    ppermute x2, starting transfers between devices, cyclic(): lax.ppermute(value, axis, [(i, (i + step) % size) for i in range(size)])  3.41 us
    ppermute x4, waiting for transfers between devices, neighbours(): found.append(lax.ppermute(value, axis, pairs + [(j, i) for i, j in pairs]))  3.03 us
  transfers between devices with their start and end apart: 21, of which 15 were waited for; matrix products, arithmetic and copies ran while one was open for 2% of the time, Pallas kernels for 1%

profile of v4, /device:TPU:1, one launch (start us, length us, event | category | flops | bytes accessed | tf_op | source)
XLA Modules:
  0.0 97.5 jit_solution(15704440116887844639)
XLA Ops:
  0.6 0.9 copy-done.1
  2.5 3.1 %collective-permute-start = (bf16[80,2048]{1,0:T(8,128)(2,1)S(1)}, bf16[80,2048]{1,0:T(8,128)(2,1)S(1)}, u32[]{:S(2)}, u32[]{:S(2)}) collective-permute-start(bf16[80,2048]{1,0:T(8,128)(2,1)S(1)} %pack.1.mid), channel_id=1, source_target_pairs={{0,16},{16,32},{32,48},{48,64},{64,80},{80,96},{96,112},{112,128},... | collective-permute-start | bytes 983048 | tf_op jit(solution)/shard_map/ppermute | solution.py:349
  7.9 1.1 %weights.1 = (bf16[384,768]{1,0:T(8,128)(2,1)S(1)}, bf16[384,768]{1,0:T(8,128)(2,1)S(1)}, bf16[192,192]{1,0:T(8,128)(2,1)S(1)}, bf16[192,192]{1,0:T(8,128)(2,1)S(1)}) custom-call(bf16[27,4096]{1,0:T(8,128)(2,1)S(1)} %copy-done.2, bf16[9,4096]{1,0:T(8,128)(2,1)S(1)} %copy-done.3), custom_call_target="tpu_custom_call" | custom-call | tf_op jit(solution)/shard_map/weights/pallas_call | solution.py:410
  9.6 5.1 %collective-permute-done.1.down = bf16[80,2048]{1,0:T(8,128)(2,1)S(1)} collective-permute-done((bf16[80,2048]{1,0:T(8,128)(2,1)S(1)}, bf16[80,2048]{1,0:T(8,128)(2,1)S(1)}, u32[]{:S(2)}, u32[]{:S(2)}) %collective-permute-start.1) | collective-permute-done | bytes 327712 | tf_op jit(solution)/shard_map/ppermute | solution.py:349
  14.7 1.9 %generator.1 = (bf16[96,256]{1,0:T(8,128)(2,1)S(1)}, bf16[64,256]{1,0:T(8,128)(2,1)S(1)}, bf16[2,192,1280]{2,1,0:T(8,128)(2,1)S(1)}, bf16[2,192,1280]{2,1,0:T(8,128)(2,1)S(1)}) custom-call(bf16[80,2048]{1,0:T(8,128)(2,1)S(1)} %collective-permute-done.up, bf16[80,2048]{1,0:T(8,128)(2,1)S(1)} %pack.1.mid, bf16[80,2048]{1,0:T(8,128)(2,1)S(1)} %collective-permute-done.1.down, ...), custom_call_target="tpu_custom_call" | custom-call | tf_op jit(solution)/shard_map/generator/pallas_call | solution.py:435
  16.6 0.9 copy-done
  17.6 2.7 %collective-permute-start.4 = (bf16[96,256]{1,0:T(8,128)(2,1)S(1)}, bf16[96,256]{1,0:T(8,128)(2,1)S(1)}, u32[]{:S(2)}, u32[]{:S(2)}) collective-permute-start(bf16[96,256]{1,0:T(8,128)(2,1)S(1)} %get-tuple-element.29.home), channel_id=1, source_target_pairs={{0,1},{2,3},{4,5},{6,7},{8,9},{10,11},{12,13},{14,15},{1,0},{3,2},... | collective-permute-start | bytes 147464 | tf_op jit(solution)/shard_map/ppermute | solution.py:361
  20.3 6.4 %collective-permute-start.5 = (bf16[96,256]{1,0:T(8,128)(2,1)S(1)}, bf16[96,256]{1,0:T(8,128)(2,1)S(1)}, u32[]{:S(2)}, u32[]{:S(2)}) collective-permute-start(bf16[96,256]{1,0:T(8,128)(2,1)S(1)} %get-tuple-element.29.home), channel_id=1, source_target_pairs={{1,2},{3,4},{5,6},{7,8},{9,10},{11,12},{13,14},{15,0},{2,1},{4,3},... | collective-permute-start | bytes 147464 | tf_op jit(solution)/shard_map/ppermute | solution.py:361
  26.7 5.6 %collective-permute-start.3 = (bf16[64,256]{1,0:T(8,128)(2,1)S(1)}, bf16[64,256]{1,0:T(8,128)(2,1)S(1)}, u32[]{:S(2)}, u32[]{:S(2)}) collective-permute-start(bf16[64,256]{1,0:T(8,128)(2,1)S(1)} %get-tuple-element.28), channel_id=1, source_target_pairs={{2,4},{3,5},{6,8},{7,9},{10,12},{11,13},{14,0},{15,1},{4,2},{5,3},... | collective-permute-start | bytes 98312 | tf_op jit(solution)/shard_map/ppermute | solution.py:361
  32.4 1.0 %collective-permute-done.2.far_a = bf16[64,256]{1,0:T(8,128)(2,1)S(1)} collective-permute-done((bf16[64,256]{1,0:T(8,128)(2,1)S(1)}, bf16[64,256]{1,0:T(8,128)(2,1)S(1)}, u32[]{:S(2)}, u32[]{:S(2)}) %collective-permute-start.2) | collective-permute-done | bytes 32800 | tf_op jit(solution)/shard_map/ppermute | solution.py:361
  33.4 2.0 %collective-permute-done.3.far_b = bf16[64,256]{1,0:T(8,128)(2,1)S(1)} collective-permute-done((bf16[64,256]{1,0:T(8,128)(2,1)S(1)}, bf16[64,256]{1,0:T(8,128)(2,1)S(1)}, u32[]{:S(2)}, u32[]{:S(2)}) %collective-permute-start.3) | collective-permute-done | bytes 32800 | tf_op jit(solution)/shard_map/ppermute | solution.py:361
  35.5 16.2 %discriminator.1 = (bf16[64,2048]{1,0:T(8,128)(2,1)S(1)}, bf16[8,24,896]{2,1,0:T(8,128)(2,1)S(1)}) custom-call(bf16[64,256]{1,0:T(8,128)(2,1)S(1)} %collective-permute-done.2.far_a, bf16[64,256]{1,0:T(8,128)(2,1)S(1)} %collective-permute-done.3.far_b, bf16[96,256]{1,0:T(8,128)(2,1)S(1)} %collective-permute-done.4.near_a, ...), custom_call_target="tpu_custom_call" | custom-call | tf_op jit(solution)/shard_map/discriminator/pallas_call | solution.py:454
  51.7 1.9 %collective-permute-start.6 = (bf16[4,24,896]{2,1,0:T(8,128)(2,1)S(1)}, bf16[4,24,896]{2,1,0:T(8,128)(2,1)S(1)}, u32[]{:S(2)}, u32[]{:S(2)}) collective-permute-start(bf16[4,24,896]{2,1,0:T(8,128)(2,1)S(1)} %dynamic-slice_bitcast_fusion), channel_id=1, source_target_pairs={{0,16},{16,0},{32,48},{48,32},{64,80},{80,64},{96,112},{112,96},{1... | collective-permute-start | bytes 516104 | tf_op jit(solution)/shard_map/ppermute | solution.py:353
  53.5 1.0 %collective-permute-done.6 = bf16[4,24,896]{2,1,0:T(8,128)(2,1)S(1)} collective-permute-done((bf16[4,24,896]{2,1,0:T(8,128)(2,1)S(1)}, bf16[4,24,896]{2,1,0:T(8,128)(2,1)S(1)}, u32[]{:S(2)}, u32[]{:S(2)}) %collective-permute-start.6) | collective-permute-done | bytes 172064 | tf_op jit(solution)/shard_map/ppermute | solution.py:353
  54.7 1.6 %collective-permute-start.7 = (bf16[24,896]{1,0:T(8,128)(2,1)S(1)}, bf16[24,896]{1,0:T(8,128)(2,1)S(1)}, u32[]{:S(2)}, u32[]{:S(2)}) collective-permute-start(bf16[24,896]{1,0:T(8,128)(2,1)S(1)} %get-tuple-element.46), channel_id=1, source_target_pairs={{0,64},{16,80},{32,96},{48,112},{64,0},{80,16},{96,32},{112,48},{1... | collective-permute-start | bytes 129032 | tf_op jit(solution)/shard_map/ppermute | solution.py:353
  56.2 1.9 %collective-permute-start.8 = (bf16[24,896]{1,0:T(8,128)(2,1)S(1)}, bf16[24,896]{1,0:T(8,128)(2,1)S(1)}, u32[]{:S(2)}, u32[]{:S(2)}) collective-permute-start(bf16[24,896]{1,0:T(8,128)(2,1)S(1)} %get-tuple-element.48), channel_id=1, source_target_pairs={{0,192},{16,208},{32,224},{48,240},{64,128},{80,144},{96,160},{112... | collective-permute-start | bytes 129032 | tf_op jit(solution)/shard_map/ppermute | solution.py:353
  59.0 1.3 %collective-permute-done.8 = bf16[24,896]{1,0:T(8,128)(2,1)S(1)} collective-permute-done((bf16[24,896]{1,0:T(8,128)(2,1)S(1)}, bf16[24,896]{1,0:T(8,128)(2,1)S(1)}, u32[]{:S(2)}, u32[]{:S(2)}) %collective-permute-start.8) | collective-permute-done | bytes 43040 | tf_op jit(solution)/shard_map/ppermute | solution.py:353
  60.3 2.2 %collective-permute-done.9 = bf16[24,896]{1,0:T(8,128)(2,1)S(1)} collective-permute-done((bf16[24,896]{1,0:T(8,128)(2,1)S(1)}, bf16[24,896]{1,0:T(8,128)(2,1)S(1)}, u32[]{:S(2)}, u32[]{:S(2)}) %collective-permute-start.9) | collective-permute-done | bytes 43040 | tf_op jit(solution)/shard_map/ppermute | solution.py:353
  62.7 1.2 %collective-permute-start.11 = (bf16[24,896]{1,0:T(8,128)(2,1)S(1)}, bf16[24,896]{1,0:T(8,128)(2,1)S(1)}, u32[]{:S(2)}, u32[]{:S(2)}) collective-permute-start(bf16[24,896]{1,0:T(8,128)(2,1)S(1)} %fusion.5), channel_id=1, source_target_pairs={{0,8},{1,9},{2,10},{3,11},{4,12},{5,13},{6,14},{7,15},{8,0},{9,1},... | collective-permute-start | bytes 129032 | tf_op jit(solution)/shard_map/ppermute | solution.py:353
  63.8 2.1 %collective-permute-start.12 = (bf16[24,896]{1,0:T(8,128)(2,1)S(1)}, bf16[24,896]{1,0:T(8,128)(2,1)S(1)}, u32[]{:S(2)}, u32[]{:S(2)}) collective-permute-start(bf16[24,896]{1,0:T(8,128)(2,1)S(1)} %fusion.5), channel_id=1, source_target_pairs={{0,4},{1,5},{2,6},{3,7},{4,0},{5,1},{6,2},{7,3},{8,12},{9,13},{10,... | collective-permute-start | bytes 129032 | tf_op jit(solution)/shard_map/ppermute | solution.py:353
  65.9 0.8 collective-permute-done.10
  68.5 2.4 %collective-permute-done.13 = bf16[24,896]{1,0:T(8,128)(2,1)S(1)} collective-permute-done((bf16[24,896]{1,0:T(8,128)(2,1)S(1)}, bf16[24,896]{1,0:T(8,128)(2,1)S(1)}, u32[]{:S(2)}, u32[]{:S(2)}) %collective-permute-start.13) | collective-permute-done | bytes 43040 | tf_op jit(solution)/shard_map/ppermute | solution.py:353
  70.9 4.4 %collective-permute-start.14 = (bf16[24,896]{1,0:T(8,128)(2,1)S(1)}, bf16[24,896]{1,0:T(8,128)(2,1)S(1)}, u32[]{:S(2)}, u32[]{:S(2)}) collective-permute-start(bf16[24,896]{1,0:T(8,128)(2,1)S(1)} %add_convert_fusion.1), channel_id=1, source_target_pairs={{0,3},{1,2},{2,1},{3,0},{4,7},{5,6},{6,5},{7,4},{8,11},{9,10},{10,... | collective-permute-start | bytes 129032 | tf_op jit(solution)/shard_map/ppermute | solution.py:353
  75.3 1.2 %collective-permute-start.15 = (bf16[24,896]{1,0:T(8,128)(2,1)S(1)}, bf16[24,896]{1,0:T(8,128)(2,1)S(1)}, u32[]{:S(2)}, u32[]{:S(2)}) collective-permute-start(bf16[24,896]{1,0:T(8,128)(2,1)S(1)} %add_convert_fusion.1), channel_id=1, source_target_pairs={{0,2},{1,3},{2,0},{3,1},{4,6},{5,7},{6,4},{7,5},{8,10},{9,11},{10,... | collective-permute-start | bytes 129032 | tf_op jit(solution)/shard_map/ppermute | solution.py:353
  76.5 1.0 %collective-permute-start.16 = (bf16[24,896]{1,0:T(8,128)(2,1)S(1)}, bf16[24,896]{1,0:T(8,128)(2,1)S(1)}, u32[]{:S(2)}, u32[]{:S(2)}) collective-permute-start(bf16[24,896]{1,0:T(8,128)(2,1)S(1)} %add_convert_fusion.1), channel_id=1, source_target_pairs={{0,1},{1,0},{2,3},{3,2},{4,5},{5,4},{6,7},{7,6},{8,9},{9,8},{10,11... | collective-permute-start | bytes 129032 | tf_op jit(solution)/shard_map/ppermute | solution.py:353
  77.5 4.9 %collective-permute-done.15 = bf16[24,896]{1,0:T(8,128)(2,1)S(1)} collective-permute-done((bf16[24,896]{1,0:T(8,128)(2,1)S(1)}, bf16[24,896]{1,0:T(8,128)(2,1)S(1)}, u32[]{:S(2)}, u32[]{:S(2)}) %collective-permute-start.15) | collective-permute-done | bytes 43040 | tf_op jit(solution)/shard_map/ppermute | solution.py:353
  82.5 0.9 collective-permute-start.17
  83.4 1.1 %collective-permute-start.18 = (bf16[24,896]{1,0:T(8,128)(2,1)S(1)}, bf16[24,896]{1,0:T(8,128)(2,1)S(1)}, u32[]{:S(2)}, u32[]{:S(2)}) collective-permute-start(bf16[24,896]{1,0:T(8,128)(2,1)S(1)} %add_convert_fusion.own), channel_id=1, source_target_pairs={{0,128},{16,144},{32,160},{48,176},{64,192},{80,208},{96,224},{112... | collective-permute-start | bytes 129032 | tf_op jit(solution)/shard_map/ppermute | solution.py:353
  84.5 1.3 %collective-permute-start.19 = (bf16[24,896]{1,0:T(8,128)(2,1)S(1)}, bf16[24,896]{1,0:T(8,128)(2,1)S(1)}, u32[]{:S(2)}, u32[]{:S(2)}) collective-permute-start(bf16[24,896]{1,0:T(8,128)(2,1)S(1)} %add_convert_fusion.own), channel_id=1, source_target_pairs={{0,64},{16,80},{32,96},{48,112},{64,0},{80,16},{96,32},{112,48},{1... | collective-permute-start | bytes 129032 | tf_op jit(solution)/shard_map/ppermute | solution.py:353
  85.8 1.1 %collective-permute-done.17.three = bf16[24,896]{1,0:T(8,128)(2,1)S(1)} collective-permute-done((bf16[24,896]{1,0:T(8,128)(2,1)S(1)}, bf16[24,896]{1,0:T(8,128)(2,1)S(1)}, u32[]{:S(2)}, u32[]{:S(2)}) %collective-permute-start.17) | collective-permute-done | bytes 43040 | tf_op jit(solution)/shard_map/ppermute | solution.py:353
  87.8 7.2 %collective-permute-start.20 = (bf16[4,24,896]{2,1,0:T(8,128)(2,1)S(1)}, bf16[4,24,896]{2,1,0:T(8,128)(2,1)S(1)}, u32[]{:S(2)}, u32[]{:S(2)}) collective-permute-start(bf16[4,24,896]{2,1,0:T(8,128)(2,1)S(1)} %pad_maximum_fusion), channel_id=1, source_target_pairs={{0,16},{16,0},{32,48},{48,32},{64,80},{80,64},{96,112},{112,96},{1... | collective-permute-start | bytes 516104 | tf_op jit(solution)/shard_map/ppermute | solution.py:353
  96.0 1.6 %finish.1 = (f32[9,4096]{1,0:T(8,128)}, f32[3,3,3,64]{3,2,1,0:T(4,128)}, f32[3,3,3,3,64]{4,3,2,1,0:T(4,128)}, f32[27,4096]{1,0:T(8,128)}, f32[1,64]{1,0:T(1,128)}) custom-call(bf16[24,896]{1,0:T(8,128)(2,1)S(1)} %add_convert_fusion.own, bf16[24,896]{1,0:T(8,128)(2,1)S(1)} %collective-permute-done.17.three, bf16[24,896]{1,0:T(8,128)(2,1)S(1)} %collective-permute-done.18.two, ...), custom_call_target="tpu_custom_call" | custom-call | tf_op jit(solution)/shard_map/finish/pallas_call | solution.py:481
  (57 shorter events, 8.6 us)
Async XLA Ops:
  0.6 1.0 copy-start.1
  1.6 0.7 copy-start.4
  2.3 3.6 %copy-start.5 = (bf16[64,3,3,3,3]{0,4,3,2,1:T(4,128)(2,1)S(1)}, bf16[64,3,3,3,3]{0,4,3,2,1:T(4,128)(2,1)}, u32[]{:S(2)}) copy-start(bf16[64,3,3,3,3]{0,4,3,2,1:T(4,128)(2,1)} %param.10) | copy-start | bytes 31108
  2.5 7.1 %collective-permute-start = (bf16[80,2048]{1,0:T(8,128)(2,1)S(1)}, bf16[80,2048]{1,0:T(8,128)(2,1)S(1)}, u32[]{:S(2)}, u32[]{:S(2)}) collective-permute-start(bf16[80,2048]{1,0:T(8,128)(2,1)S(1)} %pack.1.mid), channel_id=1, source_target_pairs={{0,16},{16,32},{32,48},{48,64},{64,80},{80,96},{96,112},{112,128},... | collective-permute-start | bytes 983048 | tf_op jit(solution)/shard_map/ppermute | solution.py:349
  5.6 9.1 %collective-permute-start.1 = (bf16[80,2048]{1,0:T(8,128)(2,1)S(1)}, bf16[80,2048]{1,0:T(8,128)(2,1)S(1)}, u32[]{:S(2)}, u32[]{:S(2)}) collective-permute-start(bf16[80,2048]{1,0:T(8,128)(2,1)S(1)} %pack.1.mid), channel_id=1, source_target_pairs={{0,240},{16,0},{32,16},{48,32},{64,48},{80,64},{96,80},{112,96},{1... | collective-permute-start | bytes 983048 | tf_op jit(solution)/shard_map/ppermute | solution.py:349
  6.1 0.7 copy-start.6
  6.2 1.7 %copy-start.2 = (bf16[27,4096]{1,0:T(8,128)(2,1)S(1)}, bf16[27,4096]{1,0:T(8,128)(2,1)}, u32[]{:S(2)}) copy-start(bf16[27,4096]{1,0:T(8,128)(2,1)} %flat_two.1) | copy-start | bytes 663556
  6.9 1.0 copy-start.3
  7.1 0.7 copy-start.7
  16.6 1.0 copy-start
  17.6 17.9 %collective-permute-start.4 = (bf16[96,256]{1,0:T(8,128)(2,1)S(1)}, bf16[96,256]{1,0:T(8,128)(2,1)S(1)}, u32[]{:S(2)}, u32[]{:S(2)}) collective-permute-start(bf16[96,256]{1,0:T(8,128)(2,1)S(1)} %get-tuple-element.29.home), channel_id=1, source_target_pairs={{0,1},{2,3},{4,5},{6,7},{8,9},{10,11},{12,13},{14,15},{1,0},{3,2},... | collective-permute-start | bytes 147464 | tf_op jit(solution)/shard_map/ppermute | solution.py:361
  20.3 15.2 %collective-permute-start.5 = (bf16[96,256]{1,0:T(8,128)(2,1)S(1)}, bf16[96,256]{1,0:T(8,128)(2,1)S(1)}, u32[]{:S(2)}, u32[]{:S(2)}) collective-permute-start(bf16[96,256]{1,0:T(8,128)(2,1)S(1)} %get-tuple-element.29.home), channel_id=1, source_target_pairs={{1,2},{3,4},{5,6},{7,8},{9,10},{11,12},{13,14},{15,0},{2,1},{4,3},... | collective-permute-start | bytes 147464 | tf_op jit(solution)/shard_map/ppermute | solution.py:361
  26.7 6.8 %collective-permute-start.2 = (bf16[64,256]{1,0:T(8,128)(2,1)S(1)}, bf16[64,256]{1,0:T(8,128)(2,1)S(1)}, u32[]{:S(2)}, u32[]{:S(2)}) collective-permute-start(bf16[64,256]{1,0:T(8,128)(2,1)S(1)} %get-tuple-element.28), channel_id=1, source_target_pairs={{0,2},{1,3},{4,6},{5,7},{8,10},{9,11},{12,14},{13,15},{2,0},{3,1},... | collective-permute-start | bytes 98312 | tf_op jit(solution)/shard_map/ppermute | solution.py:361
  26.7 8.8 %collective-permute-start.3 = (bf16[64,256]{1,0:T(8,128)(2,1)S(1)}, bf16[64,256]{1,0:T(8,128)(2,1)S(1)}, u32[]{:S(2)}, u32[]{:S(2)}) collective-permute-start(bf16[64,256]{1,0:T(8,128)(2,1)S(1)} %get-tuple-element.28), channel_id=1, source_target_pairs={{2,4},{3,5},{6,8},{7,9},{10,12},{11,13},{14,0},{15,1},{4,2},{5,3},... | collective-permute-start | bytes 98312 | tf_op jit(solution)/shard_map/ppermute | solution.py:361
  51.7 2.9 %collective-permute-start.6 = (bf16[4,24,896]{2,1,0:T(8,128)(2,1)S(1)}, bf16[4,24,896]{2,1,0:T(8,128)(2,1)S(1)}, u32[]{:S(2)}, u32[]{:S(2)}) collective-permute-start(bf16[4,24,896]{2,1,0:T(8,128)(2,1)S(1)} %dynamic-slice_bitcast_fusion), channel_id=1, source_target_pairs={{0,16},{16,0},{32,48},{48,32},{64,80},{80,64},{96,112},{112,96},{1... | collective-permute-start | bytes 516104 | tf_op jit(solution)/shard_map/ppermute | solution.py:353
  54.7 4.3 %collective-permute-start.7 = (bf16[24,896]{1,0:T(8,128)(2,1)S(1)}, bf16[24,896]{1,0:T(8,128)(2,1)S(1)}, u32[]{:S(2)}, u32[]{:S(2)}) collective-permute-start(bf16[24,896]{1,0:T(8,128)(2,1)S(1)} %get-tuple-element.46), channel_id=1, source_target_pairs={{0,64},{16,80},{32,96},{48,112},{64,0},{80,16},{96,32},{112,48},{1... | collective-permute-start | bytes 129032 | tf_op jit(solution)/shard_map/ppermute | solution.py:353
  56.2 4.1 %collective-permute-start.8 = (bf16[24,896]{1,0:T(8,128)(2,1)S(1)}, bf16[24,896]{1,0:T(8,128)(2,1)S(1)}, u32[]{:S(2)}, u32[]{:S(2)}) collective-permute-start(bf16[24,896]{1,0:T(8,128)(2,1)S(1)} %get-tuple-element.48), channel_id=1, source_target_pairs={{0,192},{16,208},{32,224},{48,240},{64,128},{80,144},{96,160},{112... | collective-permute-start | bytes 129032 | tf_op jit(solution)/shard_map/ppermute | solution.py:353
  58.1 4.4 %collective-permute-start.9 = (bf16[24,896]{1,0:T(8,128)(2,1)S(1)}, bf16[24,896]{1,0:T(8,128)(2,1)S(1)}, u32[]{:S(2)}, u32[]{:S(2)}) collective-permute-start(bf16[24,896]{1,0:T(8,128)(2,1)S(1)} %get-tuple-element.47), channel_id=1, source_target_pairs={{0,128},{16,144},{32,160},{48,176},{64,192},{80,208},{96,224},{112... | collective-permute-start | bytes 129032 | tf_op jit(solution)/shard_map/ppermute | solution.py:353
  62.6 4.2 %collective-permute-start.10 = (bf16[24,896]{1,0:T(8,128)(2,1)S(1)}, bf16[24,896]{1,0:T(8,128)(2,1)S(1)}, u32[]{:S(2)}, u32[]{:S(2)}) collective-permute-start(bf16[24,896]{1,0:T(8,128)(2,1)S(1)} %fusion.5), channel_id=1, source_target_pairs={{0,12},{1,13},{2,14},{3,15},{4,8},{5,9},{6,10},{7,11},{8,4},{9,5},... | collective-permute-start | bytes 129032 | tf_op jit(solution)/shard_map/ppermute | solution.py:353
  62.7 4.5 %collective-permute-start.11 = (bf16[24,896]{1,0:T(8,128)(2,1)S(1)}, bf16[24,896]{1,0:T(8,128)(2,1)S(1)}, u32[]{:S(2)}, u32[]{:S(2)}) collective-permute-start(bf16[24,896]{1,0:T(8,128)(2,1)S(1)} %fusion.5), channel_id=1, source_target_pairs={{0,8},{1,9},{2,10},{3,11},{4,12},{5,13},{6,14},{7,15},{8,0},{9,1},... | collective-permute-start | bytes 129032 | tf_op jit(solution)/shard_map/ppermute | solution.py:353
  63.8 3.9 %collective-permute-start.12 = (bf16[24,896]{1,0:T(8,128)(2,1)S(1)}, bf16[24,896]{1,0:T(8,128)(2,1)S(1)}, u32[]{:S(2)}, u32[]{:S(2)}) collective-permute-start(bf16[24,896]{1,0:T(8,128)(2,1)S(1)} %fusion.5), channel_id=1, source_target_pairs={{0,4},{1,5},{2,6},{3,7},{4,0},{5,1},{6,2},{7,3},{8,12},{9,13},{10,... | collective-permute-start | bytes 129032 | tf_op jit(solution)/shard_map/ppermute | solution.py:353
  67.8 3.1 %collective-permute-start.13 = (bf16[24,896]{1,0:T(8,128)(2,1)S(1)}, bf16[24,896]{1,0:T(8,128)(2,1)S(1)}, u32[]{:S(2)}, u32[]{:S(2)}) collective-permute-start(bf16[24,896]{1,0:T(8,128)(2,1)S(1)} %add_convert_fusion.2), channel_id=1, source_target_pairs={{0,32},{16,48},{32,0},{48,16},{64,96},{80,112},{96,64},{112,80},{1... | collective-permute-start | bytes 129032 | tf_op jit(solution)/shard_map/ppermute | solution.py:353
  70.9 6.6 %collective-permute-start.14 = (bf16[24,896]{1,0:T(8,128)(2,1)S(1)}, bf16[24,896]{1,0:T(8,128)(2,1)S(1)}, u32[]{:S(2)}, u32[]{:S(2)}) collective-permute-start(bf16[24,896]{1,0:T(8,128)(2,1)S(1)} %add_convert_fusion.1), channel_id=1, source_target_pairs={{0,3},{1,2},{2,1},{3,0},{4,7},{5,6},{6,5},{7,4},{8,11},{9,10},{10,... | collective-permute-start | bytes 129032 | tf_op jit(solution)/shard_map/ppermute | solution.py:353
  75.3 7.1 %collective-permute-start.15 = (bf16[24,896]{1,0:T(8,128)(2,1)S(1)}, bf16[24,896]{1,0:T(8,128)(2,1)S(1)}, u32[]{:S(2)}, u32[]{:S(2)}) collective-permute-start(bf16[24,896]{1,0:T(8,128)(2,1)S(1)} %add_convert_fusion.1), channel_id=1, source_target_pairs={{0,2},{1,3},{2,0},{3,1},{4,6},{5,7},{6,4},{7,5},{8,10},{9,11},{10,... | collective-permute-start | bytes 129032 | tf_op jit(solution)/shard_map/ppermute | solution.py:353
  76.5 5.9 %collective-permute-start.16 = (bf16[24,896]{1,0:T(8,128)(2,1)S(1)}, bf16[24,896]{1,0:T(8,128)(2,1)S(1)}, u32[]{:S(2)}, u32[]{:S(2)}) collective-permute-start(bf16[24,896]{1,0:T(8,128)(2,1)S(1)} %add_convert_fusion.1), channel_id=1, source_target_pairs={{0,1},{1,0},{2,3},{3,2},{4,5},{5,4},{6,7},{7,6},{8,9},{9,8},{10,11... | collective-permute-start | bytes 129032 | tf_op jit(solution)/shard_map/ppermute | solution.py:353
  82.5 4.5 %collective-permute-start.17 = (bf16[24,896]{1,0:T(8,128)(2,1)S(1)}, bf16[24,896]{1,0:T(8,128)(2,1)S(1)}, u32[]{:S(2)}, u32[]{:S(2)}) collective-permute-start(bf16[24,896]{1,0:T(8,128)(2,1)S(1)} %add_convert_fusion.own), channel_id=1, source_target_pairs={{0,192},{16,208},{32,224},{48,240},{64,128},{80,144},{96,160},{112... | collective-permute-start | bytes 129032 | tf_op jit(solution)/shard_map/ppermute | solution.py:353
  83.4 4.4 %collective-permute-start.18 = (bf16[24,896]{1,0:T(8,128)(2,1)S(1)}, bf16[24,896]{1,0:T(8,128)(2,1)S(1)}, u32[]{:S(2)}, u32[]{:S(2)}) collective-permute-start(bf16[24,896]{1,0:T(8,128)(2,1)S(1)} %add_convert_fusion.own), channel_id=1, source_target_pairs={{0,128},{16,144},{32,160},{48,176},{64,192},{80,208},{96,224},{112... | collective-permute-start | bytes 129032 | tf_op jit(solution)/shard_map/ppermute | solution.py:353
  84.5 3.2 %collective-permute-start.19 = (bf16[24,896]{1,0:T(8,128)(2,1)S(1)}, bf16[24,896]{1,0:T(8,128)(2,1)S(1)}, u32[]{:S(2)}, u32[]{:S(2)}) collective-permute-start(bf16[24,896]{1,0:T(8,128)(2,1)S(1)} %add_convert_fusion.own), channel_id=1, source_target_pairs={{0,64},{16,80},{32,96},{48,112},{64,0},{80,16},{96,32},{112,48},{1... | collective-permute-start | bytes 129032 | tf_op jit(solution)/shard_map/ppermute | solution.py:353
  87.8 8.2 %collective-permute-start.20 = (bf16[4,24,896]{2,1,0:T(8,128)(2,1)S(1)}, bf16[4,24,896]{2,1,0:T(8,128)(2,1)S(1)}, u32[]{:S(2)}, u32[]{:S(2)}) collective-permute-start(bf16[4,24,896]{2,1,0:T(8,128)(2,1)S(1)} %pad_maximum_fusion), channel_id=1, source_target_pairs={{0,16},{16,0},{32,48},{48,32},{64,80},{80,64},{96,112},{112,96},{1... | collective-permute-start | bytes 516104 | tf_op jit(solution)/shard_map/ppermute | solution.py:353
